TPU v7x, 32 devices: a whole 2x2x4 slice. The times are simulated.
32 devices in a mesh: dp: 16 (over z, x, core), expert: 2 (over y).
Axes of the slice: x: 2, y: 2, z: 4, core: 2. Of those that a mesh axis runs over, the one named last changes fastest.
Arguments:
- tokens: bfloat16 [16384, 512], P('dp'), may hold values from -6 to 6
- gain_attn: float32 [512], replicated, may hold values from 0.1 to 1.9
- w_key: bfloat16 [512, 64], P('dp'), may hold values from -0.25 to 0.25
- w_value: bfloat16 [512, 64], P('dp'), may hold values from -0.25 to 0.25
- w_router: bfloat16 [512, 24], replicated, may hold values from -0.125 to 0.125
- w_query: bfloat16 [512, 1536], P(None, 'expert'), may hold values from -0.25 to 0.25
- w_out: bfloat16 [1536, 512], P('expert'), may hold values from -33.75 to 33.75
- gain_ffn: float32 [512], replicated, may hold values from 0.1 to 1.9
- w_hidden: bfloat16 [512, 2048], P('dp', 'expert'), may hold values from -0.25 to 0.25
- w_output: bfloat16 [2048, 512], P('expert', 'dp'), may hold values from -0.1875 to 0.1875
- expert_ids: int32 [16384, 8], P('dp'), may hold values from 0 to 23, all different within a row
- lengths: int32 [16], P('dp'), may hold values from 64 to 1024, as said below
- grad_out: bfloat16 [16384, 512], P('dp', 'expert'), may hold values from -6 to 6
Outputs:
- output: bfloat16 [16384, 512], P('dp', 'expert')
- grad_tokens: bfloat16 [16384, 512], P('dp')
- grad_key: float32 [512, 64], P('dp')
- grad_value: float32 [512, 64], P('dp')
- grad_router: float32 [512, 24], replicated
- grad_query: float32 [512, 1536], P(None, 'expert')
- grad_outproj: float32 [1536, 512], P('expert')
- grad_hidden: float32 [512, 2048], P('dp', 'expert')
- grad_output: float32 [2048, 512], P('expert', 'dp')
- grad_gain_attn: float32 [512], replicated
- grad_gain_ffn: float32 [512], replicated
Inputs may be any that keep to these rules, and one draw needn't show every extreme that they name: `lengths`: in every draw one sequence has exactly 1024 real tokens and another exactly 64.
All inputs are finite; a program needn't handle non-finite values.
Results may differ from a plain program's by a relative error of at most 0.012.
The roundings to bfloat16 on the way count: a program that leaves them out, or rounds other values in their place, can miss the bound.
Values may be sent and summed in bfloat16 or wider, within the bound.
A program may use at most 192 MiB of HBM per device.

v0:
```python
import jax
import jax.numpy as jnp
from jax import lax
from jax.sharding import PartitionSpec as P

eps = 1e-05
big_neg = -1000000000.0


def product(left, right):
    return jnp.dot(left, right, preferred_element_type=jnp.float32)


def product_tn(left, right):
    return lax.dot_general(
        left, right, (((0,), (0,)), ((), ())), preferred_element_type=jnp.float32
    )


def product_nt(left, right):
    return lax.dot_general(
        left, right, (((1,), (1,)), ((), ())), preferred_element_type=jnp.float32
    )


def norm_rows(values):
    row_mean = jnp.mean(values, axis=-1, keepdims=True)
    centred = values - row_mean
    row_var = jnp.mean(centred * centred, axis=-1, keepdims=True)
    inv_scale = lax.rsqrt(row_var + eps)
    return (centred * inv_scale, inv_scale)


def norm_back(grad_rows, normed, inv_scale, gain):
    weighted = grad_rows * gain
    return inv_scale * (
        weighted
        - jnp.mean(weighted, axis=-1, keepdims=True)
        - normed * jnp.mean(weighted * normed, axis=-1, keepdims=True)
    )


def gelu_back(hidden_pre, grad_active):
    unused, gelu_pull = jax.vjp(jax.nn.gelu, hidden_pre)
    return gelu_pull(grad_active)[0]


def shards(
    tokens,
    gain_attn,
    w_key,
    w_value,
    w_router,
    w_query,
    w_out,
    gain_ffn,
    w_hidden,
    w_output,
    expert_ids,
    lengths,
    grad_out,
):
    row_count, model_width = tokens.shape
    seq_count = lengths.shape[0]
    seq_len = row_count // seq_count
    head_dim = w_key.shape[1]
    n_experts = w_router.shape[1]
    local_experts = w_query.shape[1] // head_dim
    expert_pos = lax.axis_index("expert")
    first_expert = expert_pos * local_experts
    half_rows = row_count // lax.axis_size("expert")
    row_start = expert_pos * half_rows
    query_scale = head_dim ** (-0.5)
    block_rows = min(512, seq_len)
    blocks = seq_len // block_rows
    item_count = seq_count * blocks
    key_full, value_full, hidden_full, output_full = (
        lax.all_gather(w_key, "dp", axis=0, tiled=True),
        lax.all_gather(w_value, "dp", axis=0, tiled=True),
        lax.all_gather(w_hidden, "dp", axis=0, tiled=True),
        lax.all_gather(w_output, "dp", axis=1, tiled=True),
    )
    kv_weight = jnp.concatenate((key_full, value_full), axis=1)
    slot_index = jnp.arange(row_count, dtype=jnp.int32) % seq_len
    row_length = jnp.repeat(lengths, seq_len)
    valid_rows = (slot_index < row_length).astype(jnp.float32)[:, None]
    inputs = tokens.astype(jnp.float32)
    normed_one, scale_one = norm_rows(inputs)
    hidden_one = (normed_one * gain_attn).astype(jnp.bfloat16)
    keyval = product(hidden_one, kv_weight).astype(jnp.bfloat16)
    keys_all = keyval[:, :head_dim]
    values_all = keyval[:, head_dim:]
    logits = product(hidden_one, w_router)
    choose = (
        expert_ids[:, :, None] == jnp.arange(n_experts, dtype=jnp.int32)[None, None, :]
    ).astype(jnp.float32)
    picked = jnp.sum(logits[:, None, :] * choose, axis=-1)
    gate_top = jnp.max(picked, axis=-1, keepdims=True)
    gate_exp = jnp.exp(picked - gate_top)
    gate_weights = gate_exp / jnp.sum(gate_exp, axis=-1, keepdims=True)
    dense_gate = jnp.sum(gate_weights[:, :, None] * choose, axis=1)
    local_gate = lax.dynamic_slice_in_dim(dense_gate, first_expert, local_experts, 1)
    wide_gate = jnp.repeat(local_gate, head_dim, axis=1)
    queries = (query_scale * product(hidden_one, w_query)).astype(jnp.bfloat16)
    key_slots = jnp.arange(seq_len, dtype=jnp.int32)

    def block_inputs(item_index):
        seq_index = item_index // blocks
        offset = item_index % blocks * block_rows
        start = seq_index * seq_len + offset
        query_block = lax.dynamic_slice_in_dim(queries, start, block_rows, 0).reshape(
            block_rows, local_experts, head_dim
        )
        query_slots = offset + jnp.arange(block_rows, dtype=jnp.int32)
        allowed = (key_slots[None, :] <= query_slots[:, None]) & (
            key_slots[None, :] < lengths[seq_index]
        )
        scores = jnp.einsum(
            "qeh,kh->eqk", query_block, keys_all, preferred_element_type=jnp.float32
        )
        scores = jnp.where(allowed[None], scores, big_neg)
        return (seq_index, start, query_block, keys_all, values_all, scores)

    def attend_block(item_index):
        seq_index, start, query_block, key_seq, value_seq, scores = block_inputs(item_index)
        row_top = jnp.max(scores, axis=-1, keepdims=True)
        exponent = jnp.exp(scores - row_top)
        row_total = jnp.sum(exponent, axis=-1, keepdims=True)
        probs = (exponent / row_total).astype(jnp.bfloat16)
        block_out = jnp.einsum("eqk,kh->qeh", probs, value_seq, preferred_element_type=jnp.float32)
        return (
            block_out.reshape(block_rows, local_experts * head_dim),
            row_top[:, :, 0] + jnp.log(row_total[:, :, 0]),
        )

    head_out, log_totals = lax.map(attend_block, jnp.arange(item_count, dtype=jnp.int32))
    head_out = head_out.reshape(row_count, local_experts * head_dim)
    gated = (wide_gate * head_out).astype(jnp.bfloat16)
    attended_rows = lax.psum_scatter(
        product(gated, w_out), "expert", scatter_dimension=0, tiled=True
    )
    ffn_valid = lax.dynamic_slice_in_dim(valid_rows, row_start, half_rows, 0)
    residual = lax.dynamic_slice_in_dim(inputs, row_start, half_rows, 0) + ffn_valid * attended_rows
    ffn_in, ffn_outw = (
        lax.all_gather(hidden_full, "expert", axis=1, tiled=True),
        lax.all_gather(output_full, "expert", axis=0, tiled=True),
    )
    normed_two, scale_two = norm_rows(residual)
    hidden_two = (normed_two * gain_ffn).astype(jnp.bfloat16)
    hidden_pre = product(hidden_two, ffn_in)
    active = jax.nn.gelu(hidden_pre).astype(jnp.bfloat16)
    output_rows = (residual + ffn_valid * product(active, ffn_outw)).astype(jnp.bfloat16)
    output = lax.all_to_all(output_rows, "expert", split_axis=1, concat_axis=0, tiled=True)
    kv_back, hidden_back, output_back = (kv_weight, hidden_full, output_full)
    hidden_back, output_back = (ffn_in, ffn_outw)
    grad_full = lax.all_to_all(grad_out, "expert", split_axis=0, concat_axis=1, tiled=True).astype(
        jnp.float32
    )
    grad_ffn = (ffn_valid * grad_full).astype(jnp.bfloat16)
    grad_w_two = product_tn(active, grad_ffn)
    grad_active = product_nt(grad_ffn, output_back)
    grad_inner = gelu_back(hidden_pre, grad_active).astype(jnp.bfloat16)
    grad_w_one = product_tn(hidden_two, grad_inner)
    grad_w_one, grad_w_two = (
        lax.psum_scatter(
            grad_w_one.astype(jnp.bfloat16), "expert", scatter_dimension=1, tiled=True
        ).astype(jnp.float32),
        lax.psum_scatter(
            grad_w_two.astype(jnp.bfloat16), "expert", scatter_dimension=0, tiled=True
        ).astype(jnp.float32),
    )
    grad_two = product_nt(grad_inner, hidden_back)
    grad_resid_rows = grad_full + norm_back(grad_two, normed_two, scale_two, gain_ffn)
    gain_rows = jnp.sum(grad_two * normed_two, axis=0)
    grad_resid, gain_pieces = (
        lax.all_gather(grad_resid_rows.astype(jnp.bfloat16), "expert", axis=0, tiled=True).astype(
            grad_resid_rows.dtype
        ),
        lax.all_gather(
            gain_rows[None, :].astype(jnp.bfloat16), "expert", axis=0, tiled=True
        ).astype(jnp.float32),
    )
    grad_gain_two = jnp.sum(gain_pieces, axis=0)
    grad_att = (valid_rows * grad_resid).astype(jnp.bfloat16)
    grad_wo = product_tn(gated, grad_att)
    grad_gated = product_nt(grad_att, w_out)
    grad_gate_local = jnp.sum(
        (grad_gated * head_out).reshape(row_count, local_experts, head_dim), axis=-1
    )
    grad_heads = (wide_gate * grad_gated).astype(jnp.bfloat16)

    def back_block(carried, packed):
        item_index, log_block = packed
        seq_index, start, query_block, key_seq, value_seq, scores = block_inputs(item_index)
        probs_full = jnp.exp(scores - log_block[:, :, None])
        probs = probs_full.astype(jnp.bfloat16)
        head_grad = lax.dynamic_slice_in_dim(grad_heads, start, block_rows, 0).reshape(
            block_rows, local_experts, head_dim
        )
        grad_p = jnp.einsum("qeh,kh->eqk", head_grad, value_seq, preferred_element_type=jnp.float32)
        grad_s = (
            probs_full * (grad_p - jnp.sum(probs_full * grad_p, axis=-1, keepdims=True))
        ).astype(jnp.bfloat16)
        grad_q = jnp.einsum("eqk,kh->qeh", grad_s, key_seq, preferred_element_type=jnp.float32)
        grad_k = jnp.einsum("eqk,qeh->kh", grad_s, query_block, preferred_element_type=jnp.float32)
        grad_v = jnp.einsum("eqk,qeh->kh", probs, head_grad, preferred_element_type=jnp.float32)
        previous = carried
        carried = previous + jnp.concatenate((grad_k, grad_v), axis=1)
        return (carried, grad_q.reshape(block_rows, local_experts * head_dim))

    grad_kv_local, grad_q_blocks = lax.scan(
        back_block,
        jnp.zeros((row_count, 2 * head_dim), jnp.float32),
        (jnp.arange(item_count, dtype=jnp.int32), log_totals),
    )
    grad_queries = (
        grad_q_blocks.reshape(row_count, local_experts * head_dim).astype(jnp.bfloat16)
        * query_scale
    )
    grad_wq = product_tn(hidden_one, grad_queries)
    grad_dense_local = lax.dynamic_update_slice_in_dim(
        jnp.zeros((row_count, n_experts), jnp.float32), grad_gate_local, first_expert, 1
    )
    grad_h_query, grad_kv, grad_dense = lax.psum(
        (product_nt(grad_queries, w_query), grad_kv_local, grad_dense_local), "expert"
    )
    grad_kv_low = grad_kv.astype(jnp.bfloat16)
    grad_kv_weight = product_tn(hidden_one, grad_kv_low)
    grad_picked = jnp.sum(grad_dense[:, None, :] * choose, axis=-1)
    grad_sel = gate_weights * (
        grad_picked - jnp.sum(gate_weights * grad_picked, axis=-1, keepdims=True)
    )
    grad_logits = jnp.sum(grad_sel[:, :, None] * choose, axis=1).astype(jnp.bfloat16)
    grad_wr = product_tn(hidden_one, grad_logits)
    grad_one = grad_h_query + product_nt(grad_kv_low, kv_back) + product_nt(grad_logits, w_router)
    grad_gain_one = jnp.sum(grad_one * normed_one, axis=0)
    grad_tokens = (grad_resid + norm_back(grad_one, normed_one, scale_one, gain_attn)).astype(
        jnp.bfloat16
    )
    shard_key, shard_value, shard_hidden, shard_output = (
        lax.psum_scatter(grad_kv_weight[:, :head_dim], "dp", scatter_dimension=0, tiled=True),
        lax.psum_scatter(grad_kv_weight[:, head_dim:], "dp", scatter_dimension=0, tiled=True),
        lax.psum_scatter(grad_w_one, "dp", scatter_dimension=0, tiled=True),
        lax.psum_scatter(grad_w_two, "dp", scatter_dimension=1, tiled=True),
    )
    summed_wq, summed_wo, summed_wr, summed_gain_one, summed_gain_two = lax.psum(
        (grad_wq, grad_wo, grad_wr, grad_gain_one, grad_gain_two), "dp"
    )
    return (
        output,
        grad_tokens,
        shard_key,
        shard_value,
        summed_wr,
        summed_wq,
        summed_wo,
        shard_hidden,
        shard_output,
        summed_gain_one,
        summed_gain_two,
    )


def solution(mesh):
    placed = (
        P("dp", None),
        P(),
        P("dp", None),
        P("dp", None),
        P(),
        P(None, "expert"),
        P("expert", None),
        P(),
        P("dp", "expert"),
        P("expert", "dp"),
        P("dp", None),
        P("dp"),
        P("dp", "expert"),
    )
    return jax.shard_map(
        shards,
        mesh=mesh,
        in_specs=placed,
        out_specs=(
            P("dp", "expert"),
            P("dp", None),
            P("dp", None),
            P("dp", None),
            P(),
            P(None, "expert"),
            P("expert", None),
            P("dp", "expert"),
            P("expert", "dp"),
            P(),
            P(),
        ),
        check_vma=False,
    )
```

profile of v0, /device:TPU:0, one launch (start us, length us, event | category | flops | bytes accessed | tf_op | source)
XLA Modules:
  0.0 779.5 jit_solution(11970443687311270791)
XLA Ops:
  12.9 23.9 %all_gather.24 = bf16[512,64]{1,0:T(8,128)(2,1)S(1)} all-gather(bf16[32,64]{1,0:T(8,128)(2,1)} %param.19), channel_id=1, replica_groups=mesh['dp'=16,'expert'=2] {'dp'}, dimensions={0}, use_global_device_ids=true | all-gather | bytes 69632 | tf_op jit(solution)/shard_map/all_gather | solution.py:78
  36.8 18.2 %all_gather.25 = bf16[512,64]{1,0:T(8,128)(2,1)S(1)} all-gather(bf16[32,64]{1,0:T(8,128)(2,1)} %param.20), channel_id=1, replica_groups=mesh['dp'=16,'expert'=2] {'dp'}, dimensions={0}, use_global_device_ids=true | all-gather | bytes 69632 | tf_op jit(solution)/shard_map/all_gather | solution.py:79
  59.6 141.3 %while.32 = (s32[]{:T(128)}, f32[2,512,768]{1,0,2:T(2,128)}, f32[2,12,512]{2,1,0:T(8,128)S(1)}, s32[2]{0:T(128)S(1)}, s32[1]{0:T(128)}, /*index=5*/bf16[1024,768...) while((s32[]{:T(128)}, f32[2,512,768]{1,0,2:T(2,128)}, ...), condition=%wide.region_9.10_spmd.clone.clone, body=%wide.region_6.9_spmd.clone.clone.sunk | while | flops 1668279808 | bytes 188971456 | solution.py:136
  65.1 10.3 %bitcast_reduce_fusion.2 = (f32[12,512]{1,0:T(8,128)S(1)}, f32[512,12,1024]{2,0,1:T(8,128)}) fusion(pred[512,1024]{1,0:T(8,128)(4,1)S(1)} %fusion.131, bf16[512,12,64]{0,2,1:T(8,128)(2,1)S(1)} %bitcast.204, bf16[1024,64]{0,1:T(8,128)(2,1)S(1)} %get-tuple-element.719), kind=kOutput, calls=%fused_computation.3.clone.1 | convolution fusion | flops 817883136 | bytes 26632192 | tf_op jit(solution)/shard_map/while/body/eval_jaxpr/qeh,kh->eqk/dot_general | solution.py:118
  75.4 12.0 %fusion.132 = f32[12,512]{1,0:T(8,128)S(1)} fusion(f32[512,12,1024]{2,0,1:T(8,128)} %get-tuple-element.669, f32[12,512]{1,0:T(8,128)S(1)} %get-tuple-element.670, pred[512,1024]{1,0:T(8,128)(4,1)S(1)} %fusion.131), kind=kLoop, calls=%fused_computation.6.clone.1 | loop fusion | flops 18868224 | bytes 25739264 | tf_op jit(solution)/shard_map/while/body/eval_jaxpr/reduce_sum | solution.py:128
  87.4 3.7 copy-done.2
  91.1 7.8 fusion.133
  101.9 28.6 %dynamic_update_slice.36 = f32[2,512,768]{1,0,2:T(2,128)} dynamic-update-slice(f32[2,512,768]{1,0,2:T(2,128)} %get-tuple-element.700, f32[1,512,768]{1,0,2:T(1,128)S(1)} %copy.125, s32[]{:T(128)S(6)} %copy.133, s32[]{:T(128)} %constant.193.clone.1..sunk, s32[]{:T(128)} %constant.193.clone.1..sunk) | dynamic-update-slice | bytes 3145732 | tf_op jit(solution)/shard_map/while/body/jit(dynamic_update_index_in_dim)/dynamic_update_slice | solution.py:136
  135.9 10.3 %bitcast_reduce_fusion.2 = (f32[12,512]{1,0:T(8,128)S(1)}, f32[512,12,1024]{2,0,1:T(8,128)}) fusion(pred[512,1024]{1,0:T(8,128)(4,1)S(1)} %fusion.131, bf16[512,12,64]{0,2,1:T(8,128)(2,1)S(1)} %bitcast.204, bf16[1024,64]{0,1:T(8,128)(2,1)S(1)} %get-tuple-element.719), kind=kOutput, calls=%fused_computation.3.clone.1 | convolution fusion | flops 817883136 | bytes 26632192 | tf_op jit(solution)/shard_map/while/body/eval_jaxpr/qeh,kh->eqk/dot_general | solution.py:118
  146.2 12.0 %fusion.132 = f32[12,512]{1,0:T(8,128)S(1)} fusion(f32[512,12,1024]{2,0,1:T(8,128)} %get-tuple-element.669, f32[12,512]{1,0:T(8,128)S(1)} %get-tuple-element.670, pred[512,1024]{1,0:T(8,128)(4,1)S(1)} %fusion.131), kind=kLoop, calls=%fused_computation.6.clone.1 | loop fusion | flops 18868224 | bytes 25739264 | tf_op jit(solution)/shard_map/while/body/eval_jaxpr/reduce_sum | solution.py:128
  158.2 3.4 copy-done.2
  161.6 7.8 %fusion.133 = f32[12,512,64]{1,2,0:T(8,128)} fusion(f32[512,12,1024]{2,0,1:T(8,128)S(1)} %copy-done.2, f32[12,512]{1,0:T(8,128)S(1)} %fusion.132, f32[12,512]{1,0:T(8,128)S(1)} %get-tuple-element.670, pred[512,1024]{1,0:T(8,128)(4,1)S(1)} %fusion.131, bf16[1024,64]{0,1:T(8,128)(2,1)S(1)} %get-tuple-element.720), kind=kOutput, calls=%fused_computation.7.clone.1 | convolution fusion | flops 830472192 | bytes 27443200 | tf_op jit(solution)/shard_map/while/body/eval_jaxpr/eqk,kh->qeh/dot_general | solution.py:130
  169.4 3.0 copy.125
  172.4 28.6 %dynamic_update_slice.36 = f32[2,512,768]{1,0,2:T(2,128)} dynamic-update-slice(f32[2,512,768]{1,0,2:T(2,128)} %get-tuple-element.700, f32[1,512,768]{1,0,2:T(1,128)S(1)} %copy.125, s32[]{:T(128)S(6)} %copy.133, s32[]{:T(128)} %constant.193.clone.1..sunk, s32[]{:T(128)} %constant.193.clone.1..sunk) | dynamic-update-slice | bytes 3145732 | tf_op jit(solution)/shard_map/while/body/jit(dynamic_update_index_in_dim)/dynamic_update_slice | solution.py:136
  201.0 4.3 copy.120
  214.5 3.5 all-to-all-start.1
  220.8 11.9 %all-to-all-done.1 = bf16[2,512,256]{2,1,0:T(8,128)(2,1)S(1)} async-done(((bf16[2,512,256]{2,1,0:T(8,128)(2,1)}), bf16[2,512,256]{2,1,0:T(8,128)(2,1)S(1)}, u32[]{:S(2)}, u32[]{:S(2)}) %all-to-all-start.1) | async-done | bytes 524320 | tf_op jit(solution)/shard_map/all_to_all | solution.py:156
  233.9 15.2 %reduce-scatter.14.cloned.1.call-done = f32[512,512]{1,0:T(8,128)} async-done(((f32[1024,512]{1,0:T(8,128)}), f32[512,512]{1,0:T(8,128)}) %reduce-scatter.14.cloned.1.call-update) | async-done | bytes 1048592 | tf_op jit(solution)/shard_map/reduce_scatter | solution.py:139
  251.2 19.0 %all-gather.10.cloned.1.call-done = bf16[512,2048]{1,0:T(8,128)(2,1)} async-done(((bf16[512,1024]{1,0:T(8,128)(2,1)}), bf16[512,2048]{1,0:T(8,128)(2,1)}) %all-gather.10.cloned.1.call-update) | async-done | bytes 2097168 | tf_op jit(solution)/shard_map/all_gather | solution.py:145
  270.2 5.0 fusion.65
  275.2 28.6 %all-gather.14.cloned.1.call-done = bf16[2048,512]{0,1:T(8,128)(2,1)} async-done(((bf16[1024,512]{0,1:T(8,128)(2,1)}), bf16[2048,512]{0,1:T(8,128)(2,1)}) %all-gather.14.cloned.1.call-update) | async-done | bytes 2097168 | tf_op jit(solution)/shard_map/all_gather | solution.py:146
  303.8 6.7 fusion.37
  313.8 5.8 convolution_convert_fusion
  319.7 4.5 convolution_convert_fusion.1
  324.2 10.8 %all-gather.16.cloned.1.call-done = bf16[1024,512]{1,0:T(8,128)(2,1)} async-done(((bf16[512,512]{1,0:T(8,128)(2,1)}), bf16[1024,512]{1,0:T(8,128)(2,1)}) %all-gather.16.cloned.1.call-update) | async-done | bytes 1048592 | tf_op jit(solution)/shard_map/all_gather | solution.py:176
  335.0 5.4 fusion.67
  340.5 144.9 %while.33 = (s32[]{:T(128)}, f32[1024,128]{0,1:T(8,128)S(1)}, bf16[2,512,768]{2,1,0:T(8,128)(2,1)}, s32[2]{0:T(128)S(1)}, s32[1]{0:T(128)}, /*index=5*/bf16[1024...) while((s32[]{:T(128)}, f32[1024,128]{0,1:T(8,128)S(1)}, ...), condition=%wide.region_17.18_spmd.clone.clone, body=%wide.region_15.17_spmd.clone.clone.sunk | while | flops 4103466496 | bytes 203733456 | solution.py:211
  346.4 10.2 %fusion.143 = f32[512,12,1024]{2,0,1:T(8,128)} fusion(bf16[512,12,64]{0,2,1:T(8,128)(2,1)S(1)} %bitcast.201, bf16[1024,64]{0,1:T(8,128)(2,1)S(1)} %get-tuple-element.765), kind=kOutput, calls=%fused_computation.37.clone.1 | convolution fusion | flops 805306368 | bytes 26083328 | tf_op jit(solution)/shard_map/while/body/eval_jaxpr/qeh,kh->eqk/dot_general | solution.py:118
  356.7 11.1 %fusion.145 = f32[1024,64]{0,1:T(8,128)S(1)} fusion(bf16[512,12,64]{0,2,1:T(8,128)(2,1)S(1)} %bitcast.205, f32[512,12,1024]{2,0,1:T(8,128)} %fusion.143, f32[12,512]{1,0:T(8,128)S(1)} %dynamic-slice_bitcast_fusion.2, pred[512,1024]{1,0:T(8,128)(4,1)S(1)} %fusion.144), kind=kOutput, calls=%fused_computation.30.clone.1 | convolution fusion | flops 824180736 | bytes 26763264 | tf_op jit(solution)/shard_map/while/body/eval_jaxpr/eqk,qeh->kh/dot_general | solution.py:206
  367.8 20.8 %fusion.146 = (f32[12,512]{1,0:T(8,128)S(1)}, f32[512,12,1024]{2,0,1:T(8,128)}) fusion(f32[512,12,1024]{2,0,1:T(8,128)} %fusion.143, f32[12,512]{1,0:T(8,128)S(1)} %dynamic-slice_bitcast_fusion.2, pred[512,1024]{1,0:T(8,128)(4,1)S(1)} %fusion.144, bf16[512,12,64]{0,2,1:T(8,128)(2,1)S(1)} %bitcast.206, bf16[1024,64]{0,1:T(8,128)(2,1)S(1)} %get-tuple-element.768), kind=kOutput, calls=%fused_computation.20.clone.1 | convolution fusion | flops 830466048 | bytes 51822592 | tf_op jit(solution)/shard_map/while/body/eval_jaxpr/qeh,kh->eqk/dot_general | solution.py:200
  388.6 17.0 %fusion.147 = bf16[12,512,1024]{2,1,0:T(8,128)(2,1)S(1)} fusion(f32[512,12,1024]{2,0,1:T(8,128)} %get-tuple-element.683, f32[512,12,1024]{2,0,1:T(8,128)} %fusion.143, f32[12,512]{1,0:T(8,128)S(1)} %get-tuple-element.684, f32[12,512]{1,0:T(8,128)S(1)} %dynamic-slice_bitcast_fusion.2, pred[512,1024]{1,0:T(8,128)(4,1)S(1)} %fusion.144), kind=kLoop, calls=%fused_computation.22.clone.1 | loop fusion | flops 31457280 | bytes 63488000 | tf_op jit(solution)/shard_map/while/body/eval_jaxpr/convert_element_type | solution.py:203
  408.0 3.9 fusion.148
  419.1 10.1 %fusion.143 = f32[512,12,1024]{2,0,1:T(8,128)} fusion(bf16[512,12,64]{0,2,1:T(8,128)(2,1)S(1)} %bitcast.201, bf16[1024,64]{0,1:T(8,128)(2,1)S(1)} %get-tuple-element.765), kind=kOutput, calls=%fused_computation.37.clone.1 | convolution fusion | flops 805306368 | bytes 26083328 | tf_op jit(solution)/shard_map/while/body/eval_jaxpr/qeh,kh->eqk/dot_general | solution.py:118
  429.2 10.9 %fusion.145 = f32[1024,64]{0,1:T(8,128)S(1)} fusion(bf16[512,12,64]{0,2,1:T(8,128)(2,1)S(1)} %bitcast.205, f32[512,12,1024]{2,0,1:T(8,128)} %fusion.143, f32[12,512]{1,0:T(8,128)S(1)} %dynamic-slice_bitcast_fusion.2, pred[512,1024]{1,0:T(8,128)(4,1)S(1)} %fusion.144), kind=kOutput, calls=%fused_computation.30.clone.1 | convolution fusion | flops 824180736 | bytes 26763264 | tf_op jit(solution)/shard_map/while/body/eval_jaxpr/eqk,qeh->kh/dot_general | solution.py:206
  440.2 20.6 %fusion.146 = (f32[12,512]{1,0:T(8,128)S(1)}, f32[512,12,1024]{2,0,1:T(8,128)}) fusion(f32[512,12,1024]{2,0,1:T(8,128)} %fusion.143, f32[12,512]{1,0:T(8,128)S(1)} %dynamic-slice_bitcast_fusion.2, pred[512,1024]{1,0:T(8,128)(4,1)S(1)} %fusion.144, bf16[512,12,64]{0,2,1:T(8,128)(2,1)S(1)} %bitcast.206, bf16[1024,64]{0,1:T(8,128)(2,1)S(1)} %get-tuple-element.768), kind=kOutput, calls=%fused_computation.20.clone.1 | convolution fusion | flops 830466048 | bytes 51822592 | tf_op jit(solution)/shard_map/while/body/eval_jaxpr/qeh,kh->eqk/dot_general | solution.py:200
  460.8 16.7 %fusion.147 = bf16[12,512,1024]{2,1,0:T(8,128)(2,1)S(1)} fusion(f32[512,12,1024]{2,0,1:T(8,128)} %get-tuple-element.683, f32[512,12,1024]{2,0,1:T(8,128)} %fusion.143, f32[12,512]{1,0:T(8,128)S(1)} %get-tuple-element.684, f32[12,512]{1,0:T(8,128)S(1)} %dynamic-slice_bitcast_fusion.2, pred[512,1024]{1,0:T(8,128)(4,1)S(1)} %fusion.144), kind=kLoop, calls=%fused_computation.22.clone.1 | loop fusion | flops 31457280 | bytes 63488000 | tf_op jit(solution)/shard_map/while/body/eval_jaxpr/convert_element_type | solution.py:203
  479.9 3.9 fusion.148
  492.1 26.3 %all-reduce.10 = bf16[1024,128]{0,1:T(8,128)(2,1)S(1)} all-reduce(f32[1024,128]{0,1:T(8,128)S(1)} %get-tuple-element.278), channel_id=1, replica_groups=mesh['dp'=16,'expert'=2] {'expert'}, use_global_device_ids=true, to_apply=%region_19.20 | all-reduce | flops 131072 | bytes 786432 | tf_op jit(solution)/shard_map/psum | solution.py:224
  520.6 3.7 fusion.44
  532.3 4.5 fusion.43
  537.7 3.5 all-to-all-start
  541.3 13.3 %all-gather.1 = bf16[2,1,512]{2,1,0:T(2,128)(2,1)S(1)} all-gather(bf16[1,1,512]{2,1,0:T(2,128)(2,1)S(1)} %reshape.363), channel_id=2, replica_groups=mesh['dp'=16,'expert'=2] {'expert'}, dimensions={0}, use_global_device_ids=true | all-gather | bytes 3072 | tf_op jit(solution)/shard_map/all_gather | solution.py:179
  556.5 13.8 %all-reduce.9.cloned.1.call-done = (f32[1024,512]{1,0:T(8,128)}, f32[1024,24]{0,1:T(8,128)}) async-done(((f32[1024,512]{1,0:T(8,128)}, f32[1024,24]{0,1:T(8,128)}), (f32[1024,512]{1,0:T(8,128)}, f32[1024,24]{0,1:T(8,128)})) %all-reduce.9.cloned.1.call-update) | async-done | bytes 2195472 | tf_op jit(solution)/shard_map/psum | solution.py:224
  571.9 4.8 multiply_reduce_fusion
  576.7 62.5 %all-reduce = (f32[512,24]{0,1:T(8,128)}, f32[512]{0:T(512)}, f32[512]{0:T(512)}) all-reduce(f32[512,24]{0,1:T(8,128)S(1)} %fusion.75, f32[512]{0:T(512)S(1)} %get-tuple-element.496, f32[512]{0:T(512)S(1)} %convert_reduce_fusion.1), channel_id=1, replica_groups=mesh['dp'=16,'expert'=2] {'dp'}, use_global_device_ids=true, to_apply=%region_29.30 | all-reduce | flops 13312 | bytes 106496 | tf_op jit(solution)/shard_map/psum | solution.py:246
  642.1 41.9 %all-reduce.7.cloned.1.call-done = (f32[512,768]{1,0:T(8,128)}, f32[768,512]{1,0:T(8,128)}) async-done(((f32[512,768]{1,0:T(8,128)}, f32[768,512]{1,0:T(8,128)}), (f32[512,768]{1,0:T(8,128)}, f32[768,512]{1,0:T(8,128)})) %all-reduce.7.cloned.1.call-update) | async-done | bytes 3145744 | tf_op jit(solution)/shard_map/psum | solution.py:246
  684.0 18.5 %reduce-scatter.26.cloned.1.call-done = f32[32,1024]{1,0:T(8,128)} async-done(((f32[512,1024]{1,0:T(8,128)}), f32[32,1024]{1,0:T(8,128)}) %reduce-scatter.26.cloned.1.call-update) | async-done | bytes 131088
  702.5 64.7 %reduce-scatter.18.cloned.1.call-done = f32[32,1024]{1,0:T(8,128)} async-done(((f32[512,1024]{1,0:T(8,128)}), f32[32,1024]{1,0:T(8,128)}) %reduce-scatter.18.cloned.1.call-update) | async-done | bytes 131088 | tf_op jit(solution)/shard_map/reduce_scatter | solution.py:243
  (229 shorter events, 78.0 us)
Async XLA Ops:
  8.0 202.7 %copy-start = (bf16[768,512]{1,0:T(8,128)(2,1)S(1)}, bf16[768,512]{1,0:T(8,128)(2,1)}, u32[]{:S(2)}) copy-start(bf16[768,512]{1,0:T(8,128)(2,1)} %param.23) | copy-start | bytes 2359300
  8.0 46.9 %copy-start.3 = (bf16[1024,512]{1,0:T(8,128)(2,1)S(1)}, bf16[1024,512]{1,0:T(8,128)(2,1)}, u32[]{:S(2)}) copy-start(bf16[1024,512]{1,0:T(8,128)(2,1)} %param.17) | copy-start | bytes 3145732
  8.0 205.2 %all-gather.8.cloned.1.call-start = ((), (), s32[]{:S(2)}) async-start(), calls=%async_computation.10 | async-start | bytes 1114112 | tf_op jit(solution)/shard_map/all_gather | solution.py:80
  8.8 205.2 %all-gather.12.cloned.1.call-start = ((), (), s32[]{:S(2)}) async-start(), calls=%async_computation.12 | async-start | bytes 1114112 | tf_op jit(solution)/shard_map/all_gather | solution.py:81
  9.5 239.6 %reduce-scatter.14.cloned.1.call-start = ((), (), s32[]{:S(2)}) async-start(), calls=%async_computation.9 | async-start | bytes 3145728 | tf_op jit(solution)/shard_map/reduce_scatter | solution.py:139
  9.6 47.4 %copy-start.46 = (bf16[512,768]{1,0:T(8,128)(2,1)S(1)}, bf16[512,768]{1,0:T(8,128)(2,1)}, u32[]{:S(2)}) copy-start(bf16[512,768]{1,0:T(8,128)(2,1)} %param.22) | copy-start | bytes 2359300
  11.1 45.5 %copy-start.29 = (f32[1024]{0:T(1024)}, f32[1024]{0:T(1024)S(1)}, u32[]{:S(2)}) copy-start(f32[1024]{0:T(1024)S(1)} %broadcast_multiply_fusion.2) | copy-start | bytes 12292
  12.8 43.8 %copy-start.35 = (f32[1024]{0:T(1024)}, f32[1024]{0:T(1024)S(1)}, u32[]{:S(2)}) copy-start(f32[1024]{0:T(1024)S(1)} %add_rsqrt_fusion) | copy-start | bytes 12292
  36.8 19.9 %copy-start.20 = (bf16[512,64]{1,0:T(8,128)(2,1)}, bf16[512,64]{1,0:T(8,128)(2,1)S(1)}, u32[]{:S(2)}) copy-start(bf16[512,64]{1,0:T(8,128)(2,1)S(1)} %all_gather.24) | copy-start | bytes 196612
  75.4 15.7 %copy-start.2 = (f32[512,12,1024]{2,0,1:T(8,128)S(1)}, f32[512,12,1024]{2,0,1:T(8,128)}, u32[]{:S(2)}) copy-start(f32[512,12,1024]{2,0,1:T(8,128)} %get-tuple-element.669) | copy-start | bytes 75497472 | tf_op jit(solution)/shard_map/while
  146.2 15.4 %copy-start.2 = (f32[512,12,1024]{2,0,1:T(8,128)S(1)}, f32[512,12,1024]{2,0,1:T(8,128)}, u32[]{:S(2)}) copy-start(f32[512,12,1024]{2,0,1:T(8,128)} %get-tuple-element.669) | copy-start | bytes 75497472 | tf_op jit(solution)/shard_map/while
  205.9 7.2 copy-start.24
  213.1 5.9 copy-start.4
  213.1 57.1 %all-gather.10.cloned.1.call-start = ((), (), s32[]{:S(2)}) async-start(), calls=%async_computation.11 | async-start | bytes 3145728 | tf_op jit(solution)/shard_map/all_gather | solution.py:145
  213.9 89.9 %all-gather.14.cloned.1.call-start = ((), (), s32[]{:S(2)}) async-start(), calls=%async_computation.13 | async-start | bytes 3145728 | tf_op jit(solution)/shard_map/all_gather | solution.py:146
  214.5 18.2 %all-to-all-start.1 = ((bf16[2,512,256]{2,1,0:T(8,128)(2,1)}), bf16[2,512,256]{2,1,0:T(8,128)(2,1)S(1)}, u32[]{:S(2)}, u32[]{:S(2)}) async-start(bf16[2,512,256]{2,1,0:T(8,128)(2,1)} %bitcast.4), calls=%async_computation.2 | async-start | bytes 1048576 | tf_op jit(solution)/shard_map/all_to_all | solution.py:156
  218.0 117.0 %all-gather.16.cloned.1.call-start = ((), (), s32[]{:S(2)}) async-start(), calls=%async_computation.14 | async-start | bytes 1572864 | tf_op jit(solution)/shard_map/all_gather | solution.py:176
  220.7 114.3 %copy-start.39 = (f32[1024]{0:T(1024)}, f32[1024]{0:T(1024)S(1)}, u32[]{:S(2)}) copy-start(f32[1024]{0:T(1024)S(1)} %fusion.61) | copy-start | bytes 12292
  220.8 93.0 %copy-start.43 = (f32[512]{0:T(512)}, f32[512]{0:T(512)S(1)}, u32[]{:S(2)}) copy-start(f32[512]{0:T(512)S(1)} %dynamic-slice.3) | copy-start | bytes 6148
  232.8 37.4 %copy-start.41 = (f32[512]{0:T(512)S(1)}, f32[512]{0:T(512)}, u32[]{:S(2)}) copy-start(f32[512]{0:T(512)} %param.24) | copy-start | bytes 6148
  250.9 68.7 %copy-start.9 = (f32[512,512]{1,0:T(8,128)}, f32[512,512]{1,0:T(8,128)S(1)}, u32[]{:S(2)}) copy-start(f32[512,512]{1,0:T(8,128)S(1)} %get-tuple-element.546) | copy-start | bytes 3145732
  303.8 6.7 copy-start.14
  313.8 212.9 %reduce-scatter.20.cloned.1.call-start = ((), (), s32[]{:S(2)}) async-start(), calls=%async_computation.17 | async-start | bytes 3145728 | tf_op jit(solution)/shard_map/reduce_scatter | solution.py:168
  319.6 209.7 %reduce-scatter.16.cloned.1.call-start = ((), (), s32[]{:S(2)}) async-start(), calls=%async_computation.15 | async-start | bytes 3145728 | tf_op jit(solution)/shard_map/reduce_scatter | solution.py:165
  324.2 246.2 %all-reduce.9.cloned.1.call-start = ((), (), s32[]{:S(2)}) async-start(), calls=%async_computation.22 | async-start | bytes 4390912 | tf_op jit(solution)/shard_map/psum | solution.py:224
  489.6 28.7 %copy-start.8 = (bf16[1024,512]{1,0:T(8,128)(2,1)S(1)}, bf16[1024,512]{1,0:T(8,128)(2,1)}, u32[]{:S(2)}) copy-start(bf16[1024,512]{1,0:T(8,128)(2,1)} %copy-done.6) | copy-start | bytes 3145732
  492.0 28.6 %copy-start.11 = (bf16[1024,512]{1,0:T(8,128)(2,1)S(1)}, bf16[1024,512]{1,0:T(8,128)(2,1)}, u32[]{:S(2)}) copy-start(bf16[1024,512]{1,0:T(8,128)(2,1)} %all-gather.16.cloned.1.call-done) | copy-start | bytes 3145732
  492.0 28.6 %copy-start.40 = (f32[1024]{0:T(1024)S(1)}, f32[1024]{0:T(1024)}, u32[]{:S(2)}) copy-start(f32[1024]{0:T(1024)} %copy-done.39) | copy-start | bytes 12292
  492.0 150.1 %reduce-scatter.24.cloned.1.call-start = ((), (), s32[]{:S(2)}) async-start(), calls=%async_computation.19 | async-start | bytes 278528
  519.6 122.5 %reduce-scatter.22.cloned.1.call-start = ((), (), s32[]{:S(2)}) async-start(), calls=%async_computation.18 | async-start | bytes 278528
  520.5 163.5 %all-reduce.7.cloned.1.call-start = ((), (), s32[]{:S(2)}) async-start(), calls=%async_computation.21 | async-start | bytes 6291456 | tf_op jit(solution)/shard_map/psum | solution.py:246
  526.6 175.9 %reduce-scatter.26.cloned.1.call-start = ((), (), s32[]{:S(2)}) async-start(), calls=%async_computation.20 | async-start | bytes 2228224
  529.3 237.9 %reduce-scatter.18.cloned.1.call-start = ((), (), s32[]{:S(2)}) async-start(), calls=%async_computation.16 | async-start | bytes 2228224 | tf_op jit(solution)/shard_map/reduce_scatter | solution.py:243
  532.3 9.0 %copy-start.45 = (bf16[512]{0:T(512)(128)(2,1)S(1)}, bf16[512]{0:T(512)(128)(2,1)}, u32[]{:S(2)}) copy-start(bf16[512]{0:T(512)(128)(2,1)} %get-tuple-element.498) | copy-start | bytes 3076
  532.3 22.4 %copy-start.21 = (bf16[512,64]{1,0:T(8,128)(2,1)S(1)}, bf16[512,64]{1,0:T(8,128)(2,1)}, u32[]{:S(2)}) copy-start(bf16[512,64]{1,0:T(8,128)(2,1)} %copy-done.20) | copy-start | bytes 196612
  532.3 22.4 %copy-start.23 = (bf16[512,64]{1,0:T(8,128)(2,1)S(1)}, bf16[512,64]{1,0:T(8,128)(2,1)}, u32[]{:S(2)}) copy-start(bf16[512,64]{1,0:T(8,128)(2,1)} %copy-done.22) | copy-start | bytes 196612
  536.8 33.6 %copy-start.27 = (s32[1024,8]{0,1:T(8,128)S(1)}, s32[1024,8]{0,1:T(8,128)}, u32[]{:S(2)}) copy-start(s32[1024,8]{0,1:T(8,128)} %param.27) | copy-start | bytes 98308
  536.8 34.6 %copy-start.25 = (f32[1024,8]{0,1:T(8,128)S(1)}, f32[1024,8]{0,1:T(8,128)}, u32[]{:S(2)}) copy-start(f32[1024,8]{0,1:T(8,128)} %copy-done.24) | copy-start | bytes 98308
  536.8 34.6 %copy-start.32 = (f32[1024]{0:T(1024)S(1)}, f32[1024]{0:T(1024)}, u32[]{:S(2)}) copy-start(f32[1024]{0:T(1024)} %copy-done.31) | copy-start | bytes 12292
  536.8 34.6 %copy-start.38 = (f32[1024]{0:T(1024)S(1)}, f32[1024]{0:T(1024)}, u32[]{:S(2)}) copy-start(f32[1024]{0:T(1024)} %copy-done.37) | copy-start | bytes 12292
  536.9 35.0 %copy-start.5 = (bf16[1024,512]{1,0:T(8,128)(2,1)S(1)}, bf16[1024,512]{1,0:T(8,128)(2,1)}, u32[]{:S(2)}) copy-start(bf16[1024,512]{1,0:T(8,128)(2,1)} %param.17) | copy-start | bytes 3145732
  536.9 35.0 %copy-start.30 = (f32[1024]{0:T(1024)S(1)}, f32[1024]{0:T(1024)}, u32[]{:S(2)}) copy-start(f32[1024]{0:T(1024)} %copy-done.29) | copy-start | bytes 12292
  536.9 35.0 %copy-start.34 = (bf16[512,24]{0,1:T(8,128)(2,1)S(1)}, bf16[512,24]{0,1:T(8,128)(2,1)}, u32[]{:S(2)}) copy-start(bf16[512,24]{0,1:T(8,128)(2,1)} %param.21) | copy-start | bytes 73732
  536.9 35.0 %copy-start.36 = (f32[1024]{0:T(1024)S(1)}, f32[1024]{0:T(1024)}, u32[]{:S(2)}) copy-start(f32[1024]{0:T(1024)} %copy-done.35) | copy-start | bytes 12292
  536.9 35.0 %copy-start.42 = (f32[512]{0:T(512)S(1)}, f32[512]{0:T(512)}, u32[]{:S(2)}) copy-start(f32[512]{0:T(512)} %param.18) | copy-start | bytes 6148
  537.7 16.9 %all-to-all-start = ((bf16[512,2,256]{2,0,1:T(8,128)(2,1)}), bf16[512,2,256]{2,0,1:T(8,128)(2,1)S(1)}, u32[]{:S(2)}, u32[]{:S(2)}) async-start(bf16[512,2,256]{2,0,1:T(8,128)(2,1)} %bitcast.133), calls=%async_computation.1 | async-start | bytes 1048576 | tf_op jit(solution)/shard_map/all_to_all | solution.py:153
  571.9 67.3 %copy-start.12 = (bf16[1024,512]{1,0:T(8,128)(2,1)S(1)}, bf16[1024,512]{1,0:T(8,128)(2,1)}, u32[]{:S(2)}) copy-start(bf16[1024,512]{1,0:T(8,128)(2,1)} %all-gather.16.cloned.1.call-done) | copy-start | bytes 3145732
  684.0 86.6 %copy-start.15 = (f32[768,512]{1,0:T(8,128)S(1)}, f32[768,512]{1,0:T(8,128)}, u32[]{:S(2)}) copy-start(f32[768,512]{1,0:T(8,128)} %get-tuple-element.792) | copy-start | bytes 4718596
  (18 other events, 48.9 us)
Sparse Core Ops, SparseCore 0:
  11.3 40.9 all-gather.7
  54.6 36.9 all-gather.11
  215.6 54.5 all-gather.9
  271.7 32.0 all-gather.13
  492.1 78.1 all-reduce.8
  574.9 109.0 all-reduce.6
Sparse Core Ops, SparseCore 1:
  213.2 35.9 reduce-scatter.13
  313.8 21.1 all-gather.15
  337.2 31.8 reduce-scatter.19
  371.3 31.7 reduce-scatter.15
  519.7 55.9 reduce-scatter.23
  580.2 55.1 reduce-scatter.21
  639.9 62.5 reduce-scatter.25
  706.7 60.5 reduce-scatter.17
where the time goes:
time: 794 us; the launch traced here: 779 us
  waiting for transfers between devices  227 us (29%)
  matrix products  186 us (23%)
  blocking collectives  144 us (18%)
  local copies, waits for them, and re-layouts  102 us (13%)
  other arithmetic  83.7 us (11%)
  between operations  17.3 us (2%)
  loops' own time  11.1 us (1%)
  starting transfers between devices  7.99 us (1%)
    dynamic_update_slice x8, local copies, waits for them, and re-layouts, shards(): lax.map(attend_block, jnp.arange(item_count, dtype=jnp.int32))  65.6 us
    reduce_scatter x1, waiting for transfers between devices, shards(): lax.psum_scatter(grad_w_one, 'dp', scatter_dimension=0, tiled=True)  64.7 us
    psum x1, blocking collectives, shards(): lax.psum((grad_wq, grad_wo, grad_wr, grad_gain_one, grad_gain_two), 'dp')  62.5 us
    psum x1, waiting for transfers between devices, shards(): lax.psum((grad_wq, grad_wo, grad_wr, grad_gain_one, grad_gain_two), 'dp')  41.9 us
    dot_general x2, matrix products, back_block(): jnp.einsum('qeh,kh->eqk', head_grad, value_seq, preferred_element_type=jn...  41.5 us
    dot_general x4, matrix products, block_inputs(): jnp.einsum('qeh,kh->eqk', query_block, keys_all, preferred_element_type=j...  40.9 us
    convert_element_type x2, other arithmetic, back_block(): grad_s = (probs_full * (grad_p - jnp.sum(probs_full * grad_p, axis=-1, ke...  33.7 us
    all_gather x1, waiting for transfers between devices, shards(): lax.all_gather(output_full, 'expert', axis=0, tiled=True)  28.6 us
  transfers between devices with their start and end apart: 16, of which 9 were waited for; matrix products, arithmetic and copies ran while one was open for 44% of the time, Pallas kernels for 0%

commit v1 on v0

v1 whole, which is shorter than its diff:
```python
import functools

import jax
import jax.numpy as jnp
from jax import lax
from jax.experimental import pallas as pl
from jax.experimental.pallas import tpu as pltpu
from jax.sharding import PartitionSpec as P

f32 = jnp.float32
bf16 = jnp.bfloat16
eps = 1e-05
lowest = -1e30
rb = 128


def nn(left, right):
    return jnp.dot(left, right, preferred_element_type=f32)


def nt(left, right):
    return lax.dot_general(left, right, (((1,), (1,)), ((), ())), preferred_element_type=f32)


def tn(left, right):
    return lax.dot_general(left, right, (((0,), (0,)), ((), ())), preferred_element_type=f32)


def norm_rows(x):
    centred = x - jnp.mean(x, axis=-1, keepdims=True)
    inv = lax.rsqrt(jnp.mean(centred * centred, axis=-1, keepdims=True) + eps)
    return centred * inv, inv


def norm_back(u, normed, inv, gain):
    w = u * gain
    return inv * (
        w
        - jnp.mean(w, axis=-1, keepdims=True)
        - normed * jnp.mean(w * normed, axis=-1, keepdims=True)
    )


def lanes(shape):
    return lax.broadcasted_iota(jnp.int32, shape, len(shape) - 1)


def main_kernel(
    len_ref, tok, gain1, wkv, wr, wq, wo, gain2, W, ids, go,
    out_ref, gres_ref, h1_own, h1T, gh1q, kvg, glog, gF, gwo, gwq, gain2_ref,
    h1, KK, VV, KKT, VVT, idl, gateb, dense, Qs, PT, O, qf, gated, n2, r2, res,
    h2, h2T, gfT, gf, actS, giS, gh2, acc, gatt, gg, dOs, gdense, DS, gK, gV, dQ, gq,
):
    rows, width = tok.shape[0] * rb, tok.shape[2]
    nb = tok.shape[0] // 2
    top = ids.shape[2]
    groups = wq.shape[1] // 128
    ffh = W.shape[3] // 2
    y = lax.axis_index("expert")
    length = len_ref[0]

    def own(i):
        return 2 * i + y

    @pl.loop(0, 2 * nb)
    def _(b):
        normed, _ = norm_rows(tok[b].astype(f32))
        h = (normed * gain1[...]).astype(bf16)
        h1[b] = h
        kv = nn(h, wkv[...])
        at = pl.ds(pl.multiple_of(b * rb, rb), rb)
        k2, v2 = kv[:, :128], kv[:, 128:]
        KK[at, :] = k2.astype(bf16)
        VV[at, :] = v2.astype(bf16)
        KKT[:, at] = k2.T.astype(bf16)
        VVT[:, at] = v2.T.astype(bf16)

    lane = lanes((rb, 128))
    half = (lane >= 64).astype(jnp.int32)

    @pl.loop(0, nb)
    def _(i):
        h = h1[own(i)]
        at = pl.ds(pl.multiple_of(i * rb, rb), rb)
        h1_own[at, :] = h
        h1T[:, at] = h.astype(f32).T.astype(bf16)
        logits = nn(h, wr[...])
        here = ids[own(i)]
        spread = [jnp.broadcast_to(here[:, k : k + 1], (rb, 128)) for k in range(top)]
        chosen = lane == spread[0]
        for k in range(1, top):
            chosen = chosen | (lane == spread[k])
        most = jnp.max(jnp.where(chosen, logits, lowest), axis=-1, keepdims=True)
        e = jnp.where(chosen, jnp.exp(jnp.where(chosen, logits - most, 0.0)), 0.0)
        g = e / jnp.sum(e, axis=-1, keepdims=True)
        dense[at, :] = g
        for k in range(top):
            gk = jnp.sum(jnp.where(lane == spread[k], g, 0.0), axis=-1, keepdims=True)
            gateb[i, k] = jnp.broadcast_to(gk, (rb, 128))
            idl[i, k] = spread[k] - half
        qf[...] = 0.125 * nn(h, wq[...])

        @pl.loop(0, rb // 16)
        def _(c):
            cut = pl.ds(pl.multiple_of(c * 16, 16), 16)
            parts = [qf[cut, pl.ds(128 * g, 128)] for g in range(groups)]
            for k in range(top):
                mine = idl[i, k, cut, :]
                val = jnp.zeros((16, 128), f32)
                for g in range(groups):
                    val = jnp.where(mine == 2 * g, parts[g], val)
                Qs[i, k, cut, :] = val.astype(bf16)

    diag = lax.broadcasted_iota(jnp.int32, (256, 256), 0) <= rb * y + lanes((256, 256)) % 128
    for i in range(nb):
        nk = 256 * i
        start = 128 * i * (i + 1)

        @pl.loop(0, top // 2)
        def _(p):
            q = Qs[i, pl.ds(2 * p, 2)].reshape(256, 128)
            cols = pl.ds(pl.multiple_of(p * 256, 256), 256)
            s1 = nt(KK[nk : nk + 256, :], q)
            s1 = jnp.where(diag, s1, lowest)
            m = jnp.max(s1, axis=0, keepdims=True)
            if nk:
                s0 = nt(KK[0:nk, :], q)
                m = jnp.maximum(m, jnp.max(s0, axis=0, keepdims=True))
                p0 = jnp.exp(s0 - m)
            p1 = jnp.exp(s1 - m)
            tot = jnp.sum(p1, axis=0, keepdims=True)
            if nk:
                tot = tot + jnp.sum(p0, axis=0, keepdims=True)
            inv = 1.0 / tot
            p1 = (p1 * inv).astype(bf16)
            PT[start + nk : start + nk + 256, cols] = p1
            o = nn(VVT[:, nk : nk + 256], p1)
            if nk:
                p0 = (p0 * inv).astype(bf16)
                PT[start : start + nk, cols] = p0
                o = o + nn(VVT[:, 0:nk], p0)
            O[i, pl.ds(2 * p, 2)] = o.T.reshape(2, rb, 128)

    @pl.loop(0, nb)
    def _(i):
        at = pl.ds(pl.multiple_of(i * rb, rb), rb)

        @pl.loop(0, rb // 16)
        def _(c):
            cut = pl.ds(pl.multiple_of(c * 16, 16), 16)
            cutr = pl.ds(pl.multiple_of(i * rb + c * 16, 16), 16)
            mine = [idl[i, k, cut, :] for k in range(top)]
            vals = [gateb[i, k, cut, :] * O[i, k, cut, :] for k in range(top)]
            for g in range(groups):
                val = jnp.zeros((16, 128), f32)
                for k in range(top):
                    val = jnp.where(mine[k] == 2 * g, vals[k], val)
                gated[cutr, pl.ds(128 * g, 128)] = val.astype(bf16)

        valid = (rb * own(i) + lax.broadcasted_iota(jnp.int32, (rb, 1), 0) < length).astype(f32)
        r = tok[own(i)].astype(f32) + valid * nn(gated[at, :], wo[...])
        res[at, :] = r
        normed, inv = norm_rows(r)
        n2[at, :] = normed
        r2[at, :] = inv
        h = normed * gain2[...]
        h2[at, :] = h.astype(bf16)
        h2T[:, at] = h.T.astype(bf16)
        gfi = valid * go[at, :].astype(f32)
        gf[at, :] = gfi.astype(bf16)
        gfT[:, at] = gfi.T.astype(bf16)

    c0 = 0.7978845608028654
    c1 = 0.044715
    ch = 512
    for e in range(2):
        for j in range(ffh // ch):
            first = e == 0 and j == 0

            @pl.loop(0, nb)
            def _(i):
                at = pl.ds(pl.multiple_of(i * rb, rb), rb)
                w1 = W[e, :, :, j * ch : (j + 1) * ch].reshape(width, ch)
                w2 = W[e, :, :, ffh + j * ch : ffh + (j + 1) * ch].reshape(width, ch)
                v = nn(h2[at, :], w1)
                ga = nn(gf[at, :], w2)
                vv = v * v
                t = jnp.tanh(v * (c0 + (c0 * c1) * vv))
                hp = 0.5 + 0.5 * t
                act = (v * hp).astype(bf16)
                d = hp + (0.5 * v) * (1.0 - t * t) * (c0 + (3 * c0 * c1) * vv)
                gi = (d * ga).astype(bf16)
                actS[at, :] = act
                giS[at, :] = gi
                a = nt(act, w2)
                b = nt(gi, w1)
                if not first:
                    a = a + acc[at, :]
                    b = b + gh2[at, :]
                acc[at, :] = a
                gh2[at, :] = b

            gF[e, :, :, j * ch : (j + 1) * ch] = (
                nn(h2T[...], giS[...]).astype(bf16).reshape(16, width // 16, ch)
            )
            gF[e, :, :, ffh + j * ch : ffh + (j + 1) * ch] = (
                nn(gfT[...], actS[...]).astype(bf16).reshape(16, width // 16, ch)
            )

    gain2_ref[...] = jnp.zeros_like(gain2_ref)

    @pl.loop(0, nb)
    def _(i):
        at = pl.ds(pl.multiple_of(i * rb, rb), rb)
        valid = (rb * own(i) + lax.broadcasted_iota(jnp.int32, (rb, 1), 0) < length).astype(f32)
        out_ref[at, :] = (res[at, :] + valid * acc[at, :]).astype(bf16)
        u, normed = gh2[at, :], n2[at, :]
        gain2_ref[...] += jnp.sum(u * normed, axis=0, keepdims=True)
        gr = go[at, :].astype(f32) + norm_back(u, normed, r2[at, :], gain2[...])
        gres_ref[at, :] = gr
        ga = (valid * gr).astype(bf16)
        gatt[at, :] = ga
        gg[...] = nt(ga, wo[...])

        @pl.loop(0, rb // 16)
        def _(c):
            cut = pl.ds(pl.multiple_of(c * 16, 16), 16)
            cutr = pl.ds(pl.multiple_of(i * rb + c * 16, 16), 16)
            parts = [gg[cut, pl.ds(128 * g, 128)] for g in range(groups)]
            ln = lanes((16, 128))
            hf = (ln >= 64).astype(jnp.int32)
            gd = jnp.zeros((16, 128), f32)
            for k in range(top):
                mine = idl[i, k, cut, :]
                val = jnp.zeros((16, 128), f32)
                for g in range(groups):
                    val = jnp.where(mine == 2 * g, parts[g], val)
                dot = jnp.sum(val * O[i, k, cut, :], axis=-1, keepdims=True)
                gd = jnp.where(mine + hf == ln, dot, gd)
                dOs[i, k, cut, :] = (gateb[i, k, cut, :] * val).astype(bf16)
            dn = dense[cutr, :]
            gs = dn * (gd - jnp.sum(dn * gd, axis=-1, keepdims=True))
            glog[cutr, :] = gs.astype(bf16)

    gwo[...] = tn(gated[...], gatt[...]).astype(bf16)

    gK[...] = jnp.zeros_like(gK)
    gV[...] = jnp.zeros_like(gV)
    for i in range(nb):
        nk = 256 * (i + 1)
        start = 128 * i * (i + 1)

        @pl.loop(0, top // 2)
        def _(p):
            do = dOs[i, pl.ds(2 * p, 2)].reshape(256, 128)
            cols = pl.ds(pl.multiple_of(p * 256, 256), 256)
            dp = nt(VV[0:nk, :], do)
            pr = PT[start : start + nk, cols].astype(f32)
            d = jnp.sum(pr * dp, axis=0, keepdims=True)
            ds = (pr * (dp - d)).astype(bf16)
            DS[0:nk, cols] = ds
            dq = nn(KKT[:, 0:nk], ds)
            dQ[pl.ds(2 * p, 2)] = dq.T.reshape(2, rb, 128)

        gK[0:nk, :] += nn(DS[0:nk, :], Qs[i].reshape(top * rb, 128))
        gV[0:nk, :] += nn(PT[start : start + nk, :], dOs[i].reshape(top * rb, 128))

        @pl.loop(0, rb // 16)
        def _(c):
            cut = pl.ds(pl.multiple_of(c * 16, 16), 16)
            cutr = pl.ds(pl.multiple_of(i * rb + c * 16, 16), 16)
            mine = [idl[i, k, cut, :] for k in range(top)]
            vals = [dQ[k, cut, :] for k in range(top)]
            for g in range(groups):
                val = jnp.zeros((16, 128), f32)
                for k in range(top):
                    val = jnp.where(mine[k] == 2 * g, vals[k], val)
                gq[cutr, pl.ds(128 * g, 128)] = val.astype(bf16) * 0.125

    gwq[...] = nn(h1T[...], gq[...]).astype(bf16)
    gh1q[...] = nt(gq[...], wq[...])

    @pl.loop(0, 2 * nb)
    def _(b):
        at = pl.ds(pl.multiple_of(b * rb, rb), rb)
        a, c = gK[at, :], gV[at, :]
        a = a + pltpu.roll(a, 64, 1)
        c = c + pltpu.roll(c, 64, 1)
        kvg[b] = jnp.where(lane < 64, a, c)


def shards(
    tokens, gain_attn, w_key, w_value, w_router, w_query, w_out, gain_ffn,
    w_hidden, w_output, expert_ids, lengths, grad_out,
):
    rows, width = tokens.shape
    y = lax.axis_index("expert")
    nb = rows // rb // 2
    top = expert_ids.shape[1]
    n_experts = w_router.shape[1]
    hd = w_key.shape[1]
    own_rows = rows // 2
    pay = 2 * w_hidden.shape[1]
    kv_full = lax.all_gather(jnp.concatenate((w_key, w_value), 1), "dp", axis=0, tiled=True)
    wk, wv = kv_full[:, :hd], kv_full[:, hd:]
    wkv4 = jnp.concatenate((wk, wk, wv, wv), 1)
    wr = jnp.pad(w_router, ((0, 0), (0, 128 - n_experts)))
    W = lax.all_gather(
        jnp.concatenate((w_hidden, w_output.T), 1), ("expert", "dp"), axis=0, tiled=True
    ).reshape(2, 16, width // 16, pay)
    wq = lax.all_gather(w_query, "expert", axis=1, tiled=True)
    wo = lax.all_gather(w_out, "expert", axis=0, tiled=True)
    go_all = lax.all_gather(grad_out, "expert", axis=1, tiled=True)
    go = lax.dynamic_index_in_dim(
        go_all.reshape(nb, 2, rb, width), y, 1, keepdims=False
    ).reshape(own_rows, width)
    tok = tokens.reshape(2 * nb, rb, width)
    ids = expert_ids.reshape(2 * nb, rb, top)
    sds = jax.ShapeDtypeStruct
    fq = wq.shape[1]
    total = 128 * nb * (nb + 1)
    vm = pltpu.VMEM
    tk = top * rb
    outs = pl.pallas_call(
        main_kernel,
        out_shape=(
            sds((own_rows, width), bf16),
            sds((own_rows, width), f32),
            sds((own_rows, width), bf16),
            sds((width, own_rows), bf16),
            sds((own_rows, width), f32),
            sds((2 * nb, rb, 128), f32),
            sds((own_rows, 128), bf16),
            sds(W.shape, bf16),
            sds(wo.shape, bf16),
            sds(wq.shape, bf16),
            sds((1, width), f32),
        ),
        in_specs=[pl.BlockSpec(memory_space=pltpu.SMEM)]
        + [pl.BlockSpec(memory_space=pltpu.VMEM)] * 10,
        out_specs=[pl.BlockSpec(memory_space=pltpu.VMEM)] * 11,
        scratch_shapes=[
            vm((2 * nb, rb, width), bf16),
            vm((rows, 128), bf16),
            vm((rows, 128), bf16),
            vm((128, rows), bf16),
            vm((128, rows), bf16),
            vm((nb, top, rb, 128), jnp.int32),
            vm((nb, top, rb, 128), f32),
            vm((own_rows, 128), f32),
            vm((nb, top, rb, 128), bf16),
            vm((total, tk), bf16),
            vm((nb, top, rb, 128), f32),
            vm((rb, fq), f32),
            vm((own_rows, fq), bf16),
            vm((own_rows, width), f32),
            vm((own_rows, 1), f32),
            vm((own_rows, width), f32),
            vm((own_rows, width), bf16),
            vm((width, own_rows), bf16),
            vm((width, own_rows), bf16),
            vm((own_rows, width), bf16),
            vm((own_rows, 512), bf16),
            vm((own_rows, 512), bf16),
            vm((own_rows, width), f32),
            vm((own_rows, width), f32),
            vm((own_rows, width), bf16),
            vm((rb, fq), f32),
            vm((nb, top, rb, 128), bf16),
            vm((own_rows, 128), f32),
            vm((rows, tk), bf16),
            vm((rows, 128), f32),
            vm((rows, 128), f32),
            vm((top, rb, 128), f32),
            vm((own_rows, fq), bf16),
        ],
        compiler_params=pltpu.CompilerParams(vmem_limit_bytes=62 * 2**20),
    )(
        lengths, tok, gain_attn[None], wkv4, wr, wq, wo, gain_ffn[None], W, ids, go,
    )
    out_own, gres, h1_own, h1T, gh1q, kvg, glog, gF, gwo, gwq, gain2 = outs
    kv_sum = lax.psum(kvg, "expert")
    kv_own = (
        lax.dynamic_index_in_dim(kv_sum.reshape(nb, 2, rb, 128), y, 1, keepdims=False)
        .reshape(own_rows, 128)
        .astype(bf16)
    )
    gh1 = gh1q + nt(kv_own, kv_full) + nt(glog, wr)
    own_x = lax.dynamic_index_in_dim(
        tokens.reshape(nb, 2, rb, width), y, 1, keepdims=False
    ).reshape(own_rows, width)
    n1, r1 = norm_rows(own_x.astype(f32))
    gain1_rows = jnp.sum(gh1 * n1, axis=0)
    gt = (gres + norm_back(gh1, n1, r1, gain_attn)).astype(bf16)

    def weave(own):
        both = lax.all_gather(own.reshape(nb, 1, rb, -1), "expert", axis=1, tiled=True)
        return both.reshape(rows, -1)

    grad_tokens = weave(gt)
    both = lax.all_to_all(
        out_own.reshape(nb, 1, rb, width), "expert", split_axis=3, concat_axis=1, tiled=True
    )
    output = both.reshape(rows, width // 2)
    gkv = lax.psum_scatter(
        lax.psum(nn(h1T, kv_own), "expert"), "dp", scatter_dimension=0, tiled=True
    )
    gF_own = lax.psum_scatter(
        gF.reshape(2, width, pay), "expert", scatter_dimension=0, tiled=True
    ).reshape(width, pay).astype(f32)
    gF_own = lax.psum_scatter(gF_own, "dp", scatter_dimension=0, tiled=True)
    gwq_own = lax.psum_scatter(gwq, "expert", scatter_dimension=1, tiled=True)
    gwo_own = lax.psum_scatter(gwo, "expert", scatter_dimension=0, tiled=True)
    gwq_own, gwo_own = lax.psum((gwq_own.astype(f32), gwo_own.astype(f32)), "dp")
    grad_router, gain1g, gain2g = lax.psum(
        (nn(h1T, glog)[:, :n_experts], gain1_rows, gain2[0]), ("dp", "expert")
    )
    return (
        output, grad_tokens, gkv[:, :hd], gkv[:, hd:], grad_router, gwq_own, gwo_own,
        gF_own[:, : pay // 2], gF_own[:, pay // 2 :].T, gain1g, gain2g,
    )


def solution(mesh):
    placed = (
        P("dp", None), P(), P("dp", None), P("dp", None), P(), P(None, "expert"),
        P("expert", None), P(), P("dp", "expert"), P("expert", "dp"), P("dp", None),
        P("dp"), P("dp", "expert"),
    )
    return jax.shard_map(
        shards,
        mesh=mesh,
        in_specs=placed,
        out_specs=(
            P("dp", "expert"), P("dp", None), P("dp", None), P("dp", None), P(),
            P(None, "expert"), P("expert", None), P("dp", "expert"), P("expert", "dp"),
            P(), P(),
        ),
        check_vma=False,
    )
```

time: 794 us -> 538 us (0.68); the launches traced: 779 us -> 537 us
  matrix products: 186 us -> 3.38 us
  local copies, waits for them, and re-layouts: 102 us -> 13.4 us
  Pallas kernels: 0 us -> 76.7 us
  other arithmetic: 83.7 us -> 7.35 us
  blocking collectives: 144 us -> 194 us
  loops' own time: 11.1 us -> 0 us
    dot_general x32 -> x4, matrix products: 186 us -> 3.38 us  [the longest x2 2.13 us: nt(): lax.dot_general(left, right, (((1,), (1,)), ((), ())), preferred_element_...]
    psum x2 -> x4, blocking collectives: 88.8 us -> 171 us  [the longest x1 90.4 us: shards(): lax.psum((gwq_own.astype(f32), gwo_own.astype(f32)), 'dp')]
    pallas_call x0 -> x1, Pallas kernels: none -> 76.7 us  [shards(): pl.pallas_call(main_kernel, out_shape=(sds((own_rows, width), bf16), sds(...]
    all_gather x5, waiting for transfers between devices: 58.4 us -> 131 us  [the longest x1 65.4 us: shards(): lax.all_gather(jnp.concatenate((w_hidden, w_output.T), 1), ('expert', 'dp...]
    dynamic_update_slice x9 -> x0, local copies, waits for them, and re-layouts: 66 us -> none  [the longest x8 65.6 us: shards(): lax.map(attend_block, jnp.arange(item_count, dtype=jnp.int32))]
    psum x2 -> x0, waiting for transfers between devices: 55.8 us -> none  [the longest x1 41.9 us: shards(): lax.psum((grad_wq, grad_wo, grad_wr, grad_gain_one, grad_gain_two), 'dp')]
    convert_element_type x9 -> x2, other arithmetic: 45.7 us -> 5.27 us  [the longest x1 4.06 us: shards(): gF_own = lax.psum_scatter(gF.reshape(2, width, pay), 'expert', scatter_di...]
    reduce_sum x14 -> x2, other arithmetic: 33 us -> 0.43 us  [the longest x1 0.28 us: norm_rows(): inv = lax.rsqrt(jnp.mean(centred * centred, axis=-1, keepdims=True) + eps)]
  transfers between devices with their start and end apart: 16 -> 11, of which waited for: 9 -> 9; matrix products, arithmetic and copies ran while one was open for 44% -> 4% of each run, Pallas kernels for 0% -> 0%
where the time goes in v1:
time: 538 us; the launch traced here: 537 us
  waiting for transfers between devices  223 us (41%)
  blocking collectives  194 us (36%)
  Pallas kernels  76.7 us (14%)
  between operations  15.1 us (3%)
  local copies, waits for them, and re-layouts  13.4 us (2%)
  other arithmetic  7.35 us (1%)
    psum x1, blocking collectives, shards(): lax.psum((gwq_own.astype(f32), gwo_own.astype(f32)), 'dp')  90.4 us
    pallas_call x1, Pallas kernels, shards(): pl.pallas_call(main_kernel, out_shape=(sds((own_rows, width), bf16), sds(...  76.7 us
    all_gather x1, waiting for transfers between devices, shards(): lax.all_gather(jnp.concatenate((w_hidden, w_output.T), 1), ('expert', 'dp...  65.4 us
    psum x1, blocking collectives, shards(): lax.psum((nn(h1T, glog)[:, :n_experts], gain1_rows, gain2[0]), ('dp', 'ex...  41.4 us
    psum x1, blocking collectives, shards(): kv_sum = lax.psum(kvg, 'expert')  30.2 us
    reduce_scatter x1, waiting for transfers between devices, shards(): gwo_own = lax.psum_scatter(gwo, 'expert', scatter_dimension=0, tiled=True)  28.9 us
    all_gather x1, waiting for transfers between devices, shards(): wo = lax.all_gather(w_out, 'expert', axis=0, tiled=True)  28.8 us
    reduce_scatter x1, waiting for transfers between devices, shards(): gwq_own = lax.psum_scatter(gwq, 'expert', scatter_dimension=1, tiled=True)  26.8 us
  transfers between devices with their start and end apart: 11, of which 9 were waited for; matrix products, arithmetic and copies ran while one was open for 4% of the time, Pallas kernels for 0%

profile of v1, /device:TPU:0, one launch (start us, length us, event | category | flops | bytes accessed | tf_op | source)
XLA Modules:
  0.0 537.4 jit_solution(6060812877812244935)
XLA Ops:
  7.3 0.7 all-gather.12.cloned.1.call-update
  8.0 0.7 all-gather.6.cloned.1.call-update
  8.8 0.7 all-gather.8.cloned.1.call-update
  9.5 0.7 pad_maximum_fusion.1
  10.2 0.0 reduce-scatter.10.cloned.1.call-start
  10.3 0.1 copy.36
  10.4 1.0 copy.37
  12.1 0.7 pad.4.wr
  12.8 0.1 pad_maximum_fusion.2
  12.8 23.4 %all_gather.18 = bf16[512,128]{1,0:T(8,128)(2,1)S(1)} all-gather(bf16[32,128]{1,0:T(8,128)(2,1)S(1)} %pad_maximum_fusion.2), channel_id=1, replica_groups=mesh['dp'=16,'expert'=2] {'dp'}, dimensions={0}, use_global_device_ids=true | all-gather | bytes 139264 | tf_op jit(solution)/shard_map/all_gather | solution.py:304
  36.2 0.1 fusion.5
  36.3 0.9 pad_maximum_fusion.wkv
  37.2 1.9 constant_dynamic-slice_fusion
  39.1 23.3 %all-gather.6.cloned.1.call-done.wq = bf16[512,1536]{1,0:T(8,128)(2,1)} async-done(((bf16[512,768]{1,0:T(8,128)(2,1)}), bf16[512,1536]{1,0:T(8,128)(2,1)}) %all-gather.6.cloned.1.call-update) | async-done | bytes 1572880 | tf_op jit(solution)/shard_map/all_gather | solution.py:311
  62.4 28.8 %all-gather.8.cloned.1.call-done.wo = bf16[1536,512]{1,0:T(8,128)(2,1)} async-done(((bf16[768,512]{1,0:T(8,128)(2,1)}), bf16[1536,512]{1,0:T(8,128)(2,1)}) %all-gather.8.cloned.1.call-update) | async-done | bytes 1572880 | tf_op jit(solution)/shard_map/all_gather | solution.py:312
  91.2 65.4 %all-gather.10.cloned.1.call-done = bf16[1024,2048]{1,0:T(8,128)(2,1)} async-done(((bf16[32,2048]{1,0:T(8,128)(2,1)}), bf16[1024,2048]{1,0:T(8,128)(2,1)}) %all-gather.10.cloned.1.call-update) | async-done | bytes 4194320 | tf_op jit(solution)/shard_map/all_gather | solution.py:308
  156.6 76.7 %shard_map.212 = (bf16[512,512]{1,0:T(8,128)(2,1)}, f32[512,512]{1,0:T(8,128)}, bf16[512,512]{1,0:T(8,128)(2,1)}, bf16[512,512]{1,0:T(8,128)(2,1)}, f32[512,512]...) custom-call(s32[1]{0:T(128)S(6)} %copy.51.len_ref, ...), custom_call_target="tpu_custom_call" | custom-call | tf_op jit(solution)/shard_map/pallas_call | solution.py:324
  233.3 0.0 reduce-scatter.14.cloned.1.call-start
  233.4 1.1 copy-done
  234.5 0.1 convert_reduce_fusion
  234.7 0.3 multiply_reduce_fusion.2
  235.0 30.2 %all-reduce.5 = bf16[4,2,128,128]{3,2,1,0:T(8,128)(2,1)S(1)} all-reduce(f32[4,2,128,128]{3,2,1,0:T(8,128)S(1)} %bitcast.67), channel_id=1, replica_groups=mesh['dp'=16,'expert'=2] {'expert'}, use_global_device_ids=true, to_apply=%region_2.3 | all-reduce | flops 131072 | bytes 786432 | tf_op jit(solution)/shard_map/psum | solution.py:382
  265.3 1.0 fusion.8
  266.3 1.5 convolution_add_fusion.1
  267.8 0.0 all-gather.14.cloned.1.call-start
  267.9 0.6 multiply_reduce_fusion
  268.5 0.6 copy-done.2
  269.1 1.2 add_convert_fusion
  270.4 0.7 reduce-scatter.6.cloned.1.call-update
  271.2 0.7 reduce-scatter.8.cloned.1.call-update
  271.9 25.2 %reduce-scatter.10.cloned.1.call-done = bf16[1,512,2048]{2,1,0:T(8,128)(2,1)} async-done(((bf16[2,512,2048]{2,1,0:T(8,128)(2,1)}), bf16[1,512,2048]{2,1,0:T(8,128)(2,1)}) %reduce-scatter.10.cloned.1.call-update) | async-done | bytes 2097168 | tf_op jit(solution)/shard_map/reduce_scatter | solution.py:408
  297.1 4.1 bitcast_convert_fusion
  301.2 1.0 copy-done.4
  302.2 1.1 copy.39
  303.2 3.5 all-to-all-start
  306.7 0.2 fusion.1
  307.0 41.4 %all-reduce.1 = (f32[512,24]{0,1:T(8,128)}, f32[512]{0:T(512)}, f32[512]{0:T(512)}) all-reduce(f32[512,24]{0,1:T(8,128)S(1)} %fusion.1, f32[512]{0:T(512)S(1)} %get-tuple-element.31, f32[512]{0:T(512)S(1)} %bitcast.74), channel_id=1, replica_groups=mesh['dp'=16,'expert'=2] {'dp','expert'}, use_global_device_ids=true, to_apply=%region_7.8 | all-reduce | flops 13312 | bytes 106496 | tf_op jit(solution)/shard_map/psum | solution.py:415
  348.4 1.1 copy.40
  349.5 5.3 reduce-scatter.14.cloned.1.call-done
  354.8 8.8 %psum.56 = f32[32,128]{1,0:T(8,128)S(1)} all-reduce(f32[32,128]{1,0:T(8,128)} %reduce-scatter.14.cloned.1.call-done), channel_id=1, replica_groups=mesh['dp'=16,'expert'=2] {'expert'}, use_global_device_ids=true, to_apply=%region_5.6 | all-reduce | flops 4096 | bytes 32768 | tf_op jit(solution)/shard_map/psum | solution.py:406
  363.6 0.7 fusion.6
  364.3 13.1 %all-gather.14.cloned.1.call-done = bf16[4,2,128,512]{3,2,0,1:T(8,128)(2,1)} async-done(((bf16[4,1,128,512]{3,2,0,1:T(8,128)(2,1)}), bf16[4,2,128,512]{3,2,0,1:T(8,128)(2,1)}) %all-gather.14.cloned.1.call-update) | async-done | bytes 1048592 | tf_op jit(solution)/shard_map/all_gather | solution.py:397
  377.4 2.3 copy.42
  379.6 26.8 %reduce-scatter.6.cloned.1.call-done = bf16[512,768]{1,0:T(8,128)(2,1)} async-done(((bf16[512,1536]{1,0:T(8,128)(2,1)}), bf16[512,768]{1,0:T(8,128)(2,1)}) %reduce-scatter.6.cloned.1.call-update) | async-done | bytes 786448 | tf_op jit(solution)/shard_map/reduce_scatter | solution.py:412
  406.4 28.9 %reduce-scatter.8.cloned.1.call-done = bf16[768,512]{1,0:T(8,128)(2,1)} async-done(((bf16[1536,512]{1,0:T(8,128)(2,1)}), bf16[768,512]{1,0:T(8,128)(2,1)}) %reduce-scatter.8.cloned.1.call-update) | async-done | bytes 786448 | tf_op jit(solution)/shard_map/reduce_scatter | solution.py:413
  435.3 90.4 %all-reduce.6 = (f32[512,768]{1,0:T(8,128)}, f32[768,512]{1,0:T(8,128)}) all-reduce(bf16[512,768]{1,0:T(8,128)(2,1)} %reduce-scatter.6.cloned.1.call-done, bf16[768,512]{1,0:T(8,128)(2,1)} %reduce-scatter.8.cloned.1.call-done), channel_id=1, replica_groups=mesh['dp'=16,'expert'=2] {'dp'}, use_global_device_ids=true, to_apply=%region_9.10 | all-reduce | flops 786432 | bytes 4718592 | tf_op jit(solution)/shard_map/psum | solution.py:414
  525.7 3.2 reduce-scatter.12.cloned.1.call-done
  528.9 1.7 slice_bitcast_fusion
  (43 shorter events, 0.5 us)
Async XLA Ops:
  7.2 2.3 copy-start.6
  7.2 2.3 copy-start.7
  7.2 3.1 copy-start.9
  7.2 3.2 copy-start.8
  7.2 5.5 %copy-start.12 = (bf16[32,64]{1,0:T(8,128)(2,1)S(1)}, bf16[32,64]{1,0:T(8,128)(2,1)}, u32[]{:S(2)}) copy-start(bf16[32,64]{1,0:T(8,128)(2,1)} %param.15) | copy-start | bytes 12292
  7.2 5.5 %copy-start.11 = (bf16[32,64]{1,0:T(8,128)(2,1)S(1)}, bf16[32,64]{1,0:T(8,128)(2,1)}, u32[]{:S(2)}) copy-start(bf16[32,64]{1,0:T(8,128)(2,1)} %param.16) | copy-start | bytes 12292
  7.2 30.0 %all-gather.12.cloned.1.call-start = ((), (), s32[]{:S(2)}) async-start(), calls=%async_computation.9 | async-start | bytes 1572864 | tf_op jit(solution)/shard_map/all_gather | solution.py:313
  8.0 54.5 %all-gather.6.cloned.1.call-start = ((), (), s32[]{:S(2)}) async-start(), calls=%async_computation.6 | async-start | bytes 2359296 | tf_op jit(solution)/shard_map/all_gather | solution.py:311
  8.7 82.5 %all-gather.8.cloned.1.call-start = ((), (), s32[]{:S(2)}) async-start(), calls=%async_computation.7 | async-start | bytes 2359296 | tf_op jit(solution)/shard_map/all_gather | solution.py:312
  9.5 147.1 %all-gather.10.cloned.1.call-start = ((), (), s32[]{:S(2)}) async-start(), calls=%async_computation.8 | async-start | bytes 4325376 | tf_op jit(solution)/shard_map/all_gather | solution.py:308
  10.2 286.9 %reduce-scatter.10.cloned.1.call-start = ((), (), s32[]{:S(2)}) async-start(), calls=%async_computation.13 | async-start | bytes 6291456 | tf_op jit(solution)/shard_map/reduce_scatter | solution.py:408
  233.3 1.2 copy-start
  233.3 1.7 copy-start.3
  233.3 31.9 %copy-start.1 = (bf16[512,512]{1,0:T(8,128)(2,1)S(1)}, bf16[512,512]{1,0:T(8,128)(2,1)}, u32[]{:S(2)}) copy-start(bf16[512,512]{1,0:T(8,128)(2,1)} %get-tuple-element.26) | copy-start | bytes 1572868
  233.3 121.5 %reduce-scatter.14.cloned.1.call-start = ((), (), s32[]{:S(2)}) async-start(), calls=%async_computation.15 | async-start | bytes 278528 | tf_op jit(solution)/shard_map/reduce_scatter | solution.py:405
  265.2 2.7 copy-start.5
  265.2 2.7 copy-start.10
  267.8 109.5 %all-gather.14.cloned.1.call-start = ((), (), s32[]{:S(2)}) async-start(), calls=%async_computation.10 | async-start | bytes 1572864 | tf_op jit(solution)/shard_map/all_gather | solution.py:397
  267.9 1.3 copy-start.2
  270.4 136.0 %reduce-scatter.6.cloned.1.call-start = ((), (), s32[]{:S(2)}) async-start(), calls=%async_computation.11 | async-start | bytes 2359296 | tf_op jit(solution)/shard_map/reduce_scatter | solution.py:412
  271.1 164.2 %reduce-scatter.8.cloned.1.call-start = ((), (), s32[]{:S(2)}) async-start(), calls=%async_computation.12 | async-start | bytes 2359296 | tf_op jit(solution)/shard_map/reduce_scatter | solution.py:413
  271.9 257.0 %reduce-scatter.12.cloned.1.call-start = ((), (), s32[]{:S(2)}) async-start(), calls=%async_computation.14 | async-start | bytes 4456448 | tf_op jit(solution)/shard_map/reduce_scatter | solution.py:411
  301.1 1.0 copy-start.4
  301.2 5.8 %copy-start.13 = (f32[1,512]{1,0:T(1,128)S(1)}, f32[1,512]{1,0:T(1,128)}, u32[]{:S(2)}) copy-start(f32[1,512]{1,0:T(1,128)} %get-tuple-element.30) | copy-start | bytes 6148
  303.2 45.2 %all-to-all-start = ((bf16[4,1,128,512]{2,0,1,3:T(4,128)(2,1)}), bf16[4,1,128,512]{2,0,1,3:T(4,128)(2,1)S(1)}, u32[]{:S(2)}, u32[]{:S(2)}) async-start(bf16[4,1,128,512]{2,0,1,3:T(4,128)(2,1)} %copy.39), calls=%async_computation | async-start | bytes 1048576 | tf_op jit(solution)/shard_map/all_to_all | solution.py:401
Sparse Core Ops, SparseCore 0:
  9.6 23.9 all-gather.11
  35.2 27.2 all-gather.5
  64.0 27.1 all-gather.7
  94.5 62.0 all-gather.9
  233.5 63.5 reduce-scatter.9
  300.9 53.9 reduce-scatter.13
  357.0 20.3 all-gather.13
  380.3 26.0 reduce-scatter.5
  409.2 26.0 reduce-scatter.7
  439.5 89.3 reduce-scatter.11

commit v2 on v1

v2 whole, which is shorter than its diff:
```python
import functools

import jax
import jax.numpy as jnp
from jax import lax
from jax.experimental import pallas as pl
from jax.experimental.pallas import tpu as pltpu
from jax.sharding import PartitionSpec as P

f32 = jnp.float32
bf16 = jnp.bfloat16
eps = 1e-05
lowest = -1e30
rb = 128


def nn(left, right):
    return jnp.dot(left, right, preferred_element_type=f32)


def nt(left, right):
    return lax.dot_general(left, right, (((1,), (1,)), ((), ())), preferred_element_type=f32)


def tn(left, right):
    return lax.dot_general(left, right, (((0,), (0,)), ((), ())), preferred_element_type=f32)


def norm_rows(x):
    centred = x - jnp.mean(x, axis=-1, keepdims=True)
    inv = lax.rsqrt(jnp.mean(centred * centred, axis=-1, keepdims=True) + eps)
    return centred * inv, inv


def norm_back(u, normed, inv, gain):
    w = u * gain
    return inv * (
        w
        - jnp.mean(w, axis=-1, keepdims=True)
        - normed * jnp.mean(w * normed, axis=-1, keepdims=True)
    )


def lanes(shape):
    return lax.broadcasted_iota(jnp.int32, shape, len(shape) - 1)


MESH = pl.DeviceIdType.MESH

in_names = [
    "len_ref",
    "tok",
    "gain1",
    "wr",
    "gain2",
    "ids",
    "wkv_in",
    "wq_in",
    "wo_in",
    "w_in",
    "go_in",
]
out_names = [
    "out",
    "gt",
    "gwq",
    "gwo",
    "gwh",
    "gwT",
    "gkv",
    "small",
]


def scratch(rows, width, nb, top, fq, ff, nz, shard):
    vm = pltpu.VMEM
    own = rows // 2
    half = fq // 2
    total = 128 * nb * (nb + 1)
    ring = (nz, 2, 2)
    ch = ff // 4
    woc = half // (4 * nz)
    return {
        "wkvg": vm(ring + (shard, 128), bf16),
        "W": vm((2, 2) + ring + (shard, 2 * ch), bf16),
        "WQ": vm((2, width, half), bf16),
        "WO": vm((2, half, width), bf16),
        "GO": vm((2, nb, rb, width // 2), bf16),
        "h1": vm((2 * nb, rb, width), bf16),
        "h1T": vm((width, own), bf16),
        "KK": vm((rows, 128), bf16),
        "VV": vm((rows, 128), bf16),
        "KKT": vm((128, rows), bf16),
        "VVT": vm((128, rows), bf16),
        "idl": vm((nb, top, rb, 128), jnp.int32),
        "gateb": vm((nb, top, rb, 128), f32),
        "dense": vm((own, 128), f32),
        "Qs": vm((nb, top, rb, 128), bf16),
        "PT": vm((total, top * rb), bf16),
        "O": vm((nb, top, rb, 128), f32),
        "wide": vm((rb, fq), f32),
        "gated": vm((own, fq), bf16),
        "n2": vm((own, width), f32),
        "r2": vm((own, 1), f32),
        "res": vm((own, width), f32),
        "h2": vm((own, width), bf16),
        "h2T": vm((width, own), bf16),
        "gfT": vm((width, own), bf16),
        "gf": vm((own, width), bf16),
        "gh2": vm((own, width), f32),
        "acc": vm((own, width), f32),
        "gatt": vm((own, width), bf16),
        "dOs": vm((nb, top, rb, 128), bf16),
        "glog": vm((own, 128), bf16),
        "DS": vm((rows, top * rb), bf16),
        "gK": vm((rows, 128), f32),
        "gV": vm((rows, 128), f32),
        "dQ": vm((top, rb, 128), f32),
        "gain_rows": vm((2, width), f32),
        "outx": vm((nb, rb, width // 2), bf16),
        "kvs": vm((nb, 2, rb, 128), bf16),
        "kvr": vm((nb, rb, 128), bf16),
        "F": vm((2, 2) + ring + (shard, 2 * ch), bf16),
        "FC": vm((2, 2, nz, 2, shard, 2 * ch), bf16),
        "FY0": vm((nz, 2, shard, 2 * ch), bf16),
        "FX0": vm((nz, shard, 2 * ch), bf16),
        "FZ0": vm((nz - 1, shard, 2 * ch), bf16),
        "FX1": vm((2, nz, shard, 2 * ch), bf16),
        "FZ1": vm((nz - 1, 2, shard, 2 * ch), bf16),
        "FY1": vm((shard, 2 * ch), bf16),
        "Q": vm((2,) + ring + (shard, half), bf16),
        "QC": vm((2, nz, 2, shard, half), bf16),
        "QX": vm((2, nz, shard, half), bf16),
        "QY": vm((nz, shard, half), bf16),
        "QZ": vm((nz - 1, shard, half), bf16),
        "QA": vm(ring + (shard, half), bf16),
        "P": vm((2,) + ring + (woc, width), bf16),
        "PC": vm((2, nz, 2, woc, width), bf16),
        "PX": vm((2, nz, woc, width), bf16),
        "PY": vm((nz, woc, width), bf16),
        "PZ": vm((nz - 1, woc, width), bf16),
        "PA": vm(ring + (woc, width), bf16),
        "K": vm(ring + (shard, 128), f32),
        "KC": vm((nz, 2, shard, 128), f32),
        "KX": vm((nz, shard, 128), f32),
        "KZ": vm((nz - 1, shard, 128), f32),
        "KY": vm((2, shard, 128), f32),
        "S": vm((4, 32, width), f32),
        "SR": vm((3, 32, width), f32),
        "SZ": vm((nz, 32, width), f32),
        "send": pltpu.SemaphoreType.DMA((96,)),
        "recv": pltpu.SemaphoreType.DMA((96,)),
        "local": pltpu.SemaphoreType.DMA((8,)),
    }


class Refs:
    pass


def kernel(names, outer, *refs):
    r = Refs()
    for name, ref in zip(names, refs):
        setattr(r, name, ref)
    nb = r.tok.shape[0] // 2
    width = r.tok.shape[2]
    top = r.ids.shape[2]
    fq = r.gated.shape[1]
    half = fq // 2
    groups = fq // 128
    r.gq = r.gated
    r.actS = r.DS.at[0 : nb * rb, 0 : r.W.shape[6] // 2]
    r.giS = r.DS.at[0 : nb * rb, r.W.shape[6] // 2 : r.W.shape[6]]
    nz = r.W.shape[2]
    ch = r.W.shape[6] // 2
    shard = r.W.shape[5]
    d = lax.axis_index("dp")
    y = lax.axis_index("expert")
    n, m = d // outer, d % outer
    z, x, c = n // 4, (n // 2) % 2, n % 2
    length = r.len_ref[0]

    def device(z, x, c, y):
        return ((z * 4 + x * 2 + c) * outer + m, y)

    over_c = device(z, x, 1 - c, y)
    over_x = device(z, 1 - x, c, y)
    over_y = device(z, x, c, 1 - y)
    zs = [(z + k) % nz for k in range(1, nz)]
    over_z = [device(k, x, c, y) for k in zs]
    used = [0]
    sent = []

    def send(source, target, to):
        k = used[0]
        used[0] += 1
        copy = pltpu.make_async_remote_copy(
            src_ref=source, dst_ref=target, send_sem=r.send.at[k], recv_sem=r.recv.at[k],
            device_id=to, device_id_type=MESH,
        )
        copy.start()
        sent.append(copy)
        return copy

    def here(k, source, target):
        copy = pltpu.make_async_copy(source, target, r.local.at[k])
        copy.start()
        return copy

    def got(*copies):
        for copy in copies:
            copy.wait_recv()

    def own(i):
        return 2 * i + y

    def cut(i, size):
        return pl.ds(pl.multiple_of(i * size, size), size)

    def valid_rows(i):
        return (rb * own(i) + lax.broadcasted_iota(jnp.int32, (rb, 1), 0) < length).astype(f32)

    l_w = here(0, r.w_in, r.W.at[:, y, z, x, c])
    l_q = here(1, r.wq_in, r.WQ.at[y])
    l_o = here(2, r.wo_in, r.WO.at[y])
    l_g = here(3, r.go_in.at[:, y], r.GO.at[y])
    l_kv = here(4, r.wkv_in, r.wkvg.at[z, x, c])
    barrier = pltpu.get_barrier_semaphore()
    peers = [over_c, over_x, over_y] + over_z
    for peer in peers:
        pl.semaphore_signal(barrier, inc=1, device_id=peer, device_id_type=MESH)
    pl.semaphore_wait(barrier, len(peers))
    kv_c = send(r.wkv_in, r.wkvg.at[z, x, c], over_c)
    w_y = send(r.w_in, r.W.at[:, y, z, x, c], over_y)
    qrows = cut(c, width // 2)
    q_y = send(r.wq_in.at[qrows, :], r.WQ.at[y, qrows, :], over_y)
    l_w.wait()
    l_kv.wait()

    @pl.loop(0, 2 * nb)
    def _(b):
        normed, _ = norm_rows(r.tok[b].astype(f32))
        r.h1[b] = (normed * r.gain1[...]).astype(bf16)

    got(kv_c)
    kv_x = send(r.wkvg.at[z, x], r.wkvg.at[z, x], over_x)
    got(w_y)

    def w_over_z(j):
        return [
            send(r.W.at[j, :, z, x, c], r.W.at[j, :, z, x, c], to) for to in over_z
        ]

    w0_z = w_over_z(0)

    lane = lanes((rb, 128))
    upper = (lane >= 64).astype(jnp.int32)

    def gates(i):
        h = r.h1[own(i)]
        at = cut(i, rb)
        r.h1T[:, at] = h.astype(f32).T.astype(bf16)
        logits = nn(h, r.wr[...])
        ids = r.ids[own(i)]
        spread = [jnp.broadcast_to(ids[:, k : k + 1], (rb, 128)) for k in range(top)]
        chosen = lane == spread[0]
        for k in range(1, top):
            chosen = chosen | (lane == spread[k])
        most = jnp.max(jnp.where(chosen, logits, lowest), axis=-1, keepdims=True)
        e = jnp.where(chosen, jnp.exp(jnp.where(chosen, logits - most, 0.0)), 0.0)
        g = e / jnp.sum(e, axis=-1, keepdims=True)
        r.dense[at, :] = g
        for k in range(top):
            gk = jnp.sum(jnp.where(lane == spread[k], g, 0.0), axis=-1, keepdims=True)
            r.gateb[i, k] = jnp.broadcast_to(gk, (rb, 128))
            r.idl[i, k] = spread[k] - upper

    pl.loop(0, nb // 2)(gates)
    got(kv_x)
    kv_z = [send(r.wkvg.at[z], r.wkvg.at[z], to) for to in over_z]
    pl.loop(nb // 2, nb)(gates)

    got(*kv_z)

    @pl.loop(0, 2 * nb)
    def _(b):
        kv = nn(r.h1[b], r.wkvg[...].reshape(width, 128))
        at = cut(b, rb)
        swapped = pltpu.roll(kv, 64, 1)
        k2 = jnp.where(lane < 64, kv, swapped)
        v2 = jnp.where(lane < 64, swapped, kv)
        r.KK[at, :] = k2.astype(bf16)
        r.VV[at, :] = v2.astype(bf16)
        r.KKT[:, at] = k2.T.astype(bf16)
        r.VVT[:, at] = v2.T.astype(bf16)

    got(q_y)
    q_c = send(r.WQ.at[1 - y, qrows, :], r.WQ.at[1 - y, qrows, :], over_c)
    orows = cut(c, half // 2)
    o_y = send(r.wo_in.at[orows, :], r.WO.at[y, orows, :], over_y)
    l_q.wait()
    got(q_c)

    @pl.loop(0, nb)
    def _(i):
        h = r.h1[own(i)]
        for e in range(2):
            r.wide[:, e * half : (e + 1) * half] = 0.125 * nn(h, r.WQ[e])

        @pl.loop(0, rb // 16)
        def _(t):
            at = cut(t, 16)
            parts = [r.wide[at, pl.ds(128 * g, 128)] for g in range(groups)]
            for k in range(top):
                mine = r.idl[i, k, at, :]
                val = jnp.zeros((16, 128), f32)
                for g in range(groups):
                    val = jnp.where(mine == 2 * g, parts[g], val)
                r.Qs[i, k, at, :] = val.astype(bf16)

    diag = lax.broadcasted_iota(jnp.int32, (256, 256), 0) <= rb * y + lanes((256, 256)) % 128

    def attend(i):
        nk = 256 * i
        start = 128 * i * (i + 1)

        @pl.loop(0, top // 2)
        def _(p):
            q = r.Qs[i, pl.ds(2 * p, 2)].reshape(256, 128)
            cols = cut(p, 256)
            s1 = nt(r.KK[nk : nk + 256, :], q)
            s1 = jnp.where(diag, s1, lowest)
            most = jnp.max(s1, axis=0, keepdims=True)
            if nk:
                s0 = nt(r.KK[0:nk, :], q)
                most = jnp.maximum(most, jnp.max(s0, axis=0, keepdims=True))
                p0 = jnp.exp(s0 - most)
            p1 = jnp.exp(s1 - most)
            tot = jnp.sum(p1, axis=0, keepdims=True)
            if nk:
                tot = tot + jnp.sum(p0, axis=0, keepdims=True)
            inv = 1.0 / tot
            p1 = (p1 * inv).astype(bf16)
            r.PT[start + nk : start + nk + 256, cols] = p1
            o = nn(r.VVT[:, nk : nk + 256], p1)
            if nk:
                p0 = (p0 * inv).astype(bf16)
                r.PT[start : start + nk, cols] = p0
                o = o + nn(r.VVT[:, 0:nk], p0)
            r.O[i, pl.ds(2 * p, 2)] = o.T.reshape(2, rb, 128)

    attend(0)
    attend(1)
    got(*w0_z)
    w0_x = send(r.W.at[0, :, :, x, c], r.W.at[0, :, :, x, c], over_x)
    w1_z = w_over_z(1)
    attend(2)
    g_y = send(r.go_in.at[:, 1 - y], r.GO.at[y], over_y)
    attend(3)
    for i in range(4, nb):
        attend(i)
    got(w0_x)
    w0_c = send(r.W.at[0, :, :, :, c], r.W.at[0, :, :, :, c], over_c)
    got(o_y)
    o_c = send(r.WO.at[1 - y, orows, :], r.WO.at[1 - y, orows, :], over_c)
    got(*w1_z)
    w1_x = send(r.W.at[1, :, :, x, c], r.W.at[1, :, :, x, c], over_x)
    l_o.wait()
    l_g.wait()
    got(o_c)
    got(g_y)

    def project(i):
        at = cut(i, rb)

        @pl.loop(0, rb // 16)
        def _(t):
            at = cut(t, 16)
            atr = pl.ds(pl.multiple_of(i * rb + t * 16, 16), 16)
            mine = [r.idl[i, k, at, :] for k in range(top)]
            vals = [r.gateb[i, k, at, :] * r.O[i, k, at, :] for k in range(top)]
            for g in range(groups):
                val = jnp.zeros((16, 128), f32)
                for k in range(top):
                    val = jnp.where(mine[k] == 2 * g, vals[k], val)
                r.gated[atr, pl.ds(128 * g, 128)] = val.astype(bf16)

        valid = valid_rows(i)
        att = nn(r.gated[at, 0:half], r.WO[0]) + nn(r.gated[at, half:fq], r.WO[1])
        row = r.tok[own(i)].astype(f32) + valid * att
        r.res[at, :] = row
        normed, inv = norm_rows(row)
        r.n2[at, :] = normed
        r.r2[at, :] = inv
        h = normed * r.gain2[...]
        r.h2[at, :] = h.astype(bf16)
        r.h2T[:, at] = h.T.astype(bf16)
        for s in range(2):
            side = pl.ds(s * (width // 2), width // 2)
            g = valid * r.GO[s, i].astype(f32)
            r.gf[at, side] = g.astype(bf16)
            r.gfT[side, at] = g.T.astype(bf16)

    pl.loop(0, nb)(project)

    c0 = 0.7978845608028654
    c1 = 0.044715

    def feed(j, e):
        first = j == 0 and e == 0

        @pl.loop(0, nb)
        def _(i):
            at = cut(i, rb)
            w1 = r.W[j, e, :, :, :, :, 0:ch].reshape(width, ch)
            w2 = r.W[j, e, :, :, :, :, ch : 2 * ch].reshape(width, ch)
            v = nn(r.h2[at, :], w1)
            ga = nn(r.gf[at, :], w2)
            vv = v * v
            t = jnp.tanh(v * (c0 + (c0 * c1) * vv))
            hp = 0.5 + 0.5 * t
            act = (v * hp).astype(bf16)
            slope = hp + (0.5 * v) * (1.0 - t * t) * (c0 + (3 * c0 * c1) * vv)
            gi = (slope * ga).astype(bf16)
            r.actS[at, :] = act
            r.giS[at, :] = gi
            a = nt(act, w2)
            b = nt(gi, w1)
            if not first:
                a = a + r.acc[at, :]
                b = b + r.gh2[at, :]
            r.acc[at, :] = a
            r.gh2[at, :] = b

        shape = (nz, 2, 2, shard, ch)
        r.F[j, e, :, :, :, :, 0:ch] = nn(r.h2T[...], r.giS[...]).astype(bf16).reshape(shape)
        r.F[j, e, :, :, :, :, ch : 2 * ch] = (
            nn(r.gfT[...], r.actS[...]).astype(bf16).reshape(shape)
        )
        return send(r.F.at[j, e, :, :, 1 - c], r.FC.at[j, e], over_c)

    def f_add_c(j, e):
        @pl.loop(0, 2 * nz)
        def _(t):
            a, b = t // 2, t % 2
            r.F[j, e, a, b, c] = r.F[j, e, a, b, c] + r.FC[j, e, a, b]

    got(w0_c)
    f00 = feed(0, 0)
    got(w1_x)
    w1_c = send(r.W.at[1, :, :, :, c], r.W.at[1, :, :, :, c], over_c)
    f01 = feed(0, 1)
    got(f00)
    f_add_c(0, 0)
    got(f01)
    f_add_c(0, 1)
    f0_y = send(r.F.at[0, 1 - y, :, :, c], r.FY0, over_y)
    got(w1_c)
    f10 = feed(1, 0)
    f11 = feed(1, 1)
    got(f10)
    f_add_c(1, 0)
    got(f11)
    f_add_c(1, 1)
    f1_x = send(r.F.at[1, :, :, 1 - x, c], r.FX1, over_x)

    r.gain_rows[...] = jnp.zeros_like(r.gain_rows)

    def turn(i):
        at = cut(i, rb)
        valid = valid_rows(i)
        outs = (r.res[at, :] + valid * r.acc[at, :]).astype(bf16)
        mine, other = outs[:, : width // 2], outs[:, width // 2 :]
        low = y == 0
        r.out[i, y] = jnp.where(low, mine, other)
        r.outx[i] = jnp.where(low, other, mine)
        u, normed = r.gh2[at, :], r.n2[at, :]
        r.gain_rows[1:2, :] += jnp.sum(u * normed, axis=0, keepdims=True)
        back = norm_back(u, normed, r.r2[at, :], r.gain2[...])
        go = jnp.concatenate((r.GO[0, i], r.GO[1, i]), axis=1).astype(f32)
        gr = go + back
        r.res[at, :] = gr
        ga = (valid * gr).astype(bf16)
        r.gatt[at, :] = ga
        for e in range(2):
            r.wide[:, e * half : (e + 1) * half] = nt(ga, r.WO[e])

        @pl.loop(0, rb // 16)
        def _(t):
            at = cut(t, 16)
            atr = pl.ds(pl.multiple_of(i * rb + t * 16, 16), 16)
            parts = [r.wide[at, pl.ds(128 * g, 128)] for g in range(groups)]
            ln = lanes((16, 128))
            hf = (ln >= 64).astype(jnp.int32)
            gd = jnp.zeros((16, 128), f32)
            for k in range(top):
                mine = r.idl[i, k, at, :]
                val = jnp.zeros((16, 128), f32)
                for g in range(groups):
                    val = jnp.where(mine == 2 * g, parts[g], val)
                dot = jnp.sum(val * r.O[i, k, at, :], axis=-1, keepdims=True)
                gd = jnp.where(mine + hf == ln, dot, gd)
                r.dOs[i, k, at, :] = (r.gateb[i, k, at, :] * val).astype(bf16)
            dn = r.dense[atr, :]
            gs = dn * (gd - jnp.sum(dn * gd, axis=-1, keepdims=True))
            r.glog[atr, :] = gs.astype(bf16)

    pl.loop(0, nb)(turn)
    out_y = send(r.outx, r.out.at[:, y], over_y)

    woc = r.P.shape[4]
    for e in range(2):
        r.P[e] = (
            tn(r.gated[:, e * half : (e + 1) * half], r.gatt[...])
            .astype(bf16)
            .reshape(nz, 2, 2, woc, width)
        )
    p_c = send(r.P.at[:, :, :, 1 - c], r.PC, over_c)

    r.gK[...] = jnp.zeros_like(r.gK)
    r.gV[...] = jnp.zeros_like(r.gV)

    def back(i):
        nk = 256 * (i + 1)
        start = 128 * i * (i + 1)

        @pl.loop(0, top // 2)
        def _(p):
            do = r.dOs[i, pl.ds(2 * p, 2)].reshape(256, 128)
            cols = cut(p, 256)
            dp = nt(r.VV[0:nk, :], do)
            pr = r.PT[start : start + nk, cols].astype(f32)
            s = jnp.sum(pr * dp, axis=0, keepdims=True)
            ds = (pr * (dp - s)).astype(bf16)
            r.DS[0:nk, cols] = ds
            dq = nn(r.KKT[:, 0:nk], ds)
            r.dQ[pl.ds(2 * p, 2)] = dq.T.reshape(2, rb, 128)

        r.gK[0:nk, :] += nn(r.DS[0:nk, :], r.Qs[i].reshape(top * rb, 128))
        r.gV[0:nk, :] += nn(r.PT[start : start + nk, :], r.dOs[i].reshape(top * rb, 128))

        @pl.loop(0, rb // 16)
        def _(t):
            at = cut(t, 16)
            atr = pl.ds(pl.multiple_of(i * rb + t * 16, 16), 16)
            mine = [r.idl[i, k, at, :] for k in range(top)]
            vals = [r.dQ[k, at, :] for k in range(top)]
            for g in range(groups):
                val = jnp.zeros((16, 128), f32)
                for k in range(top):
                    val = jnp.where(mine[k] == 2 * g, vals[k], val)
                r.gq[atr, pl.ds(128 * g, 128)] = val.astype(bf16) * 0.125

    back(0)
    got(p_c)

    @pl.loop(0, 4 * nz)
    def _(t):
        e, a, b = t // (2 * nz), (t // 2) % nz, t % 2
        r.P[e, a, b, c] = r.P[e, a, b, c] + r.PC[e, a, b]

    p_x = send(r.P.at[:, :, 1 - x, c], r.PX, over_x)
    back(1)
    got(f0_y)

    @pl.loop(0, 2 * nz)
    def _(t):
        a, b = t // 2, t % 2
        r.F[0, y, a, b, c] = r.F[0, y, a, b, c] + r.FY0[a, b]

    f0_x = send(r.F.at[0, y, :, 1 - x, c], r.FX0, over_x)
    back(2)
    got(f1_x)

    @pl.loop(0, 2 * nz)
    def _(t):
        e, a = t // nz, t % nz
        r.F[1, e, a, x, c] = r.F[1, e, a, x, c] + r.FX1[e, a]

    f1_z = [send(r.F.at[1, :, k, x, c], r.FZ1.at[i], to) for i, (k, to) in enumerate(zip(zs, over_z))]
    got(p_x)

    @pl.loop(0, 2 * nz)
    def _(t):
        e, a = t // nz, t % nz
        r.P[e, a, x, c] = r.P[e, a, x, c] + r.PX[e, a]

    p_y = send(r.P.at[1 - y, :, x, c], r.PY, over_y)
    back(3)
    for i in range(4, nb):
        back(i)

    @pl.loop(0, nb)
    def _(i):
        for s in range(2):
            at = pl.ds(pl.multiple_of((2 * i + s) * rb, rb), rb)
            a, b = r.gK[at, :], r.gV[at, :]
            a = a + pltpu.roll(a, 64, 1)
            b = b + pltpu.roll(b, 64, 1)
            r.kvs[i, s] = jnp.where(lane < 64, a, b).astype(bf16)

    kv_y = send(r.kvs.at[:, 1 - y], r.kvr, over_y)
    for e in range(2):
        r.Q[e] = (
            nn(r.h1T[...], r.gq[:, e * half : (e + 1) * half])
            .astype(bf16)
            .reshape(nz, 2, 2, shard, half)
        )
    q_c2 = send(r.Q.at[:, :, :, 1 - c], r.QC, over_c)
    got(f0_x)

    @pl.loop(0, nz)
    def _(a):
        r.F[0, y, a, x, c] = r.F[0, y, a, x, c] + r.FX0[a]

    f0_z = [send(r.F.at[0, y, k, x, c], r.FZ0.at[i], to) for i, (k, to) in enumerate(zip(zs, over_z))]
    got(q_c2)

    @pl.loop(0, 4 * nz)
    def _(t):
        e, a, b = t // (2 * nz), (t // 2) % nz, t % 2
        r.Q[e, a, b, c] = r.Q[e, a, b, c] + r.QC[e, a, b]

    q_x = send(r.Q.at[:, :, 1 - x, c], r.QX, over_x)

    got(kv_y)

    def finish(i):
        at = cut(i, rb)
        low = (r.kvs[i, y].astype(f32) + r.kvr[i].astype(f32)).astype(bf16)
        r.kvr[i] = low
        g = nt(low, r.wkvg[...].reshape(width, 128)) + nt(r.glog[at, :], r.wr[...])
        for e in range(2):
            g = g + nt(r.gq[at, e * half : (e + 1) * half], r.WQ[e])
        normed, inv = norm_rows(r.tok[own(i)].astype(f32))
        r.gain_rows[0:1, :] += jnp.sum(g * normed, axis=0, keepdims=True)
        r.gt[i, y] = (r.res[at, :] + norm_back(g, normed, inv, r.gain1[...])).astype(bf16)

    pl.loop(0, nb)(finish)
    gt_y = send(r.gt.at[:, y], r.gt.at[:, y], over_y)

    r.K[...] = nn(r.h1T[...], r.kvr[...].reshape(nb * rb, 128)).reshape(nz, 2, 2, shard, 128)
    k_c = send(r.K.at[:, :, 1 - c], r.KC, over_c)
    routed = jnp.zeros((128, width), f32)
    for i in range(nb):
        routed = routed + tn(r.glog[i * rb : (i + 1) * rb, :], r.h1[own(i)])
    r.S[0] = routed[0:32]
    r.S[0, 30:32, :] = r.gain_rows[...]
    s_c = send(r.S.at[0], r.SR.at[0], over_c)

    got(k_c)

    @pl.loop(0, 2 * nz)
    def _(t):
        a, b = t // 2, t % 2
        r.K[a, b, c] = r.K[a, b, c] + r.KC[a, b]

    k_x = send(r.K.at[:, 1 - x, c], r.KX, over_x)
    got(s_c)
    r.S[1] = r.S[0] + r.SR[0]
    s_x = send(r.S.at[1], r.SR.at[1], over_x)

    got(p_y)

    @pl.loop(0, nz)
    def _(a):
        r.P[y, a, x, c] = r.P[y, a, x, c] + r.PY[a]

    p_z = [send(r.P.at[y, k, x, c], r.PZ.at[i], to) for i, (k, to) in enumerate(zip(zs, over_z))]
    got(*f1_z)
    for e in range(2):
        v = r.F[1, e, z, x, c].astype(f32)
        for k in range(nz - 1):
            v = v + r.FZ1[k, e].astype(f32)
        r.F[1, e, z, x, c] = v.astype(bf16)
    f1_y = send(r.F.at[1, 1 - y, z, x, c], r.FY1, over_y)
    got(k_x)

    @pl.loop(0, nz)
    def _(a):
        r.K[a, x, c] = r.K[a, x, c] + r.KX[a]

    k_z = [send(r.K.at[k, x, c], r.KZ.at[i], to) for i, (k, to) in enumerate(zip(zs, over_z))]
    got(s_x)
    r.S[2] = r.S[1] + r.SR[1]
    s_y = send(r.S.at[2], r.SR.at[2], over_y)
    got(*f0_z)
    v = r.F[0, y, z, x, c].astype(f32)
    for k in range(nz - 1):
        v = v + r.FZ0[k].astype(f32)
    r.gwh[:, 0:ch] = v[:, 0:ch]
    r.gwT[:, 0:ch] = v[:, ch : 2 * ch]

    got(q_x)

    @pl.loop(0, 2 * nz)
    def _(t):
        e, a = t // nz, t % nz
        r.Q[e, a, x, c] = r.Q[e, a, x, c] + r.QX[e, a]

    q_y2 = send(r.Q.at[1 - y, :, x, c], r.QY, over_y)
    got(*p_z)
    v = r.P[y, z, x, c].astype(f32)
    for k in range(nz - 1):
        v = v + r.PZ[k].astype(f32)
    r.PA[z, x, c] = v.astype(bf16)
    pa_z = [send(r.PA.at[z, x, c], r.PA.at[z, x, c], to) for to in over_z]
    got(*k_z)
    v = r.K[z, x, c]
    for k in range(nz - 1):
        v = v + r.KZ[k]
    r.KY[0] = v
    k_y = send(r.KY.at[0], r.KY.at[1], over_y)
    got(s_y)
    r.S[3] = r.S[2] + r.SR[2]
    r.SZ[z] = r.S[3]
    s_z = [send(r.S.at[3], r.SZ.at[z], to) for to in over_z]
    got(f1_y)
    v = r.F[1, y, z, x, c].astype(f32) + r.FY1[...].astype(f32)
    r.gwh[:, ch : 2 * ch] = v[:, 0:ch]
    r.gwT[:, ch : 2 * ch] = v[:, ch : 2 * ch]
    got(*pa_z)
    pa_x = send(r.PA.at[:, x, c], r.PA.at[:, x, c], over_x)
    got(q_y2)

    @pl.loop(0, nz)
    def _(a):
        r.Q[y, a, x, c] = r.Q[y, a, x, c] + r.QY[a]

    q_z = [send(r.Q.at[y, k, x, c], r.QZ.at[i], to) for i, (k, to) in enumerate(zip(zs, over_z))]
    got(k_y)
    r.gkv[...] = r.KY[0] + r.KY[1]
    got(*s_z)
    v = r.SZ[0]
    for k in range(1, nz):
        v = v + r.SZ[k]
    r.small[...] = v
    got(*q_z)
    v = r.Q[y, z, x, c].astype(f32)
    for k in range(nz - 1):
        v = v + r.QZ[k].astype(f32)
    r.QA[z, x, c] = v.astype(bf16)
    qa_z = [send(r.QA.at[z, x, c], r.QA.at[z, x, c], to) for to in over_z]
    got(pa_x)
    pa_c = send(r.PA.at[:, :, c], r.PA.at[:, :, c], over_c)
    got(*qa_z)
    qa_x = send(r.QA.at[:, x, c], r.QA.at[:, x, c], over_x)
    got(pa_c)

    @pl.loop(0, 4 * nz)
    def _(t):
        at = cut(t, woc)
        r.gwo[at, :] = r.PA[t // 4, (t // 2) % 2, t % 2].astype(f32)

    got(qa_x)
    qa_c = send(r.QA.at[:, :, c], r.QA.at[:, :, c], over_c)
    got(qa_c)

    @pl.loop(0, 4 * nz)
    def _(t):
        at = cut(t, shard)
        r.gwq[at, :] = r.QA[t // 4, (t // 2) % 2, t % 2].astype(f32)

    got(out_y, gt_y)
    for copy in sent:
        copy.wait_send()


def shards(
    tokens, gain_attn, w_key, w_value, w_router, w_query, w_out, gain_ffn,
    w_hidden, w_output, expert_ids, lengths, grad_out,
):
    rows, width = tokens.shape
    dp = lax.axis_size("dp")
    inner = min(dp, 16)
    outer = dp // inner
    nz = inner // 4
    nb = rows // rb // 2
    top = expert_ids.shape[1]
    n_experts = w_router.shape[1]
    hd = w_key.shape[1]
    half = w_query.shape[1]
    ffh = w_hidden.shape[1]
    ch = ffh // 2
    near = [[g * outer + k for k in range(outer)] for g in range(inner)]
    wkv = jnp.concatenate((w_key, w_value), 1)
    wt = w_output.T
    w_in = jnp.stack(
        [
            jnp.concatenate((w_hidden[:, :ch], wt[:, :ch]), 1),
            jnp.concatenate((w_hidden[:, ch:], wt[:, ch:]), 1),
        ]
    )
    if outer > 1:
        wkv = lax.all_gather(wkv, "dp", axis=0, tiled=True, axis_index_groups=near)
        w_in = lax.all_gather(w_in, "dp", axis=1, tiled=True, axis_index_groups=near)
    wr = jnp.pad(w_router, ((0, 0), (0, 128 - n_experts)))
    shard = width // inner
    sds = jax.ShapeDtypeStruct
    spec = scratch(rows, width, nb, top, 2 * half, 2 * ffh, nz, shard)
    names = in_names + out_names + list(spec)
    vmem = pl.BlockSpec(memory_space=pltpu.VMEM)
    anyw = pl.BlockSpec(memory_space=pl.ANY)
    out, gt, gwq, gwo, gwh, gwT, gkv, small = pl.pallas_call(
        functools.partial(kernel, names, outer),
        out_shape=(
            sds((nb, 2, rb, width // 2), bf16),
            sds((nb, 2, rb, width), bf16),
            sds((width, half), f32),
            sds((half, width), f32),
            sds((shard, ffh), f32),
            sds((shard, ffh), f32),
            sds((shard, 128), f32),
            sds((32, width), f32),
        ),
        in_specs=[pl.BlockSpec(memory_space=pltpu.SMEM)] + [vmem] * 5 + [anyw] * 5,
        out_specs=[vmem] * 8,
        scratch_shapes=list(spec.values()),
        compiler_params=pltpu.CompilerParams(
            collective_id=0, has_side_effects=True, vmem_limit_bytes=63 * 2**20
        ),
    )(
        lengths, tokens.reshape(2 * nb, rb, width), gain_attn[None], wr, gain_ffn[None],
        expert_ids.reshape(2 * nb, rb, top), wkv, w_query, w_out, w_in,
        grad_out.reshape(nb, 2, rb, width // 2),
    )
    if outer > 1:
        gwq, gwo, small = lax.psum((gwq, gwo, small), "dp", axis_index_groups=near)
        gwh, gwT, gkv = (
            lax.psum_scatter(v, "dp", scatter_dimension=0, tiled=True, axis_index_groups=near)
            for v in (gwh, gwT, gkv)
        )
    return (
        out.reshape(rows, width // 2), gt.reshape(rows, width), gkv[:, :hd], gkv[:, hd:],
        small[:n_experts].T, gwq, gwo, gwh, gwT.T, small[30], small[31],
    )


def solution(mesh):
    placed = (
        P("dp", None), P(), P("dp", None), P("dp", None), P(), P(None, "expert"),
        P("expert", None), P(), P("dp", "expert"), P("expert", "dp"), P("dp", None),
        P("dp"), P("dp", "expert"),
    )
    return jax.shard_map(
        shards,
        mesh=mesh,
        in_specs=placed,
        out_specs=(
            P("dp", "expert"), P("dp", None), P("dp", None), P("dp", None), P(),
            P(None, "expert"), P("expert", None), P("dp", "expert"), P("expert", "dp"),
            P(), P(),
        ),
        check_vma=False,
    )
```

time: 538 us -> 179 us (0.33)
  waiting for transfers between devices: 223 us -> 0 us
  blocking collectives: 194 us -> 0 us
  Pallas kernels: 76.7 us -> 158 us
  between operations: 15.1 us -> 1.32 us
    psum x4 -> x0, blocking collectives: 171 us -> none  [the longest x1 90.4 us: shards(): lax.psum((gwq_own.astype(f32), gwo_own.astype(f32)), 'dp')]
    all_gather x5 -> x0, waiting for transfers between devices: 131 us -> none  [the longest x1 65.4 us: shards(): lax.all_gather(jnp.concatenate((w_hidden, w_output.T), 1), ('expert', 'dp...]
    reduce_scatter x5 -> x0, waiting for transfers between devices: 89.3 us -> none  [the longest x1 28.9 us: shards(): gwo_own = lax.psum_scatter(gwo, 'expert', scatter_dimension=0, tiled=True)]
    pallas_call x1, Pallas kernels: 76.7 us -> 158 us  [shards(): pl.pallas_call(functools.partial(kernel, names, outer), out_shape=(sds((n...]
    all_gather x1 -> x0, blocking collectives: 23.4 us -> none  [shards(): lax.all_gather(jnp.concatenate((w_key, w_value), 1), 'dp', axis=0, tiled=...]
    unnamed x30 -> x18, local copies, waits for them, and re-layouts: 3.92 us -> 10 us
  transfers between devices with their start and end apart: 11 -> 0, of which waited for: 9 -> 0; matrix products, arithmetic and copies ran while one was open for 4% -> 0% of each run, Pallas kernels for 0% -> 0%
where the time goes in v2:
time: 179 us; the launch traced here: 178 us
  Pallas kernels  158 us (88%)
  local copies, waits for them, and re-layouts  16.6 us (9%)
  other arithmetic  2.07 us (1%)
    pallas_call x1, Pallas kernels, shards(): pl.pallas_call(functools.partial(kernel, names, outer), out_shape=(sds((n...  158 us
    unnamed x18, local copies, waits for them, and re-layouts  10 us

profile of v2, /device:TPU:0, one launch (start us, length us, event | category | flops | bytes accessed | tf_op | source)
XLA Modules:
  0.0 178.0 jit_solution(274817856303229004)
XLA Ops:
  1.3 1.4 pad_maximum_fusion.1.refs_6_
  2.7 0.8 fusion.1
  3.5 0.8 fusion.2
  4.3 0.7 pad_maximum_fusion.refs_9_
  4.9 0.9 copy.24
  5.8 0.7 pad.4.refs_3_
  6.5 1.8 copy.25
  8.2 158.0 %shard_map.212 = (bf16[4,2,128,256]{3,2,1,0:T(8,128)(2,1)}, bf16[4,2,128,512]{3,2,1,0:T(8,128)(2,1)}, f32[512,768]{1,0:T(8,128)}, f32[768,512]{1,0:T(8,128)}, f3...) custom-call(s32[1]{0:T(128)S(6)} %copy.32.refs_0_, ...), custom_call_target="tpu_custom_call" | custom-call | tf_op jit(solution)/shard_map/pallas_call | solution.py:804
  166.3 0.0 copy-start.2
  166.3 1.4 fusion
  167.7 1.4 slice_bitcast_fusion
  169.1 1.5 fusion.3
  170.6 0.0 copy-start.1
  170.6 2.0 %copy.33 = bf16[1024,256]{1,0:T(8,128)(2,1)} copy(bf16[1024,256]{1,0:T(8,128)(2,1)} %bitcast.21) | data formatting | bytes 1048576
  172.6 0.0 copy-done.2
  172.6 1.0 copy.34
  173.5 0.0 copy-done.1
  173.5 0.0 copy-start
  173.5 1.1 copy.35
  174.7 0.8 copy-done
  175.5 0.0 copy-start.4
  175.5 0.0 copy-start.3
  175.5 1.1 copy.36
  176.7 0.0 copy-done.4
  176.7 0.7 copy.37
  177.3 0.0 copy-done.3
  177.3 0.7 copy.38
  (1 shorter events, 0.0 us)
Async XLA Ops:
  166.3 6.3 %copy-start.2 = (bf16[4,2,128,512]{3,2,1,0:T(8,128)(2,1)S(1)}, bf16[4,2,128,512]{3,2,1,0:T(8,128)(2,1)}, u32[]{:S(2)}) copy-start(bf16[4,2,128,512]{3,2,1,0:T(8,128)(2,1)} %get-tuple-element.20) | copy-start | bytes 3145732
  170.6 3.0 %copy-start.1 = (f32[512,768]{1,0:T(8,128)S(1)}, f32[512,768]{1,0:T(8,128)}, u32[]{:S(2)}) copy-start(f32[512,768]{1,0:T(8,128)} %get-tuple-element.53) | copy-start | bytes 4718596
  173.5 2.0 %copy-start = (f32[768,512]{1,0:T(8,128)S(1)}, f32[768,512]{1,0:T(8,128)}, u32[]{:S(2)}) copy-start(f32[768,512]{1,0:T(8,128)} %get-tuple-element.54) | copy-start | bytes 4718596
  175.5 1.1 copy-start.4
  175.5 1.8 %copy-start.3 = (f32[32,1024]{1,0:T(8,128)S(1)}, f32[32,1024]{1,0:T(8,128)}, u32[]{:S(2)}) copy-start(f32[32,1024]{1,0:T(8,128)} %get-tuple-element.26) | copy-start | bytes 393220

commit v3 on v2

--- a/solution.py
+++ b/solution.py
@@ -51,20 +51,22 @@
     "len_ref",
     "tok",
     "gain1",
-    "wr",
+    "wrt",
     "gain2",
-    "ids",
-    "wkv_in",
+    "idst",
+    "wk_in",
+    "wv_in",
     "wq_in",
     "wo_in",
-    "w_in",
+    "wh_in",
+    "wt_in",
     "go_in",
 ]
 out_names = [
     "out",
     "gt",
-    "gwq",
-    "gwo",
+    "QA",
+    "PA",
     "gwh",
     "gwT",
     "gkv",
@@ -112,7 +114,8 @@
         "gatt": vm((own, width), bf16),
         "dOs": vm((nb, top, rb, 128), bf16),
         "glog": vm((own, 128), bf16),
-        "DS": vm((rows, top * rb), bf16),
+        "AG": vm((own, 2 * ch), bf16),
+        "wrp": vm((128, width), bf16),
         "gK": vm((rows, 128), f32),
         "gV": vm((rows, 128), f32),
         "dQ": vm((top, rb, 128), f32),
@@ -123,23 +126,22 @@
         "F": vm((2, 2) + ring + (shard, 2 * ch), bf16),
         "FC": vm((2, 2, nz, 2, shard, 2 * ch), bf16),
         "FY0": vm((nz, 2, shard, 2 * ch), bf16),
-        "FX0": vm((nz, shard, 2 * ch), bf16),
-        "FZ0": vm((nz - 1, shard, 2 * ch), bf16),
+        "FZ0": vm((nz - 1, 2, shard, 2 * ch), bf16),
+        "FX0": vm((shard, 2 * ch), bf16),
         "FX1": vm((2, nz, shard, 2 * ch), bf16),
-        "FZ1": vm((nz - 1, 2, shard, 2 * ch), bf16),
-        "FY1": vm((shard, 2 * ch), bf16),
-        "Q": vm((2,) + ring + (shard, half), bf16),
+        "FY1": vm((nz, shard, 2 * ch), bf16),
+        "FZ1": vm((nz - 1, shard, 2 * ch), bf16),
         "QC": vm((2, nz, 2, shard, half), bf16),
-        "QX": vm((2, nz, shard, half), bf16),
-        "QY": vm((nz, shard, half), bf16),
+        "QXA": vm((2, nz, shard, half // 2), bf16),
+        "QYA": vm((nz, shard, half // 2), bf16),
+        "QYB": vm((nz, 2, shard, half // 2), bf16),
+        "QXB": vm((nz, shard, half // 2), bf16),
         "QZ": vm((nz - 1, shard, half), bf16),
-        "QA": vm(ring + (shard, half), bf16),
         "P": vm((2,) + ring + (woc, width), bf16),
         "PC": vm((2, nz, 2, woc, width), bf16),
         "PX": vm((2, nz, woc, width), bf16),
         "PY": vm((nz, woc, width), bf16),
         "PZ": vm((nz - 1, woc, width), bf16),
-        "PA": vm(ring + (woc, width), bf16),
         "K": vm(ring + (shard, 128), f32),
         "KC": vm((nz, 2, shard, 128), f32),
         "KX": vm((nz, shard, 128), f32),
@@ -164,13 +166,14 @@
         setattr(r, name, ref)
     nb = r.tok.shape[0] // 2
     width = r.tok.shape[2]
-    top = r.ids.shape[2]
+    top = r.idst.shape[0]
     fq = r.gated.shape[1]
     half = fq // 2
     groups = fq // 128
     r.gq = r.gated
-    r.actS = r.DS.at[0 : nb * rb, 0 : r.W.shape[6] // 2]
-    r.giS = r.DS.at[0 : nb * rb, r.W.shape[6] // 2 : r.W.shape[6]]
+    r.Q = r.W.at[0, :, :, :, :, :, 0:half]
+    r.actS = r.AG.at[:, 0 : r.W.shape[6] // 2]
+    r.giS = r.AG.at[:, r.W.shape[6] // 2 : r.W.shape[6]]
     nz = r.W.shape[2]
     ch = r.W.shape[6] // 2
     shard = r.W.shape[5]
@@ -220,38 +223,53 @@
     def valid_rows(i):
         return (rb * own(i) + lax.broadcasted_iota(jnp.int32, (rb, 1), 0) < length).astype(f32)
 
-    l_w = here(0, r.w_in, r.W.at[:, y, z, x, c])
-    l_q = here(1, r.wq_in, r.WQ.at[y])
-    l_o = here(2, r.wo_in, r.WO.at[y])
-    l_g = here(3, r.go_in.at[:, y], r.GO.at[y])
-    l_kv = here(4, r.wkv_in, r.wkvg.at[z, x, c])
+    l_w = [
+        here(2 * j + k, ref.at[:, j * ch : (j + 1) * ch],
+             r.W.at[j, y, z, x, c, :, k * ch : (k + 1) * ch])
+        for j in range(2)
+        for k, ref in enumerate((r.wh_in, r.wt_in))
+    ]
+    l_q = here(4, r.wq_in, r.WQ.at[y])
+    l_o = here(5, r.wo_in, r.WO.at[y])
+    l_g = here(6, r.go_in.at[:, y], r.GO.at[y])
+    r.wkvg[z, x, c] = jnp.concatenate((r.wk_in[...], r.wv_in[...]), axis=1)
     barrier = pltpu.get_barrier_semaphore()
     peers = [over_c, over_x, over_y] + over_z
     for peer in peers:
         pl.semaphore_signal(barrier, inc=1, device_id=peer, device_id_type=MESH)
     pl.semaphore_wait(barrier, len(peers))
-    kv_c = send(r.wkv_in, r.wkvg.at[z, x, c], over_c)
-    w_y = send(r.w_in, r.W.at[:, y, z, x, c], over_y)
+    kv_c = send(r.wkvg.at[z, x, c], r.wkvg.at[z, x, c], over_c)
+    for copy in l_w:
+        copy.wait()
+    w_y = send(r.W.at[:, y, z, x, c], r.W.at[:, y, z, x, c], over_y)
     qrows = cut(c, width // 2)
     q_y = send(r.wq_in.at[qrows, :], r.WQ.at[y, qrows, :], over_y)
-    l_w.wait()
-    l_kv.wait()
-
+    spare = jnp.zeros((128 - r.wrt.shape[0], width), f32)
+    r.wrp[...] = jnp.concatenate((r.wrt[...].astype(f32), spare), axis=0).astype(bf16)
+
+    def w_part(k):
+        return r.W.at[k // 2, :, :, :, :, :, pl.ds((k % 2) * ch, ch)]
+
+    def w_over_z(k, both=False):
+        view = w_part(k).at[:, z, :, c] if both else w_part(k).at[:, z, x, c]
+        return [send(view, view, to) for to in over_z]
+
+    def w_over_x(k, line=True):
+        view = w_part(k).at[:, :, x, c] if line else w_part(k).at[:, z, x, c]
+        return send(view, view, over_x)
+
+    def w_over_c(k):
+        view = w_part(k).at[:, :, :, c]
+        return send(view, view, over_c)
     @pl.loop(0, 2 * nb)
     def _(b):
         normed, _ = norm_rows(r.tok[b].astype(f32))
         r.h1[b] = (normed * r.gain1[...]).astype(bf16)
-
     got(kv_c)
     kv_x = send(r.wkvg.at[z, x], r.wkvg.at[z, x], over_x)
     got(w_y)
-
-    def w_over_z(j):
-        return [
-            send(r.W.at[j, :, z, x, c], r.W.at[j, :, z, x, c], to) for to in over_z
-        ]
-
     w0_z = w_over_z(0)
+    w3_x = w_over_x(3, False)
 
     lane = lanes((rb, 128))
     upper = (lane >= 64).astype(jnp.int32)
@@ -260,8 +278,8 @@
         h = r.h1[own(i)]
         at = cut(i, rb)
         r.h1T[:, at] = h.astype(f32).T.astype(bf16)
-        logits = nn(h, r.wr[...])
-        ids = r.ids[own(i)]
+        logits = nt(h, r.wrp[...])
+        ids = r.idst[:, cut(own(i), rb)].astype(f32).T.astype(jnp.int32)
         spread = [jnp.broadcast_to(ids[:, k : k + 1], (rb, 128)) for k in range(top)]
         chosen = lane == spread[0]
         for k in range(1, top):
@@ -279,7 +297,6 @@
     got(kv_x)
     kv_z = [send(r.wkvg.at[z], r.wkvg.at[z], to) for to in over_z]
     pl.loop(nb // 2, nb)(gates)
-
     got(*kv_z)
 
     @pl.loop(0, 2 * nb)
@@ -293,14 +310,16 @@
         r.VV[at, :] = v2.astype(bf16)
         r.KKT[:, at] = k2.T.astype(bf16)
         r.VVT[:, at] = v2.T.astype(bf16)
-
+    got(*w0_z)
+    w0_x = w_over_x(0)
+    w1_z = w_over_z(1)
     got(q_y)
     q_c = send(r.WQ.at[1 - y, qrows, :], r.WQ.at[1 - y, qrows, :], over_c)
     orows = cut(c, half // 2)
     o_y = send(r.wo_in.at[orows, :], r.WO.at[y, orows, :], over_y)
+    g_y = send(r.go_in.at[:, 1 - y], r.GO.at[y], over_y)
     l_q.wait()
     got(q_c)
-
     @pl.loop(0, nb)
     def _(i):
         h = r.h1[own(i)]
@@ -317,14 +336,13 @@
                 for g in range(groups):
                     val = jnp.where(mine == 2 * g, parts[g], val)
                 r.Qs[i, k, at, :] = val.astype(bf16)
-
     diag = lax.broadcasted_iota(jnp.int32, (256, 256), 0) <= rb * y + lanes((256, 256)) % 128
 
     def attend(i):
         nk = 256 * i
         start = 128 * i * (i + 1)
 
-        @pl.loop(0, top // 2)
+        @pl.loop(0, top // 2, unroll=4)
         def _(p):
             q = r.Qs[i, pl.ds(2 * p, 2)].reshape(256, 128)
             cols = cut(p, 256)
@@ -350,26 +368,27 @@
             r.O[i, pl.ds(2 * p, 2)] = o.T.reshape(2, rb, 128)
 
     attend(0)
+    got(*w1_z)
+    w1_x = w_over_x(1)
+    w2_z = w_over_z(2)
     attend(1)
-    got(*w0_z)
-    w0_x = send(r.W.at[0, :, :, x, c], r.W.at[0, :, :, x, c], over_x)
-    w1_z = w_over_z(1)
     attend(2)
-    g_y = send(r.go_in.at[:, 1 - y], r.GO.at[y], over_y)
-    attend(3)
-    for i in range(4, nb):
+    got(w0_x)
+    w0_c = w_over_c(0)
+    got(*w2_z)
+    w2_x = w_over_x(2)
+    got(w3_x)
+    w3_z = w_over_z(3, True)
+    for i in range(3, nb):
         attend(i)
-    got(w0_x)
-    w0_c = send(r.W.at[0, :, :, :, c], r.W.at[0, :, :, :, c], over_c)
     got(o_y)
     o_c = send(r.WO.at[1 - y, orows, :], r.WO.at[1 - y, orows, :], over_c)
-    got(*w1_z)
-    w1_x = send(r.W.at[1, :, :, x, c], r.W.at[1, :, :, x, c], over_x)
+    got(w1_x)
+    w1_c = w_over_c(1)
     l_o.wait()
     l_g.wait()
     got(o_c)
     got(g_y)
-
     def project(i):
         at = cut(i, rb)
 
@@ -406,31 +425,28 @@
     c0 = 0.7978845608028654
     c1 = 0.044715
 
-    def feed(j, e):
-        first = j == 0 and e == 0
-
-        @pl.loop(0, nb)
-        def _(i):
-            at = cut(i, rb)
-            w1 = r.W[j, e, :, :, :, :, 0:ch].reshape(width, ch)
-            w2 = r.W[j, e, :, :, :, :, ch : 2 * ch].reshape(width, ch)
+    def feed(j, e, first=False):
+
+        w1 = r.W[j, e, :, :, :, :, 0:ch].reshape(width, ch)
+        w2 = r.W[j, e, :, :, :, :, ch : 2 * ch].reshape(width, ch)
+        for i in range(nb // 2):
+            at = pl.ds(i * 256, 256)
             v = nn(r.h2[at, :], w1)
             ga = nn(r.gf[at, :], w2)
             vv = v * v
-            t = jnp.tanh(v * (c0 + (c0 * c1) * vv))
-            hp = 0.5 + 0.5 * t
-            act = (v * hp).astype(bf16)
-            slope = hp + (0.5 * v) * (1.0 - t * t) * (c0 + (3 * c0 * c1) * vv)
-            gi = (slope * ga).astype(bf16)
-            r.actS[at, :] = act
-            r.giS[at, :] = gi
-            a = nt(act, w2)
-            b = nt(gi, w1)
-            if not first:
-                a = a + r.acc[at, :]
-                b = b + r.gh2[at, :]
-            r.acc[at, :] = a
-            r.gh2[at, :] = b
+            hp = 0.5 + 0.5 * jnp.tanh(v * (c0 + (c0 * c1) * vv))
+            act = v * hp
+            slope = hp + act * (1.0 - hp) * (2 * c0 + (6 * c0 * c1) * vv)
+            r.actS[at, :] = act.astype(bf16)
+            r.giS[at, :] = (slope * ga).astype(bf16)
+        a = nt(r.actS[...], w2)
+        b = nt(r.giS[...], w1)
+        if first:
+            r.acc[...] = a
+            r.gh2[...] = b
+        else:
+            r.acc[...] += a
+            r.gh2[...] += b
 
         shape = (nz, 2, 2, shard, ch)
         r.F[j, e, :, :, :, :, 0:ch] = nn(r.h2T[...], r.giS[...]).astype(bf16).reshape(shape)
@@ -444,26 +460,24 @@
         def _(t):
             a, b = t // 2, t % 2
             r.F[j, e, a, b, c] = r.F[j, e, a, b, c] + r.FC[j, e, a, b]
-
-    got(w0_c)
-    f00 = feed(0, 0)
-    got(w1_x)
-    w1_c = send(r.W.at[1, :, :, :, c], r.W.at[1, :, :, :, c], over_c)
-    f01 = feed(0, 1)
-    got(f00)
-    f_add_c(0, 0)
-    got(f01)
-    f_add_c(0, 1)
+    got(w0_c, w1_c)
+    f0p = feed(0, 1 - y, True)
+    got(w2_x)
+    w2_c = w_over_c(2)
+    f0m = feed(0, y)
+    got(f0p)
+    f_add_c(0, 1 - y)
     f0_y = send(r.F.at[0, 1 - y, :, :, c], r.FY0, over_y)
-    got(w1_c)
-    f10 = feed(1, 0)
-    f11 = feed(1, 1)
-    got(f10)
-    f_add_c(1, 0)
-    got(f11)
-    f_add_c(1, 1)
-    f1_x = send(r.F.at[1, :, :, 1 - x, c], r.FX1, over_x)
-
+    got(*w3_z)
+    w3_c = w_over_c(3)
+    got(f0m)
+    f_add_c(0, y)
+    got(w2_c, w3_c)
+    f1p = feed(1, 1 - y)
+    f1m = feed(1, y)
+    got(f1p)
+    f_add_c(1, 1 - y)
+    f1_xa = send(r.F.at[1, 1 - y, :, 1 - x, c], r.FX1.at[0], over_x)
     r.gain_rows[...] = jnp.zeros_like(r.gain_rows)
 
     def turn(i):
@@ -505,8 +519,22 @@
             gs = dn * (gd - jnp.sum(dn * gd, axis=-1, keepdims=True))
             r.glog[atr, :] = gs.astype(bf16)
 
-    pl.loop(0, nb)(turn)
+    pl.loop(0, nb // 2)(turn)
+    got(f1m)
+    f_add_c(1, y)
+    f1_xb = send(r.F.at[1, y, :, 1 - x, c], r.FX1.at[1], over_x)
+    pl.loop(nb // 2, nb)(turn)
     out_y = send(r.outx, r.out.at[:, y], over_y)
+    got(f0_y)
+
+    @pl.loop(0, 2 * nz)
+    def _(t):
+        a, b = t // 2, t % 2
+        r.F[0, y, a, b, c] = r.F[0, y, a, b, c] + r.FY0[a, b]
+
+    f0_z = [
+        send(r.F.at[0, y, k, :, c], r.FZ0.at[i], to) for i, (k, to) in enumerate(zip(zs, over_z))
+    ]
 
     woc = r.P.shape[4]
     for e in range(2):
@@ -516,15 +544,15 @@
             .reshape(nz, 2, 2, woc, width)
         )
     p_c = send(r.P.at[:, :, :, 1 - c], r.PC, over_c)
-
     r.gK[...] = jnp.zeros_like(r.gK)
     r.gV[...] = jnp.zeros_like(r.gV)
 
     def back(i):
         nk = 256 * (i + 1)
         start = 128 * i * (i + 1)
-
-        @pl.loop(0, top // 2)
+        r.gV[0:nk, :] += nn(r.PT[start : start + nk, :], r.dOs[i].reshape(top * rb, 128))
+
+        @pl.loop(0, top // 2, unroll=4)
         def _(p):
             do = r.dOs[i, pl.ds(2 * p, 2)].reshape(256, 128)
             cols = cut(p, 256)
@@ -532,12 +560,9 @@
             pr = r.PT[start : start + nk, cols].astype(f32)
             s = jnp.sum(pr * dp, axis=0, keepdims=True)
             ds = (pr * (dp - s)).astype(bf16)
-            r.DS[0:nk, cols] = ds
+            r.PT[start : start + nk, cols] = ds
             dq = nn(r.KKT[:, 0:nk], ds)
             r.dQ[pl.ds(2 * p, 2)] = dq.T.reshape(2, rb, 128)
-
-        r.gK[0:nk, :] += nn(r.DS[0:nk, :], r.Qs[i].reshape(top * rb, 128))
-        r.gV[0:nk, :] += nn(r.PT[start : start + nk, :], r.dOs[i].reshape(top * rb, 128))
 
         @pl.loop(0, rb // 16)
         def _(t):
@@ -561,23 +586,22 @@
 
     p_x = send(r.P.at[:, :, 1 - x, c], r.PX, over_x)
     back(1)
-    got(f0_y)
-
-    @pl.loop(0, 2 * nz)
-    def _(t):
-        a, b = t // 2, t % 2
-        r.F[0, y, a, b, c] = r.F[0, y, a, b, c] + r.FY0[a, b]
-
-    f0_x = send(r.F.at[0, y, :, 1 - x, c], r.FX0, over_x)
+    got(f1_xa, f1_xb)
+
+    @pl.loop(0, nz)
+    def _(a):
+        r.F[1, 1 - y, a, x, c] = r.F[1, 1 - y, a, x, c] + r.FX1[0, a]
+        r.F[1, y, a, x, c] = r.F[1, y, a, x, c] + r.FX1[1, a]
+
+    f1_y = send(r.F.at[1, 1 - y, :, x, c], r.FY1, over_y)
     back(2)
-    got(f1_x)
-
-    @pl.loop(0, 2 * nz)
-    def _(t):
-        e, a = t // nz, t % nz
-        r.F[1, e, a, x, c] = r.F[1, e, a, x, c] + r.FX1[e, a]
-
-    f1_z = [send(r.F.at[1, :, k, x, c], r.FZ1.at[i], to) for i, (k, to) in enumerate(zip(zs, over_z))]
+    got(*f0_z)
+    for b in range(2):
+        v = r.F[0, y, z, b, c].astype(f32)
+        for k in range(nz - 1):
+            v = v + r.FZ0[k, b].astype(f32)
+        r.F[0, y, z, b, c] = v.astype(bf16)
+    f0_x = send(r.F.at[0, y, z, 1 - x, c], r.FX0, over_x)
     got(p_x)
 
     @pl.loop(0, 2 * nz)
@@ -586,9 +610,41 @@
         r.P[e, a, x, c] = r.P[e, a, x, c] + r.PX[e, a]
 
     p_y = send(r.P.at[1 - y, :, x, c], r.PY, over_y)
-    back(3)
-    for i in range(4, nb):
+    got(f1_y)
+
+    @pl.loop(0, nz)
+    def _(a):
+        r.F[1, y, a, x, c] = r.F[1, y, a, x, c] + r.FY1[a]
+
+    f1_z = [
+        send(r.F.at[1, y, k, x, c], r.FZ1.at[i], to) for i, (k, to) in enumerate(zip(zs, over_z))
+    ]
+    for i in range(3, nb):
         back(i)
+    for copy in [w_y, w3_x, w0_x, w1_x, w2_x, w0_c, w1_c, w2_c, w3_c, *w0_z, *w1_z, *w2_z, *w3_z]:
+        copy.wait_send()
+        sent[:] = [other for other in sent if other is not copy]
+    for e in range(2):
+        r.Q[e] = (
+            nn(r.h1T[...], r.gq[:, e * half : (e + 1) * half])
+            .astype(bf16)
+            .reshape(nz, 2, 2, shard, half)
+        )
+    q_c2 = send(r.Q.at[:, :, :, 1 - c], r.QC, over_c)
+    for i in range(nb):
+        nk = 256 * (i + 1)
+        start = 128 * i * (i + 1)
+        r.gK[0:nk, :] += nn(r.PT[start : start + nk, :], r.Qs[i].reshape(top * rb, 128))
+    got(q_c2)
+
+    @pl.loop(0, 4 * nz)
+    def _(t):
+        e, a, b = t // (2 * nz), (t // 2) % nz, t % 2
+        r.Q[e, a, b, c] = r.Q[e, a, b, c] + r.QC[e, a, b]
+
+    one, two = pl.ds(0, half // 2), pl.ds(half // 2, half // 2)
+    qa_x = send(r.Q.at[:, :, 1 - x, c, :, one], r.QXA, over_x)
+    qb_y = send(r.Q.at[1 - y, :, :, c, :, two], r.QYB, over_y)
 
     @pl.loop(0, nb)
     def _(i):
@@ -600,38 +656,44 @@
             r.kvs[i, s] = jnp.where(lane < 64, a, b).astype(bf16)
 
     kv_y = send(r.kvs.at[:, 1 - y], r.kvr, over_y)
+    g = nn(r.glog[...], r.wrp[...])
     for e in range(2):
-        r.Q[e] = (
-            nn(r.h1T[...], r.gq[:, e * half : (e + 1) * half])
-            .astype(bf16)
-            .reshape(nz, 2, 2, shard, half)
-        )
-    q_c2 = send(r.Q.at[:, :, :, 1 - c], r.QC, over_c)
-    got(f0_x)
+        g = g + nt(r.gq[:, e * half : (e + 1) * half], r.WQ[e])
+    r.acc[...] = g
+    got(p_y)
 
     @pl.loop(0, nz)
     def _(a):
-        r.F[0, y, a, x, c] = r.F[0, y, a, x, c] + r.FX0[a]
-
-    f0_z = [send(r.F.at[0, y, k, x, c], r.FZ0.at[i], to) for i, (k, to) in enumerate(zip(zs, over_z))]
-    got(q_c2)
-
-    @pl.loop(0, 4 * nz)
+        r.P[y, a, x, c] = r.P[y, a, x, c] + r.PY[a]
+
+    p_z = [send(r.P.at[y, k, x, c], r.PZ.at[i], to) for i, (k, to) in enumerate(zip(zs, over_z))]
+    got(f0_x)
+    v = r.F[0, y, z, x, c].astype(f32) + r.FX0[...].astype(f32)
+    r.gwh[:, 0:ch] = v[:, 0:ch]
+    r.gwT[:, 0:ch] = v[:, ch : 2 * ch]
+    got(qa_x)
+
+    @pl.loop(0, 2 * nz)
     def _(t):
-        e, a, b = t // (2 * nz), (t // 2) % nz, t % 2
-        r.Q[e, a, b, c] = r.Q[e, a, b, c] + r.QC[e, a, b]
-
-    q_x = send(r.Q.at[:, :, 1 - x, c], r.QX, over_x)
-
+        e, a = t // nz, t % nz
+        r.Q[e, a, x, c, :, one] = r.Q[e, a, x, c, :, one] + r.QXA[e, a]
+
+    qa_y = send(r.Q.at[1 - y, :, x, c, :, one], r.QYA, over_y)
+    got(qb_y)
+
+    @pl.loop(0, 2 * nz)
+    def _(t):
+        a, b = t // 2, t % 2
+        r.Q[y, a, b, c, :, two] = r.Q[y, a, b, c, :, two] + r.QYB[a, b]
+
+    qb_x = send(r.Q.at[y, :, 1 - x, c, :, two], r.QXB, over_x)
     got(kv_y)
 
     def finish(i):
         at = cut(i, rb)
         low = (r.kvs[i, y].astype(f32) + r.kvr[i].astype(f32)).astype(bf16)
         r.kvr[i] = low
-        g = nt(low, r.wkvg[...].reshape(width, 128)) + nt(r.glog[at, :], r.wr[...])
-        for e in range(2):
-            g = g + nt(r.gq[at, e * half : (e + 1) * half], r.WQ[e])
+        g = r.acc[at, :] + nt(low, r.wkvg[...].reshape(width, 128))
         normed, inv = norm_rows(r.tok[own(i)].astype(f32))
         r.gain_rows[0:1, :] += jnp.sum(g * normed, axis=0, keepdims=True)
         r.gt[i, y] = (r.res[at, :] + norm_back(g, normed, inv, r.gain1[...])).astype(bf16)
@@ -648,6 +710,14 @@
     r.S[0, 30:32, :] = r.gain_rows[...]
     s_c = send(r.S.at[0], r.SR.at[0], over_c)
 
+    got(qa_y, qb_x)
+
+    @pl.loop(0, nz)
+    def _(a):
+        r.Q[y, a, x, c, :, one] = r.Q[y, a, x, c, :, one] + r.QYA[a]
+        r.Q[y, a, x, c, :, two] = r.Q[y, a, x, c, :, two] + r.QXB[a]
+
+    q_z = [send(r.Q.at[y, k, x, c], r.QZ.at[i], to) for i, (k, to) in enumerate(zip(zs, over_z))]
     got(k_c)
 
     @pl.loop(0, 2 * nz)
@@ -659,52 +729,42 @@
     got(s_c)
     r.S[1] = r.S[0] + r.SR[0]
     s_x = send(r.S.at[1], r.SR.at[1], over_x)
-
-    got(p_y)
-
-    @pl.loop(0, nz)
-    def _(a):
-        r.P[y, a, x, c] = r.P[y, a, x, c] + r.PY[a]
-
-    p_z = [send(r.P.at[y, k, x, c], r.PZ.at[i], to) for i, (k, to) in enumerate(zip(zs, over_z))]
-    got(*f1_z)
-    for e in range(2):
-        v = r.F[1, e, z, x, c].astype(f32)
-        for k in range(nz - 1):
-            v = v + r.FZ1[k, e].astype(f32)
-        r.F[1, e, z, x, c] = v.astype(bf16)
-    f1_y = send(r.F.at[1, 1 - y, z, x, c], r.FY1, over_y)
-    got(k_x)
-
-    @pl.loop(0, nz)
-    def _(a):
-        r.K[a, x, c] = r.K[a, x, c] + r.KX[a]
-
-    k_z = [send(r.K.at[k, x, c], r.KZ.at[i], to) for i, (k, to) in enumerate(zip(zs, over_z))]
-    got(s_x)
-    r.S[2] = r.S[1] + r.SR[1]
-    s_y = send(r.S.at[2], r.SR.at[2], over_y)
-    got(*f0_z)
-    v = r.F[0, y, z, x, c].astype(f32)
-    for k in range(nz - 1):
-        v = v + r.FZ0[k].astype(f32)
-    r.gwh[:, 0:ch] = v[:, 0:ch]
-    r.gwT[:, 0:ch] = v[:, ch : 2 * ch]
-
-    got(q_x)
-
-    @pl.loop(0, 2 * nz)
-    def _(t):
-        e, a = t // nz, t % nz
-        r.Q[e, a, x, c] = r.Q[e, a, x, c] + r.QX[e, a]
-
-    q_y2 = send(r.Q.at[1 - y, :, x, c], r.QY, over_y)
     got(*p_z)
     v = r.P[y, z, x, c].astype(f32)
     for k in range(nz - 1):
         v = v + r.PZ[k].astype(f32)
     r.PA[z, x, c] = v.astype(bf16)
     pa_z = [send(r.PA.at[z, x, c], r.PA.at[z, x, c], to) for to in over_z]
+    got(*f1_z)
+    v = r.F[1, y, z, x, c].astype(f32)
+    for k in range(nz - 1):
+        v = v + r.FZ1[k].astype(f32)
+    r.gwh[:, ch : 2 * ch] = v[:, 0:ch]
+    r.gwT[:, ch : 2 * ch] = v[:, ch : 2 * ch]
+    got(k_x)
+
+    @pl.loop(0, nz)
+    def _(a):
+        r.K[a, x, c] = r.K[a, x, c] + r.KX[a]
+
+    k_z = [send(r.K.at[k, x, c], r.KZ.at[i], to) for i, (k, to) in enumerate(zip(zs, over_z))]
+    got(s_x)
+    r.S[2] = r.S[1] + r.SR[1]
+    s_y = send(r.S.at[2], r.SR.at[2], over_y)
+    got(*q_z)
+    v = r.Q[y, z, x, c].astype(f32)
+    for k in range(nz - 1):
+        v = v + r.QZ[k].astype(f32)
+    r.QA[z, x, c] = v.astype(bf16)
+    view = r.QA.at[z, x, c, :, one]
+    ga_z = [send(view, view, to) for to in over_z]
+    view = r.QA.at[z, x, c, :, two]
+    gb_x = send(view, view, over_x)
+    got(*pa_z)
+    pa_x = send(r.PA.at[:, x, c], r.PA.at[:, x, c], over_x)
+    got(gb_x)
+    view = r.QA.at[z, :, c, :, two]
+    gb_z = [send(view, view, to) for to in over_z]
     got(*k_z)
     v = r.K[z, x, c]
     for k in range(nz - 1):
@@ -715,19 +775,14 @@
     r.S[3] = r.S[2] + r.SR[2]
     r.SZ[z] = r.S[3]
     s_z = [send(r.S.at[3], r.SZ.at[z], to) for to in over_z]
-    got(f1_y)
-    v = r.F[1, y, z, x, c].astype(f32) + r.FY1[...].astype(f32)
-    r.gwh[:, ch : 2 * ch] = v[:, 0:ch]
-    r.gwT[:, ch : 2 * ch] = v[:, ch : 2 * ch]
-    got(*pa_z)
-    pa_x = send(r.PA.at[:, x, c], r.PA.at[:, x, c], over_x)
-    got(q_y2)
-
-    @pl.loop(0, nz)
-    def _(a):
-        r.Q[y, a, x, c] = r.Q[y, a, x, c] + r.QY[a]
-
-    q_z = [send(r.Q.at[y, k, x, c], r.QZ.at[i], to) for i, (k, to) in enumerate(zip(zs, over_z))]
+    got(*ga_z)
+    view = r.QA.at[:, x, c, :, one]
+    ga_x = send(view, view, over_x)
+    got(pa_x)
+    pa_c = send(r.PA.at[:, :, c], r.PA.at[:, :, c], over_c)
+    got(*gb_z)
+    view = r.QA.at[:, :, c, :, two]
+    gb_c = send(view, view, over_c)
     got(k_y)
     r.gkv[...] = r.KY[0] + r.KY[1]
     got(*s_z)
@@ -735,35 +790,32 @@
     for k in range(1, nz):
         v = v + r.SZ[k]
     r.small[...] = v
-    got(*q_z)
-    v = r.Q[y, z, x, c].astype(f32)
-    for k in range(nz - 1):
-        v = v + r.QZ[k].astype(f32)
-    r.QA[z, x, c] = v.astype(bf16)
-    qa_z = [send(r.QA.at[z, x, c], r.QA.at[z, x, c], to) for to in over_z]
-    got(pa_x)
-    pa_c = send(r.PA.at[:, :, c], r.PA.at[:, :, c], over_c)
-    got(*qa_z)
-    qa_x = send(r.QA.at[:, x, c], r.QA.at[:, x, c], over_x)
-    got(pa_c)
-
-    @pl.loop(0, 4 * nz)
-    def _(t):
-        at = cut(t, woc)
-        r.gwo[at, :] = r.PA[t // 4, (t // 2) % 2, t % 2].astype(f32)
-
-    got(qa_x)
-    qa_c = send(r.QA.at[:, :, c], r.QA.at[:, :, c], over_c)
-    got(qa_c)
-
-    @pl.loop(0, 4 * nz)
-    def _(t):
-        at = cut(t, shard)
-        r.gwq[at, :] = r.QA[t // 4, (t // 2) % 2, t % 2].astype(f32)
-
+    got(ga_x)
+    view = r.QA.at[:, :, c, :, one]
+    ga_c = send(view, view, over_c)
+    got(pa_c, gb_c, ga_c)
     got(out_y, gt_y)
     for copy in sent:
         copy.wait_send()
+
+
+def close(out, gt, QA, PA, gwh, gwT, gkv, small,
+          o_out, o_gt, o_wq, o_wo, o_wh, o_wT, o_k, o_v, o_wr, o_g1, o_g2, sem):
+    first = pltpu.make_async_copy(out, o_out, sem.at[0])
+    second = pltpu.make_async_copy(gt, o_gt, sem.at[1])
+    first.start()
+    second.start()
+    o_wq[...] = QA[...].astype(f32)
+    o_wo[...] = PA[...].astype(f32)
+    o_wh[...] = gwh[...]
+    o_wT[...] = gwT[...]
+    o_k[...] = gkv[:, 0:64]
+    o_v[...] = gkv[:, 64:128]
+    o_wr[...] = small[0 : o_wr.shape[0], :]
+    o_g1[...] = small[30:31, :]
+    o_g2[...] = small[31:32, :]
+    first.wait()
+    second.wait()
 
 
 def shards(
@@ -778,61 +830,76 @@
     nb = rows // rb // 2
     top = expert_ids.shape[1]
     n_experts = w_router.shape[1]
-    hd = w_key.shape[1]
     half = w_query.shape[1]
     ffh = w_hidden.shape[1]
-    ch = ffh // 2
     near = [[g * outer + k for k in range(outer)] for g in range(inner)]
-    wkv = jnp.concatenate((w_key, w_value), 1)
     wt = w_output.T
-    w_in = jnp.stack(
-        [
-            jnp.concatenate((w_hidden[:, :ch], wt[:, :ch]), 1),
-            jnp.concatenate((w_hidden[:, ch:], wt[:, ch:]), 1),
-        ]
-    )
     if outer > 1:
-        wkv = lax.all_gather(wkv, "dp", axis=0, tiled=True, axis_index_groups=near)
-        w_in = lax.all_gather(w_in, "dp", axis=1, tiled=True, axis_index_groups=near)
-    wr = jnp.pad(w_router, ((0, 0), (0, 128 - n_experts)))
+        w_key, w_value, w_hidden, wt = (
+            lax.all_gather(v, "dp", axis=0, tiled=True, axis_index_groups=near)
+            for v in (w_key, w_value, w_hidden, wt)
+        )
     shard = width // inner
+    woc = half // inner
     sds = jax.ShapeDtypeStruct
     spec = scratch(rows, width, nb, top, 2 * half, 2 * ffh, nz, shard)
     names = in_names + out_names + list(spec)
     vmem = pl.BlockSpec(memory_space=pltpu.VMEM)
     anyw = pl.BlockSpec(memory_space=pl.ANY)
-    out, gt, gwq, gwo, gwh, gwT, gkv, small = pl.pallas_call(
+    out, gt, QA, PA, gwh, gwT, gkv, small = pl.pallas_call(
         functools.partial(kernel, names, outer),
         out_shape=(
             sds((nb, 2, rb, width // 2), bf16),
             sds((nb, 2, rb, width), bf16),
-            sds((width, half), f32),
-            sds((half, width), f32),
+            sds((nz, 2, 2, shard, half), bf16),
+            sds((nz, 2, 2, woc, width), bf16),
             sds((shard, ffh), f32),
             sds((shard, ffh), f32),
             sds((shard, 128), f32),
             sds((32, width), f32),
         ),
-        in_specs=[pl.BlockSpec(memory_space=pltpu.SMEM)] + [vmem] * 5 + [anyw] * 5,
+        in_specs=[pl.BlockSpec(memory_space=pltpu.SMEM)] + [vmem] * 7 + [anyw] * 5,
         out_specs=[vmem] * 8,
         scratch_shapes=list(spec.values()),
         compiler_params=pltpu.CompilerParams(
             collective_id=0, has_side_effects=True, vmem_limit_bytes=63 * 2**20
         ),
     )(
-        lengths, tokens.reshape(2 * nb, rb, width), gain_attn[None], wr, gain_ffn[None],
-        expert_ids.reshape(2 * nb, rb, top), wkv, w_query, w_out, w_in,
+        lengths, tokens.reshape(2 * nb, rb, width), gain_attn[None], w_router.T, gain_ffn[None],
+        expert_ids.T, w_key, w_value, w_query, w_out, w_hidden, wt,
         grad_out.reshape(nb, 2, rb, width // 2),
     )
+    out, gt, gwq, gwo, gwh, gwT, gk, gv, gwr, g1, g2 = pl.pallas_call(
+        close,
+        out_shape=(
+            sds(out.shape, bf16),
+            sds(gt.shape, bf16),
+            sds((width, half), f32),
+            sds((half, width), f32),
+            sds((shard, ffh), f32),
+            sds((shard, ffh), f32),
+            sds((shard, 64), f32),
+            sds((shard, 64), f32),
+            sds((n_experts, width), f32),
+            sds((1, width), f32),
+            sds((1, width), f32),
+        ),
+        in_specs=[anyw] * 2 + [vmem] * 6,
+        out_specs=[anyw] * 2 + [vmem] * 9,
+        scratch_shapes=[pltpu.SemaphoreType.DMA((2,))],
+        compiler_params=pltpu.CompilerParams(vmem_limit_bytes=32 * 2**20),
+    )(out, gt, QA.reshape(width, half), PA.reshape(half, width), gwh, gwT, gkv, small)
     if outer > 1:
-        gwq, gwo, small = lax.psum((gwq, gwo, small), "dp", axis_index_groups=near)
-        gwh, gwT, gkv = (
+        gwq, gwo, gwr, g1, g2 = lax.psum(
+            (gwq, gwo, gwr, g1, g2), "dp", axis_index_groups=near
+        )
+        gwh, gwT, gk, gv = (
             lax.psum_scatter(v, "dp", scatter_dimension=0, tiled=True, axis_index_groups=near)
-            for v in (gwh, gwT, gkv)
+            for v in (gwh, gwT, gk, gv)
         )
     return (
-        out.reshape(rows, width // 2), gt.reshape(rows, width), gkv[:, :hd], gkv[:, hd:],
-        small[:n_experts].T, gwq, gwo, gwh, gwT.T, small[30], small[31],
+        out.reshape(rows, width // 2), gt.reshape(rows, width), gk, gv, gwr.T, gwq, gwo,
+        gwh, gwT.T, g1[0], g2[0],
     )
 
 

time: 179 us -> 138 us (0.77)
  Pallas kernels: 158 us -> 128 us
  local copies, waits for them, and re-layouts: 16.6 us -> 7.89 us
  other arithmetic: 2.07 us -> 0 us
    pallas_call x1, Pallas kernels: 158 us -> 125 us  [shards(): pl.pallas_call(functools.partial(kernel, names, outer), out_shape=(sds((n...]
    slice x4 -> x0, local copies, waits for them, and re-layouts: 4.44 us -> none  [the longest x1 1.47 us: shards(): gkv[:, hd:]]
    pallas_call x0 -> x1, Pallas kernels: none -> 2.92 us  [shards(): pl.pallas_call(close, out_shape=(sds(out.shape, bf16), sds(gt.shape, bf16...]
    unnamed x18 -> x16, local copies, waits for them, and re-layouts: 10 us -> 7.89 us
where the time goes in v3:
time: 138 us; the launch traced here: 137 us
  Pallas kernels  128 us (93%)
  local copies, waits for them, and re-layouts  7.89 us (6%)
  between operations  1.5 us (1%)
    pallas_call x1, Pallas kernels, shards(): pl.pallas_call(functools.partial(kernel, names, outer), out_shape=(sds((n...  125 us
    unnamed x16, local copies, waits for them, and re-layouts  7.89 us
    pallas_call x1, Pallas kernels, shards(): pl.pallas_call(close, out_shape=(sds(out.shape, bf16), sds(gt.shape, bf16...  2.92 us

profile of v3, /device:TPU:0, one launch (start us, length us, event | category | flops | bytes accessed | tf_op | source)
XLA Modules:
  0.0 137.3 jit_solution(9140492640208879557)
XLA Ops:
  1.3 125.0 %shard_map.212 = (bf16[4,2,128,256]{3,2,1,0:T(8,128)(2,1)}, bf16[4,2,128,512]{3,2,1,0:T(8,128)(2,1)}, bf16[4,2,2,32,768]{4,3,2,1,0:T(8,128)(2,1)}, bf16[4,2,2,48...) custom-call(s32[1]{0:T(128)S(6)} %copy.24.refs_0_, ...), custom_call_target="tpu_custom_call" | custom-call | tf_op jit(solution)/shard_map/pallas_call | solution.py:849
  126.3 0.0 copy-start
  126.3 1.2 copy-done
  127.5 0.0 copy-start.1
  127.5 1.1 copy-done.1
  128.6 0.0 copy-start.2
  128.6 1.1 copy-done.2
  129.8 0.0 copy-start.3
  129.8 1.0 copy-done.3
  130.8 0.0 copy-start.4
  130.8 0.9 copy-done.4
  131.7 0.0 copy-start.5
  131.7 0.9 copy-done.5
  132.6 0.0 copy-start.6
  132.6 0.8 copy-done.6
  133.5 0.0 copy-start.7
  133.5 0.7 copy-done.7
  134.2 2.9 %shard_map.213 = (bf16[4,2,128,256]{3,2,1,0:T(8,128)(2,1)}, bf16[4,2,128,512]{3,2,1,0:T(8,128)(2,1)}, f32[512,768]{1,0:T(8,128)}, f32[768,512]{1,0:T(8,128)}, f3...) custom-call(bf16[4,2,128,256]{3,2,1,0:T(8,128)(2,1)S(1)} %copy-done., ...), custom_call_target="tpu_custom_call" | custom-call | tf_op jit(solution)/shard_map/pallas_call | solution.py:872
Async XLA Ops:
  126.3 1.2 copy-start
  127.5 1.1 copy-start.1
  128.6 1.1 copy-start.2
  129.8 1.0 copy-start.3
  130.8 0.9 copy-start.4
  131.7 0.9 copy-start.5
  132.6 0.8 copy-start.6
  133.5 0.7 copy-start.7

commit v4 on v3

--- a/solution.py
+++ b/solution.py
@@ -49,7 +49,7 @@
 
 in_names = [
     "len_ref",
-    "tok",
+    "tok_in",
     "gain1",
     "wrt",
     "gain2",
@@ -71,6 +71,7 @@
     "gwT",
     "gkv",
     "small",
+    "gain1_out",
 ]
 
 
@@ -83,6 +84,12 @@
     ch = ff // 4
     woc = half // (4 * nz)
     return {
+        "tok": vm((2 * nb, rb, width), bf16),
+        "outm": vm((nb, rb, width // 2), bf16),
+        "gts": vm((nb, rb, width), bf16),
+        "G": vm((4, 1, width), f32),
+        "GR": vm((3, 1, width), f32),
+        "GZ": vm((nz, 1, width), f32),
         "wkvg": vm(ring + (shard, 128), bf16),
         "W": vm((2, 2) + ring + (shard, 2 * ch), bf16),
         "WQ": vm((2, width, half), bf16),
@@ -150,9 +157,9 @@
         "S": vm((4, 32, width), f32),
         "SR": vm((3, 32, width), f32),
         "SZ": vm((nz, 32, width), f32),
-        "send": pltpu.SemaphoreType.DMA((96,)),
-        "recv": pltpu.SemaphoreType.DMA((96,)),
-        "local": pltpu.SemaphoreType.DMA((8,)),
+        "send": pltpu.SemaphoreType.DMA((128,)),
+        "recv": pltpu.SemaphoreType.DMA((128,)),
+        "local": pltpu.SemaphoreType.DMA((16,)),
     }
 
 
@@ -223,6 +230,7 @@
     def valid_rows(i):
         return (rb * own(i) + lax.broadcasted_iota(jnp.int32, (rb, 1), 0) < length).astype(f32)
 
+    l_tok = here(7, r.tok_in, r.tok)
     l_w = [
         here(2 * j + k, ref.at[:, j * ch : (j + 1) * ch],
              r.W.at[j, y, z, x, c, :, k * ch : (k + 1) * ch])
@@ -238,12 +246,18 @@
     for peer in peers:
         pl.semaphore_signal(barrier, inc=1, device_id=peer, device_id_type=MESH)
     pl.semaphore_wait(barrier, len(peers))
-    kv_c = send(r.wkvg.at[z, x, c], r.wkvg.at[z, x, c], over_c)
-    for copy in l_w:
-        copy.wait()
-    w_y = send(r.W.at[:, y, z, x, c], r.W.at[:, y, z, x, c], over_y)
+    kv_z = [send(r.wkvg.at[z, x, c], r.wkvg.at[z, x, c], to) for to in over_z]
+    l_w[0].wait()
+    l_w[1].wait()
+    w_y0 = send(r.W.at[0, y, z, x, c], r.W.at[0, y, z, x, c], over_y)
     qrows = cut(c, width // 2)
     q_y = send(r.wq_in.at[qrows, :], r.WQ.at[y, qrows, :], over_y)
+    l_w[2].wait()
+    l_w[3].wait()
+    w_y1 = send(r.W.at[1, y, z, x, c], r.W.at[1, y, z, x, c], over_y)
+    orows = cut(c, half // 2)
+    o_y = send(r.wo_in.at[orows, :], r.WO.at[y, orows, :], over_y)
+    g_y = send(r.go_in.at[:, 1 - y], r.GO.at[y], over_y)
     spare = jnp.zeros((128 - r.wrt.shape[0], width), f32)
     r.wrp[...] = jnp.concatenate((r.wrt[...].astype(f32), spare), axis=0).astype(bf16)
 
@@ -261,15 +275,17 @@
     def w_over_c(k):
         view = w_part(k).at[:, :, :, c]
         return send(view, view, over_c)
+    l_tok.wait()
+
     @pl.loop(0, 2 * nb)
     def _(b):
         normed, _ = norm_rows(r.tok[b].astype(f32))
         r.h1[b] = (normed * r.gain1[...]).astype(bf16)
-    got(kv_c)
-    kv_x = send(r.wkvg.at[z, x], r.wkvg.at[z, x], over_x)
-    got(w_y)
+    got(*kv_z)
+    kv_x = send(r.wkvg.at[:, x, c], r.wkvg.at[:, x, c], over_x)
+    got(w_y0)
     w0_z = w_over_z(0)
-    w3_x = w_over_x(3, False)
+    w1_z = w_over_z(1)
 
     lane = lanes((rb, 128))
     upper = (lane >= 64).astype(jnp.int32)
@@ -295,9 +311,9 @@
 
     pl.loop(0, nb // 2)(gates)
     got(kv_x)
-    kv_z = [send(r.wkvg.at[z], r.wkvg.at[z], to) for to in over_z]
+    kv_c = send(r.wkvg.at[:, :, c], r.wkvg.at[:, :, c], over_c)
     pl.loop(nb // 2, nb)(gates)
-    got(*kv_z)
+    got(kv_c)
 
     @pl.loop(0, 2 * nb)
     def _(b):
@@ -312,14 +328,14 @@
         r.VVT[:, at] = v2.T.astype(bf16)
     got(*w0_z)
     w0_x = w_over_x(0)
-    w1_z = w_over_z(1)
     got(q_y)
     q_c = send(r.WQ.at[1 - y, qrows, :], r.WQ.at[1 - y, qrows, :], over_c)
-    orows = cut(c, half // 2)
-    o_y = send(r.wo_in.at[orows, :], r.WO.at[y, orows, :], over_y)
-    g_y = send(r.go_in.at[:, 1 - y], r.GO.at[y], over_y)
+    got(w_y1)
+    w3_x = w_over_x(3, False)
+    w2_z = w_over_z(2)
     l_q.wait()
     got(q_c)
+
     @pl.loop(0, nb)
     def _(i):
         h = r.h1[own(i)]
@@ -367,24 +383,23 @@
                 o = o + nn(r.VVT[:, 0:nk], p0)
             r.O[i, pl.ds(2 * p, 2)] = o.T.reshape(2, rb, 128)
 
-    attend(0)
+    got(w3_x)
+    w3_z = w_over_z(3, True)
     got(*w1_z)
     w1_x = w_over_x(1)
-    w2_z = w_over_z(2)
+    attend(0)
     attend(1)
-    attend(2)
+    got(*w2_z)
+    w2_x = w_over_x(2)
     got(w0_x)
     w0_c = w_over_c(0)
-    got(*w2_z)
-    w2_x = w_over_x(2)
-    got(w3_x)
-    w3_z = w_over_z(3, True)
+    attend(2)
+    got(w1_x)
+    w1_c = w_over_c(1)
+    got(o_y)
+    o_c = send(r.WO.at[1 - y, orows, :], r.WO.at[1 - y, orows, :], over_c)
     for i in range(3, nb):
         attend(i)
-    got(o_y)
-    o_c = send(r.WO.at[1 - y, orows, :], r.WO.at[1 - y, orows, :], over_c)
-    got(w1_x)
-    w1_c = w_over_c(1)
     l_o.wait()
     l_g.wait()
     got(o_c)
@@ -486,7 +501,7 @@
         outs = (r.res[at, :] + valid * r.acc[at, :]).astype(bf16)
         mine, other = outs[:, : width // 2], outs[:, width // 2 :]
         low = y == 0
-        r.out[i, y] = jnp.where(low, mine, other)
+        r.outm[i] = jnp.where(low, mine, other)
         r.outx[i] = jnp.where(low, other, mine)
         u, normed = r.gh2[at, :], r.n2[at, :]
         r.gain_rows[1:2, :] += jnp.sum(u * normed, axis=0, keepdims=True)
@@ -524,7 +539,13 @@
     f_add_c(1, y)
     f1_xb = send(r.F.at[1, y, :, 1 - x, c], r.FX1.at[1], over_x)
     pl.loop(nb // 2, nb)(turn)
-    out_y = send(r.outx, r.out.at[:, y], over_y)
+    l_out = here(8, r.outm, r.out.at[:, y])
+    routed = jnp.zeros((128, width), f32)
+    for i in range(nb):
+        routed = routed + tn(r.glog[i * rb : (i + 1) * rb, :], r.h1[own(i)])
+    r.S[0] = routed[0:32]
+    r.S[0, 31:32, :] = r.gain_rows[1:2, :]
+    s_c = send(r.S.at[0], r.SR.at[0], over_c)
     got(f0_y)
 
     @pl.loop(0, 2 * nz)
@@ -544,13 +565,13 @@
             .reshape(nz, 2, 2, woc, width)
         )
     p_c = send(r.P.at[:, :, :, 1 - c], r.PC, over_c)
-    r.gK[...] = jnp.zeros_like(r.gK)
-    r.gV[...] = jnp.zeros_like(r.gV)
 
     def back(i):
         nk = 256 * (i + 1)
         start = 128 * i * (i + 1)
-        r.gV[0:nk, :] += nn(r.PT[start : start + nk, :], r.dOs[i].reshape(top * rb, 128))
+        last = i == nb - 1
+        v = nn(r.PT[start : start + nk, :], r.dOs[i].reshape(top * rb, 128))
+        r.gV[0:nk, :] = v if last else r.gV[0:nk, :] + v
 
         @pl.loop(0, top // 2, unroll=4)
         def _(p):
@@ -576,7 +597,41 @@
                     val = jnp.where(mine[k] == 2 * g, vals[k], val)
                 r.gq[atr, pl.ds(128 * g, 128)] = val.astype(bf16) * 0.125
 
-    back(0)
+    def key_sums(i):
+        v = nn(r.PT[128 * i * (i + 1) : 128 * (i + 1) * (i + 2), :], r.Qs[i].reshape(top * rb, 128))
+        at = pl.ds(0, 256 * (i + 1))
+        r.gK[at, :] = v if i == nb - 1 else r.gK[at, :] + v
+        for s in range(2):
+            at = pl.ds((2 * i + s) * rb, rb)
+            a, b = r.gK[at, :], r.gV[at, :]
+            a = a + pltpu.roll(a, 64, 1)
+            b = b + pltpu.roll(b, 64, 1)
+            r.kvs[i, s] = jnp.where(lane < 64, a, b).astype(bf16)
+        return send(r.kvs.at[i, 1 - y], r.kvr.at[i], over_y)
+
+    def finish(i):
+        at = pl.ds(i * rb, rb)
+        low = (r.kvs[i, y].astype(f32) + r.kvr[i].astype(f32)).astype(bf16)
+        r.kvr[i] = low
+        g = nn(r.glog[at, :], r.wrp[...]) + nt(low, r.wkvg[...].reshape(width, 128))
+        for e in range(2):
+            g = g + nt(r.gq[at, e * half : (e + 1) * half], r.WQ[e])
+        normed, inv = norm_rows(r.tok[own(i)].astype(f32))
+        r.gain_rows[0:1, :] += jnp.sum(g * normed, axis=0, keepdims=True)
+        back = norm_back(g, normed, inv, r.gain1[...])
+        r.gts[i] = (r.res[at, :] + back).astype(bf16)
+        return here(9 + i, r.gts.at[i], r.gt.at[i, y])
+
+    def give(i):
+        return send(r.gts.at[i], r.gt.at[i, y], over_y)
+
+    keys, ends = {}, []
+    for i in range(nb - 1, 2, -1):
+        back(i)
+        keys[i] = key_sums(i)
+    got(s_c)
+    r.S[1] = r.S[0] + r.SR[0]
+    s_x = send(r.S.at[1], r.SR.at[1], over_x)
     got(p_c)
 
     @pl.loop(0, 4 * nz)
@@ -585,7 +640,6 @@
         r.P[e, a, b, c] = r.P[e, a, b, c] + r.PC[e, a, b]
 
     p_x = send(r.P.at[:, :, 1 - x, c], r.PX, over_x)
-    back(1)
     got(f1_xa, f1_xb)
 
     @pl.loop(0, nz)
@@ -595,6 +649,14 @@
 
     f1_y = send(r.F.at[1, 1 - y, :, x, c], r.FY1, over_y)
     back(2)
+    keys[2] = key_sums(2)
+    for i in range(nb - 1, 2, -1):
+        got(keys[i])
+        ends.append(finish(i))
+    gts_y = [give(i) for i in range(nb - 1, 2, -1)]
+    got(s_x)
+    r.S[2] = r.S[1] + r.SR[1]
+    s_y = send(r.S.at[2], r.SR.at[2], over_y)
     got(*f0_z)
     for b in range(2):
         v = r.F[0, y, z, b, c].astype(f32)
@@ -602,6 +664,8 @@
             v = v + r.FZ0[k, b].astype(f32)
         r.F[0, y, z, b, c] = v.astype(bf16)
     f0_x = send(r.F.at[0, y, z, 1 - x, c], r.FX0, over_x)
+    back(1)
+    keys[1] = key_sums(1)
     got(p_x)
 
     @pl.loop(0, 2 * nz)
@@ -619,9 +683,11 @@
     f1_z = [
         send(r.F.at[1, y, k, x, c], r.FZ1.at[i], to) for i, (k, to) in enumerate(zip(zs, over_z))
     ]
-    for i in range(3, nb):
-        back(i)
-    for copy in [w_y, w3_x, w0_x, w1_x, w2_x, w0_c, w1_c, w2_c, w3_c, *w0_z, *w1_z, *w2_z, *w3_z]:
+    got(keys[2])
+    ends.append(finish(2))
+    back(0)
+    for copy in [w_y0, w_y1, w3_x, w0_x, w1_x, w2_x, w0_c, w1_c, w2_c, w3_c,
+                 *w0_z, *w1_z, *w2_z, *w3_z]:
         copy.wait_send()
         sent[:] = [other for other in sent if other is not copy]
     for e in range(2):
@@ -631,10 +697,11 @@
             .reshape(nz, 2, 2, shard, half)
         )
     q_c2 = send(r.Q.at[:, :, :, 1 - c], r.QC, over_c)
-    for i in range(nb):
-        nk = 256 * (i + 1)
-        start = 128 * i * (i + 1)
-        r.gK[0:nk, :] += nn(r.PT[start : start + nk, :], r.Qs[i].reshape(top * rb, 128))
+    keys[0] = key_sums(0)
+    got(s_y)
+    r.S[3] = r.S[2] + r.SR[2]
+    r.SZ[z] = r.S[3]
+    s_z = [send(r.S.at[3], r.SZ.at[z], to) for to in over_z]
     got(q_c2)
 
     @pl.loop(0, 4 * nz)
@@ -645,21 +712,9 @@
     one, two = pl.ds(0, half // 2), pl.ds(half // 2, half // 2)
     qa_x = send(r.Q.at[:, :, 1 - x, c, :, one], r.QXA, over_x)
     qb_y = send(r.Q.at[1 - y, :, :, c, :, two], r.QYB, over_y)
-
-    @pl.loop(0, nb)
-    def _(i):
-        for s in range(2):
-            at = pl.ds(pl.multiple_of((2 * i + s) * rb, rb), rb)
-            a, b = r.gK[at, :], r.gV[at, :]
-            a = a + pltpu.roll(a, 64, 1)
-            b = b + pltpu.roll(b, 64, 1)
-            r.kvs[i, s] = jnp.where(lane < 64, a, b).astype(bf16)
-
-    kv_y = send(r.kvs.at[:, 1 - y], r.kvr, over_y)
-    g = nn(r.glog[...], r.wrp[...])
-    for e in range(2):
-        g = g + nt(r.gq[:, e * half : (e + 1) * half], r.WQ[e])
-    r.acc[...] = g
+    gts_y.append(give(2))
+    got(keys[1])
+    ends.append(finish(1))
     got(p_y)
 
     @pl.loop(0, nz)
@@ -671,6 +726,12 @@
     v = r.F[0, y, z, x, c].astype(f32) + r.FX0[...].astype(f32)
     r.gwh[:, 0:ch] = v[:, 0:ch]
     r.gwT[:, 0:ch] = v[:, ch : 2 * ch]
+    got(keys[0])
+    ends.append(finish(0))
+    r.K[...] = nn(r.h1T[...], r.kvr[...].reshape(nb * rb, 128)).reshape(nz, 2, 2, shard, 128)
+    k_c = send(r.K.at[:, :, 1 - c], r.KC, over_c)
+    r.G[0] = r.gain_rows[0:1, :]
+    g1_c = send(r.G.at[0], r.GR.at[0], over_c)
     got(qa_x)
 
     @pl.loop(0, 2 * nz)
@@ -687,37 +748,8 @@
         r.Q[y, a, b, c, :, two] = r.Q[y, a, b, c, :, two] + r.QYB[a, b]
 
     qb_x = send(r.Q.at[y, :, 1 - x, c, :, two], r.QXB, over_x)
-    got(kv_y)
-
-    def finish(i):
-        at = cut(i, rb)
-        low = (r.kvs[i, y].astype(f32) + r.kvr[i].astype(f32)).astype(bf16)
-        r.kvr[i] = low
-        g = r.acc[at, :] + nt(low, r.wkvg[...].reshape(width, 128))
-        normed, inv = norm_rows(r.tok[own(i)].astype(f32))
-        r.gain_rows[0:1, :] += jnp.sum(g * normed, axis=0, keepdims=True)
-        r.gt[i, y] = (r.res[at, :] + norm_back(g, normed, inv, r.gain1[...])).astype(bf16)
-
-    pl.loop(0, nb)(finish)
-    gt_y = send(r.gt.at[:, y], r.gt.at[:, y], over_y)
-
-    r.K[...] = nn(r.h1T[...], r.kvr[...].reshape(nb * rb, 128)).reshape(nz, 2, 2, shard, 128)
-    k_c = send(r.K.at[:, :, 1 - c], r.KC, over_c)
-    routed = jnp.zeros((128, width), f32)
-    for i in range(nb):
-        routed = routed + tn(r.glog[i * rb : (i + 1) * rb, :], r.h1[own(i)])
-    r.S[0] = routed[0:32]
-    r.S[0, 30:32, :] = r.gain_rows[...]
-    s_c = send(r.S.at[0], r.SR.at[0], over_c)
-
-    got(qa_y, qb_x)
-
-    @pl.loop(0, nz)
-    def _(a):
-        r.Q[y, a, x, c, :, one] = r.Q[y, a, x, c, :, one] + r.QYA[a]
-        r.Q[y, a, x, c, :, two] = r.Q[y, a, x, c, :, two] + r.QXB[a]
-
-    q_z = [send(r.Q.at[y, k, x, c], r.QZ.at[i], to) for i, (k, to) in enumerate(zip(zs, over_z))]
+    gts_y.append(give(1))
+    gts_y.append(give(0))
     got(k_c)
 
     @pl.loop(0, 2 * nz)
@@ -726,96 +758,117 @@
         r.K[a, b, c] = r.K[a, b, c] + r.KC[a, b]
 
     k_x = send(r.K.at[:, 1 - x, c], r.KX, over_x)
-    got(s_c)
-    r.S[1] = r.S[0] + r.SR[0]
-    s_x = send(r.S.at[1], r.SR.at[1], over_x)
+    got(g1_c)
+    r.G[1] = r.G[0] + r.GR[0]
+    g1_x = send(r.G.at[1], r.GR.at[1], over_x)
     got(*p_z)
     v = r.P[y, z, x, c].astype(f32)
     for k in range(nz - 1):
         v = v + r.PZ[k].astype(f32)
     r.PA[z, x, c] = v.astype(bf16)
     pa_z = [send(r.PA.at[z, x, c], r.PA.at[z, x, c], to) for to in over_z]
+
+    got(qa_y, qb_x)
+
+    @pl.loop(0, nz)
+    def _(a):
+        r.Q[y, a, x, c, :, one] = r.Q[y, a, x, c, :, one] + r.QYA[a]
+        r.Q[y, a, x, c, :, two] = r.Q[y, a, x, c, :, two] + r.QXB[a]
+
+    q_z = [send(r.Q.at[y, k, x, c], r.QZ.at[i], to) for i, (k, to) in enumerate(zip(zs, over_z))]
+    got(k_x)
+
+    @pl.loop(0, nz)
+    def _(a):
+        r.K[a, x, c] = r.K[a, x, c] + r.KX[a]
+
+    k_z = [send(r.K.at[k, x, c], r.KZ.at[i], to) for i, (k, to) in enumerate(zip(zs, over_z))]
+    got(g1_x)
+    r.G[2] = r.G[1] + r.GR[1]
+    g1_y = send(r.G.at[2], r.GR.at[2], over_y)
     got(*f1_z)
     v = r.F[1, y, z, x, c].astype(f32)
     for k in range(nz - 1):
         v = v + r.FZ1[k].astype(f32)
     r.gwh[:, ch : 2 * ch] = v[:, 0:ch]
     r.gwT[:, ch : 2 * ch] = v[:, ch : 2 * ch]
-    got(k_x)
-
-    @pl.loop(0, nz)
-    def _(a):
-        r.K[a, x, c] = r.K[a, x, c] + r.KX[a]
-
-    k_z = [send(r.K.at[k, x, c], r.KZ.at[i], to) for i, (k, to) in enumerate(zip(zs, over_z))]
-    got(s_x)
-    r.S[2] = r.S[1] + r.SR[1]
-    s_y = send(r.S.at[2], r.SR.at[2], over_y)
-    got(*q_z)
-    v = r.Q[y, z, x, c].astype(f32)
-    for k in range(nz - 1):
-        v = v + r.QZ[k].astype(f32)
-    r.QA[z, x, c] = v.astype(bf16)
-    view = r.QA.at[z, x, c, :, one]
-    ga_z = [send(view, view, to) for to in over_z]
-    view = r.QA.at[z, x, c, :, two]
-    gb_x = send(view, view, over_x)
+    got(*s_z)
+    v = r.SZ[0]
+    for k in range(1, nz):
+        v = v + r.SZ[k]
+    r.small[...] = v
     got(*pa_z)
     pa_x = send(r.PA.at[:, x, c], r.PA.at[:, x, c], over_x)
-    got(gb_x)
-    view = r.QA.at[z, :, c, :, two]
-    gb_z = [send(view, view, to) for to in over_z]
     got(*k_z)
     v = r.K[z, x, c]
     for k in range(nz - 1):
         v = v + r.KZ[k]
     r.KY[0] = v
     k_y = send(r.KY.at[0], r.KY.at[1], over_y)
-    got(s_y)
-    r.S[3] = r.S[2] + r.SR[2]
-    r.SZ[z] = r.S[3]
-    s_z = [send(r.S.at[3], r.SZ.at[z], to) for to in over_z]
+    out_y = send(r.outx, r.out.at[:, y], over_y)
+    got(*q_z)
+    v = r.Q[y, z, x, c].astype(f32)
+    for k in range(nz - 1):
+        v = v + r.QZ[k].astype(f32)
+    r.QA[z, x, c] = v.astype(bf16)
+    view = r.QA.at[z, x, c, :, two]
+    gb_x = send(view, view, over_x)
+    view = r.QA.at[z, x, c, :, one]
+    ga_z = [send(view, view, to) for to in over_z]
+    got(g1_y)
+    r.G[3] = r.G[2] + r.GR[2]
+    r.GZ[z] = r.G[3]
+    g1_z = [send(r.G.at[3], r.GZ.at[z], to) for to in over_z]
+    got(gb_x)
+    view = r.QA.at[z, :, c, :, two]
+    gb_z = [send(view, view, to) for to in over_z]
+    got(pa_x)
+    pa_c = send(r.PA.at[:, :, c], r.PA.at[:, :, c], over_c)
+    got(k_y)
+    r.gkv[...] = r.KY[0] + r.KY[1]
     got(*ga_z)
     view = r.QA.at[:, x, c, :, one]
     ga_x = send(view, view, over_x)
-    got(pa_x)
-    pa_c = send(r.PA.at[:, :, c], r.PA.at[:, :, c], over_c)
+    got(*g1_z)
+    v = r.GZ[0]
+    for k in range(1, nz):
+        v = v + r.GZ[k]
+    r.gain1_out[...] = v
     got(*gb_z)
     view = r.QA.at[:, :, c, :, two]
     gb_c = send(view, view, over_c)
-    got(k_y)
-    r.gkv[...] = r.KY[0] + r.KY[1]
-    got(*s_z)
-    v = r.SZ[0]
-    for k in range(1, nz):
-        v = v + r.SZ[k]
-    r.small[...] = v
     got(ga_x)
     view = r.QA.at[:, :, c, :, one]
     ga_c = send(view, view, over_c)
     got(pa_c, gb_c, ga_c)
-    got(out_y, gt_y)
+    l_out.wait()
+    for copy in ends:
+        copy.wait()
+    got(out_y, *gts_y)
     for copy in sent:
         copy.wait_send()
 
 
-def close(out, gt, QA, PA, gwh, gwT, gkv, small,
-          o_out, o_gt, o_wq, o_wo, o_wh, o_wT, o_k, o_v, o_wr, o_g1, o_g2, sem):
-    first = pltpu.make_async_copy(out, o_out, sem.at[0])
-    second = pltpu.make_async_copy(gt, o_gt, sem.at[1])
-    first.start()
-    second.start()
-    o_wq[...] = QA[...].astype(f32)
-    o_wo[...] = PA[...].astype(f32)
-    o_wh[...] = gwh[...]
-    o_wT[...] = gwT[...]
-    o_k[...] = gkv[:, 0:64]
-    o_v[...] = gkv[:, 64:128]
-    o_wr[...] = small[0 : o_wr.shape[0], :]
-    o_g1[...] = small[30:31, :]
-    o_g2[...] = small[31:32, :]
-    first.wait()
-    second.wait()
+def close(out, gt, QA, PA, gwh, gwT, gkv, small, gain1,
+          o_out, o_gt, o_wq, o_wo, o_wh, o_wT, o_k, o_v, o_wr, o_g1, o_g2,
+          b_q, b_o, b_k, b_s, sem):
+    pairs = ((QA, b_q), (PA, b_o), (gkv, b_k), (small, b_s),
+             (gt, o_gt), (out, o_out), (gwh, o_wh), (gwT, o_wT), (gain1, o_g1))
+    copies = [pltpu.make_async_copy(a, b, sem.at[k]) for k, (a, b) in enumerate(pairs)]
+    for copy in copies:
+        copy.start()
+    copies[0].wait()
+    o_wq[...] = b_q[...].astype(f32)
+    copies[1].wait()
+    o_wo[...] = b_o[...].astype(f32)
+    copies[2].wait()
+    o_k[...] = b_k[:, 0:64]
+    o_v[...] = b_k[:, 64:128]
+    copies[3].wait()
+    o_wr[...] = b_s[0 : o_wr.shape[0], :]
+    o_g2[...] = b_s[31:32, :]
+    for copy in copies[4:]:
+        copy.wait()
 
 
 def shards(
@@ -846,7 +899,7 @@
     names = in_names + out_names + list(spec)
     vmem = pl.BlockSpec(memory_space=pltpu.VMEM)
     anyw = pl.BlockSpec(memory_space=pl.ANY)
-    out, gt, QA, PA, gwh, gwT, gkv, small = pl.pallas_call(
+    out, gt, QA, PA, gwh, gwT, gkv, small, gain1 = pl.pallas_call(
         functools.partial(kernel, names, outer),
         out_shape=(
             sds((nb, 2, rb, width // 2), bf16),
@@ -857,9 +910,10 @@
             sds((shard, ffh), f32),
             sds((shard, 128), f32),
             sds((32, width), f32),
+            sds((1, width), f32),
         ),
-        in_specs=[pl.BlockSpec(memory_space=pltpu.SMEM)] + [vmem] * 7 + [anyw] * 5,
-        out_specs=[vmem] * 8,
+        in_specs=[pl.BlockSpec(memory_space=pltpu.SMEM)] + [anyw] + [vmem] * 6 + [anyw] * 5,
+        out_specs=[anyw] * 2 + [vmem] * 7,
         scratch_shapes=list(spec.values()),
         compiler_params=pltpu.CompilerParams(
             collective_id=0, has_side_effects=True, vmem_limit_bytes=63 * 2**20
@@ -884,11 +938,17 @@
             sds((1, width), f32),
             sds((1, width), f32),
         ),
-        in_specs=[anyw] * 2 + [vmem] * 6,
-        out_specs=[anyw] * 2 + [vmem] * 9,
-        scratch_shapes=[pltpu.SemaphoreType.DMA((2,))],
-        compiler_params=pltpu.CompilerParams(vmem_limit_bytes=32 * 2**20),
-    )(out, gt, QA.reshape(width, half), PA.reshape(half, width), gwh, gwT, gkv, small)
+        in_specs=[anyw] * 9,
+        out_specs=[vmem] * 11,
+        scratch_shapes=[
+            pltpu.VMEM((width, half), bf16),
+            pltpu.VMEM((half, width), bf16),
+            pltpu.VMEM((shard, 128), f32),
+            pltpu.VMEM((32, width), f32),
+            pltpu.SemaphoreType.DMA((9,)),
+        ],
+        compiler_params=pltpu.CompilerParams(vmem_limit_bytes=63 * 2**20),
+    )(out, gt, QA.reshape(width, half), PA.reshape(half, width), gwh, gwT, gkv, small, gain1)
     if outer > 1:
         gwq, gwo, gwr, g1, g2 = lax.psum(
             (gwq, gwo, gwr, g1, g2), "dp", axis_index_groups=near

time: 138 us -> 128 us (0.928)
  local copies, waits for them, and re-layouts: 7.89 us -> 0 us
  Pallas kernels: 128 us -> 126 us
    unnamed x16 -> x0, local copies, waits for them, and re-layouts: 7.89 us -> none
    pallas_call x1, Pallas kernels: 125 us -> 122 us  [shards(): pl.pallas_call(functools.partial(kernel, names, outer), out_shape=(sds((n...]
where the time goes in v4:
time: 128 us; the launch traced here: 127 us
  Pallas kernels  126 us (98%)
  between operations  1.48 us (1%)
    pallas_call x1, Pallas kernels, shards(): pl.pallas_call(functools.partial(kernel, names, outer), out_shape=(sds((n...  122 us
    pallas_call x1, Pallas kernels, shards(): pl.pallas_call(close, out_shape=(sds(out.shape, bf16), sds(gt.shape, bf16...  4.29 us

profile of v4, /device:TPU:0, one launch (start us, length us, event | category | flops | bytes accessed | tf_op | source)
XLA Modules:
  0.0 127.5 jit_solution(12406293869927754093)
XLA Ops:
  1.3 121.7 %shard_map.212 = (bf16[4,2,128,256]{3,2,1,0:T(8,128)(2,1)}, bf16[4,2,128,512]{3,2,1,0:T(8,128)(2,1)}, bf16[4,2,2,32,768]{4,3,2,1,0:T(8,128)(2,1)}, bf16[4,2,2,48...) custom-call(s32[1]{0:T(128)S(6)} %copy.24.refs_0_, ...), custom_call_target="tpu_custom_call" | custom-call | tf_op jit(solution)/shard_map/pallas_call | solution.py:902
  123.0 4.3 %shard_map.213 = (bf16[4,2,128,256]{3,2,1,0:T(8,128)(2,1)}, bf16[4,2,128,512]{3,2,1,0:T(8,128)(2,1)}, f32[512,768]{1,0:T(8,128)}, f32[768,512]{1,0:T(8,128)}, f3...) custom-call(bf16[4,2,128,256]{3,2,1,0:T(8,128)(2,1)} %get-tuple-elem, ...), custom_call_target="tpu_custom_call" | custom-call | tf_op jit(solution)/shard_map/pallas_call | solution.py:926

commit v5 on v4

--- a/solution.py
+++ b/solution.py
@@ -342,7 +342,7 @@
         for e in range(2):
             r.wide[:, e * half : (e + 1) * half] = 0.125 * nn(h, r.WQ[e])
 
-        @pl.loop(0, rb // 16)
+        @pl.loop(0, rb // 16, unroll=4)
         def _(t):
             at = cut(t, 16)
             parts = [r.wide[at, pl.ds(128 * g, 128)] for g in range(groups)]
@@ -407,7 +407,7 @@
     def project(i):
         at = cut(i, rb)
 
-        @pl.loop(0, rb // 16)
+        @pl.loop(0, rb // 16, unroll=4)
         def _(t):
             at = cut(t, 16)
             atr = pl.ds(pl.multiple_of(i * rb + t * 16, 16), 16)
@@ -514,7 +514,7 @@
         for e in range(2):
             r.wide[:, e * half : (e + 1) * half] = nt(ga, r.WO[e])
 
-        @pl.loop(0, rb // 16)
+        @pl.loop(0, rb // 16, unroll=4)
         def _(t):
             at = cut(t, 16)
             atr = pl.ds(pl.multiple_of(i * rb + t * 16, 16), 16)
@@ -585,7 +585,7 @@
             dq = nn(r.KKT[:, 0:nk], ds)
             r.dQ[pl.ds(2 * p, 2)] = dq.T.reshape(2, rb, 128)
 
-        @pl.loop(0, rb // 16)
+        @pl.loop(0, rb // 16, unroll=4)
         def _(t):
             at = cut(t, 16)
             atr = pl.ds(pl.multiple_of(i * rb + t * 16, 16), 16)

time: 128 us -> 124 us (0.969)
  Pallas kernels: 126 us -> 122 us
    pallas_call x1, Pallas kernels: 122 us -> 118 us  [shards(): pl.pallas_call(functools.partial(kernel, names, outer), out_shape=(sds((n...]
where the time goes in v5:
time: 124 us
  Pallas kernels  122 us (98%)
  between operations  1.48 us (1%)
    pallas_call x1, Pallas kernels, shards(): pl.pallas_call(functools.partial(kernel, names, outer), out_shape=(sds((n...  118 us
    pallas_call x1, Pallas kernels, shards(): pl.pallas_call(close, out_shape=(sds(out.shape, bf16), sds(gt.shape, bf16...  4.29 us

profile of v5, /device:TPU:0, one launch (start us, length us, event | category | flops | bytes accessed | tf_op | source)
XLA Modules:
  0.0 123.9 jit_solution(16106422724872056729)
XLA Ops:
  1.3 118.1 %shard_map.212 = (bf16[4,2,128,256]{3,2,1,0:T(8,128)(2,1)}, bf16[4,2,128,512]{3,2,1,0:T(8,128)(2,1)}, bf16[4,2,2,32,768]{4,3,2,1,0:T(8,128)(2,1)}, bf16[4,2,2,48...) custom-call(s32[1]{0:T(128)S(6)} %copy.24.refs_0_, ...), custom_call_target="tpu_custom_call" | custom-call | tf_op jit(solution)/shard_map/pallas_call | solution.py:902
  119.4 4.3 %shard_map.213 = (bf16[4,2,128,256]{3,2,1,0:T(8,128)(2,1)}, bf16[4,2,128,512]{3,2,1,0:T(8,128)(2,1)}, f32[512,768]{1,0:T(8,128)}, f32[768,512]{1,0:T(8,128)}, f3...) custom-call(bf16[4,2,128,256]{3,2,1,0:T(8,128)(2,1)} %get-tuple-elem, ...), custom_call_target="tpu_custom_call" | custom-call | tf_op jit(solution)/shard_map/pallas_call | solution.py:926

commit v6 on v5

--- a/solution.py
+++ b/solution.py
@@ -107,7 +107,7 @@
         "Qs": vm((nb, top, rb, 128), bf16),
         "PT": vm((total, top * rb), bf16),
         "O": vm((nb, top, rb, 128), f32),
-        "wide": vm((rb, fq), f32),
+        "wide": vm((2 * rb, fq), f32),
         "gated": vm((own, fq), bf16),
         "n2": vm((own, width), f32),
         "r2": vm((own, 1), f32),
@@ -230,13 +230,13 @@
     def valid_rows(i):
         return (rb * own(i) + lax.broadcasted_iota(jnp.int32, (rb, 1), 0) < length).astype(f32)
 
-    l_tok = here(7, r.tok_in, r.tok)
     l_w = [
         here(2 * j + k, ref.at[:, j * ch : (j + 1) * ch],
              r.W.at[j, y, z, x, c, :, k * ch : (k + 1) * ch])
         for j in range(2)
         for k, ref in enumerate((r.wh_in, r.wt_in))
     ]
+    l_tok = here(7, r.tok_in, r.tok)
     l_q = here(4, r.wq_in, r.WQ.at[y])
     l_o = here(5, r.wo_in, r.WO.at[y])
     l_g = here(6, r.go_in.at[:, y], r.GO.at[y])
@@ -336,22 +336,28 @@
     l_q.wait()
     got(q_c)
 
-    @pl.loop(0, nb)
-    def _(i):
-        h = r.h1[own(i)]
+    def two_blocks(ref, u):
+        return jnp.concatenate((ref[own(2 * u)], ref[own(2 * u + 1)]), axis=0)
+
+    @pl.loop(0, nb // 2)
+    def _(u):
+        h = two_blocks(r.h1, u)
         for e in range(2):
             r.wide[:, e * half : (e + 1) * half] = 0.125 * nn(h, r.WQ[e])
-
-        @pl.loop(0, rb // 16, unroll=4)
-        def _(t):
-            at = cut(t, 16)
-            parts = [r.wide[at, pl.ds(128 * g, 128)] for g in range(groups)]
-            for k in range(top):
-                mine = r.idl[i, k, at, :]
-                val = jnp.zeros((16, 128), f32)
-                for g in range(groups):
-                    val = jnp.where(mine == 2 * g, parts[g], val)
-                r.Qs[i, k, at, :] = val.astype(bf16)
+        for s in range(2):
+            i = 2 * u + s
+
+            @pl.loop(0, rb // 16, unroll=4)
+            def _(t):
+                at = cut(t, 16)
+                atw = pl.ds(pl.multiple_of(s * rb + t * 16, 16), 16)
+                parts = [r.wide[atw, pl.ds(128 * g, 128)] for g in range(groups)]
+                for k in range(top):
+                    mine = r.idl[i, k, at, :]
+                    val = jnp.zeros((16, 128), f32)
+                    for g in range(groups):
+                        val = jnp.where(mine == 2 * g, parts[g], val)
+                    r.Qs[i, k, at, :] = val.astype(bf16)
     diag = lax.broadcasted_iota(jnp.int32, (256, 256), 0) <= rb * y + lanes((256, 256)) % 128
 
     def attend(i):
@@ -404,24 +410,26 @@
     l_g.wait()
     got(o_c)
     got(g_y)
-    def project(i):
-        at = cut(i, rb)
-
-        @pl.loop(0, rb // 16, unroll=4)
-        def _(t):
-            at = cut(t, 16)
-            atr = pl.ds(pl.multiple_of(i * rb + t * 16, 16), 16)
-            mine = [r.idl[i, k, at, :] for k in range(top)]
-            vals = [r.gateb[i, k, at, :] * r.O[i, k, at, :] for k in range(top)]
-            for g in range(groups):
-                val = jnp.zeros((16, 128), f32)
-                for k in range(top):
-                    val = jnp.where(mine[k] == 2 * g, vals[k], val)
-                r.gated[atr, pl.ds(128 * g, 128)] = val.astype(bf16)
-
-        valid = valid_rows(i)
+    def project(u):
+        for s in range(2):
+            i = 2 * u + s
+
+            @pl.loop(0, rb // 16, unroll=4)
+            def _(t):
+                at = cut(t, 16)
+                atr = pl.ds(pl.multiple_of(i * rb + t * 16, 16), 16)
+                mine = [r.idl[i, k, at, :] for k in range(top)]
+                vals = [r.gateb[i, k, at, :] * r.O[i, k, at, :] for k in range(top)]
+                for g in range(groups):
+                    val = jnp.zeros((16, 128), f32)
+                    for k in range(top):
+                        val = jnp.where(mine[k] == 2 * g, vals[k], val)
+                    r.gated[atr, pl.ds(128 * g, 128)] = val.astype(bf16)
+
+        at = cut(u, 2 * rb)
+        valid = valid_pair(u)
         att = nn(r.gated[at, 0:half], r.WO[0]) + nn(r.gated[at, half:fq], r.WO[1])
-        row = r.tok[own(i)].astype(f32) + valid * att
+        row = two_blocks(r.tok, u).astype(f32) + valid * att
         r.res[at, :] = row
         normed, inv = norm_rows(row)
         r.n2[at, :] = normed
@@ -431,11 +439,14 @@
         r.h2T[:, at] = h.T.astype(bf16)
         for s in range(2):
             side = pl.ds(s * (width // 2), width // 2)
-            g = valid * r.GO[s, i].astype(f32)
+            g = valid * r.GO[s, pl.ds(2 * u, 2)].reshape(2 * rb, width // 2).astype(f32)
             r.gf[at, side] = g.astype(bf16)
             r.gfT[side, at] = g.T.astype(bf16)
 
-    pl.loop(0, nb)(project)
+    def valid_pair(u):
+        return jnp.concatenate((valid_rows(2 * u), valid_rows(2 * u + 1)), axis=0)
+
+    pl.loop(0, nb // 2)(project)
 
     c0 = 0.7978845608028654
     c1 = 0.044715
@@ -495,50 +506,58 @@
     f1_xa = send(r.F.at[1, 1 - y, :, 1 - x, c], r.FX1.at[0], over_x)
     r.gain_rows[...] = jnp.zeros_like(r.gain_rows)
 
-    def turn(i):
-        at = cut(i, rb)
-        valid = valid_rows(i)
+    def turn(u):
+        at = cut(u, 2 * rb)
+        pair = pl.ds(2 * u, 2)
+        valid = valid_pair(u)
         outs = (r.res[at, :] + valid * r.acc[at, :]).astype(bf16)
         mine, other = outs[:, : width // 2], outs[:, width // 2 :]
         low = y == 0
-        r.outm[i] = jnp.where(low, mine, other)
-        r.outx[i] = jnp.where(low, other, mine)
-        u, normed = r.gh2[at, :], r.n2[at, :]
-        r.gain_rows[1:2, :] += jnp.sum(u * normed, axis=0, keepdims=True)
-        back = norm_back(u, normed, r.r2[at, :], r.gain2[...])
-        go = jnp.concatenate((r.GO[0, i], r.GO[1, i]), axis=1).astype(f32)
+        shape = (2, rb, width // 2)
+        r.outm[pair] = jnp.where(low, mine, other).reshape(shape)
+        r.outx[pair] = jnp.where(low, other, mine).reshape(shape)
+        u2, normed = r.gh2[at, :], r.n2[at, :]
+        r.gain_rows[1:2, :] += jnp.sum(u2 * normed, axis=0, keepdims=True)
+        back = norm_back(u2, normed, r.r2[at, :], r.gain2[...])
+        flat = (2 * rb, width // 2)
+        go = jnp.concatenate(
+            (r.GO[0, pair].reshape(flat), r.GO[1, pair].reshape(flat)), axis=1
+        ).astype(f32)
         gr = go + back
         r.res[at, :] = gr
         ga = (valid * gr).astype(bf16)
         r.gatt[at, :] = ga
         for e in range(2):
             r.wide[:, e * half : (e + 1) * half] = nt(ga, r.WO[e])
-
-        @pl.loop(0, rb // 16, unroll=4)
-        def _(t):
-            at = cut(t, 16)
-            atr = pl.ds(pl.multiple_of(i * rb + t * 16, 16), 16)
-            parts = [r.wide[at, pl.ds(128 * g, 128)] for g in range(groups)]
-            ln = lanes((16, 128))
-            hf = (ln >= 64).astype(jnp.int32)
-            gd = jnp.zeros((16, 128), f32)
-            for k in range(top):
-                mine = r.idl[i, k, at, :]
-                val = jnp.zeros((16, 128), f32)
-                for g in range(groups):
-                    val = jnp.where(mine == 2 * g, parts[g], val)
-                dot = jnp.sum(val * r.O[i, k, at, :], axis=-1, keepdims=True)
-                gd = jnp.where(mine + hf == ln, dot, gd)
-                r.dOs[i, k, at, :] = (r.gateb[i, k, at, :] * val).astype(bf16)
-            dn = r.dense[atr, :]
-            gs = dn * (gd - jnp.sum(dn * gd, axis=-1, keepdims=True))
-            r.glog[atr, :] = gs.astype(bf16)
-
-    pl.loop(0, nb // 2)(turn)
+        for s in range(2):
+            i = 2 * u + s
+
+            @pl.loop(0, rb // 16, unroll=4)
+            def _(t):
+                at = cut(t, 16)
+                atr = pl.ds(pl.multiple_of(i * rb + t * 16, 16), 16)
+                atw = pl.ds(pl.multiple_of(s * rb + t * 16, 16), 16)
+                parts = [r.wide[atw, pl.ds(128 * g, 128)] for g in range(groups)]
+                ln = lanes((16, 128))
+                hf = (ln >= 64).astype(jnp.int32)
+                gd = jnp.zeros((16, 128), f32)
+                for k in range(top):
+                    mine = r.idl[i, k, at, :]
+                    val = jnp.zeros((16, 128), f32)
+                    for g in range(groups):
+                        val = jnp.where(mine == 2 * g, parts[g], val)
+                    dot = jnp.sum(val * r.O[i, k, at, :], axis=-1, keepdims=True)
+                    gd = jnp.where(mine + hf == ln, dot, gd)
+                    r.dOs[i, k, at, :] = (r.gateb[i, k, at, :] * val).astype(bf16)
+                dn = r.dense[atr, :]
+                gs = dn * (gd - jnp.sum(dn * gd, axis=-1, keepdims=True))
+                r.glog[atr, :] = gs.astype(bf16)
+
+    pl.loop(0, nb // 4)(turn)
     got(f1m)
     f_add_c(1, y)
     f1_xb = send(r.F.at[1, y, :, 1 - x, c], r.FX1.at[1], over_x)
-    pl.loop(nb // 2, nb)(turn)
+    pl.loop(nb // 4, nb // 2)(turn)
     l_out = here(8, r.outm, r.out.at[:, y])
     routed = jnp.zeros((128, width), f32)
     for i in range(nb):
@@ -690,27 +709,33 @@
                  *w0_z, *w1_z, *w2_z, *w3_z]:
         copy.wait_send()
         sent[:] = [other for other in sent if other is not copy]
-    for e in range(2):
-        r.Q[e] = (
-            nn(r.h1T[...], r.gq[:, e * half : (e + 1) * half])
-            .astype(bf16)
-            .reshape(nz, 2, 2, shard, half)
+    one, two = pl.ds(0, half // 2), pl.ds(half // 2, half // 2)
+    q_c2 = []
+    for part in range(2):
+        side = pl.ds(part * (half // 2), half // 2)
+        for e in range(2):
+            at = pl.ds(e * half + part * (half // 2), half // 2)
+            r.Q[e, :, :, :, :, side] = (
+                nn(r.h1T[...], r.gq[:, at]).astype(bf16).reshape(nz, 2, 2, shard, half // 2)
+            )
+        q_c2.append(
+            send(r.Q.at[:, :, :, 1 - c, :, side], r.QC.at[:, :, :, :, side], over_c)
         )
-    q_c2 = send(r.Q.at[:, :, :, 1 - c], r.QC, over_c)
     keys[0] = key_sums(0)
     got(s_y)
     r.S[3] = r.S[2] + r.SR[2]
     r.SZ[z] = r.S[3]
     s_z = [send(r.S.at[3], r.SZ.at[z], to) for to in over_z]
-    got(q_c2)
-
-    @pl.loop(0, 4 * nz)
-    def _(t):
-        e, a, b = t // (2 * nz), (t // 2) % nz, t % 2
-        r.Q[e, a, b, c] = r.Q[e, a, b, c] + r.QC[e, a, b]
-
-    one, two = pl.ds(0, half // 2), pl.ds(half // 2, half // 2)
-    qa_x = send(r.Q.at[:, :, 1 - x, c, :, one], r.QXA, over_x)
+    for part, side in enumerate((one, two)):
+        got(q_c2[part])
+
+        @pl.loop(0, 4 * nz)
+        def _(t):
+            e, a, b = t // (2 * nz), (t // 2) % nz, t % 2
+            r.Q[e, a, b, c, :, side] = r.Q[e, a, b, c, :, side] + r.QC[e, a, b, :, side]
+
+        if part == 0:
+            qa_x = send(r.Q.at[:, :, 1 - x, c, :, one], r.QXA, over_x)
     qb_y = send(r.Q.at[1 - y, :, :, c, :, two], r.QYB, over_y)
     gts_y.append(give(2))
     got(keys[1])

time: 124 us -> 122 us (0.984)
  Pallas kernels: 122 us -> 120 us
    pallas_call x1, Pallas kernels: 118 us -> 116 us  [shards(): pl.pallas_call(functools.partial(kernel, names, outer), out_shape=(sds((n...]
where the time goes in v6:
time: 122 us
  Pallas kernels  120 us (98%)
  between operations  1.5 us (1%)
    pallas_call x1, Pallas kernels, shards(): pl.pallas_call(functools.partial(kernel, names, outer), out_shape=(sds((n...  116 us
    pallas_call x1, Pallas kernels, shards(): pl.pallas_call(close, out_shape=(sds(out.shape, bf16), sds(gt.shape, bf16...  4.29 us

profile of v6, /device:TPU:0, one launch (start us, length us, event | category | flops | bytes accessed | tf_op | source)
XLA Modules:
  0.0 121.5 jit_solution(7211545000234440419)
XLA Ops:
  1.3 115.7 %shard_map.212 = (bf16[4,2,128,256]{3,2,1,0:T(8,128)(2,1)}, bf16[4,2,128,512]{3,2,1,0:T(8,128)(2,1)}, bf16[4,2,2,32,768]{4,3,2,1,0:T(8,128)(2,1)}, bf16[4,2,2,48...) custom-call(s32[1]{0:T(128)S(6)} %copy.24.refs_0_, ...), custom_call_target="tpu_custom_call" | custom-call | tf_op jit(solution)/shard_map/pallas_call | solution.py:927
  117.0 4.3 %shard_map.213 = (bf16[4,2,128,256]{3,2,1,0:T(8,128)(2,1)}, bf16[4,2,128,512]{3,2,1,0:T(8,128)(2,1)}, f32[512,768]{1,0:T(8,128)}, f32[768,512]{1,0:T(8,128)}, f3...) custom-call(bf16[4,2,128,256]{3,2,1,0:T(8,128)(2,1)} %get-tuple-elem, ...), custom_call_target="tpu_custom_call" | custom-call | tf_op jit(solution)/shard_map/pallas_call | solution.py:951

commit v7 on v6

--- a/solution.py
+++ b/solution.py
@@ -154,9 +154,9 @@
         "KX": vm((nz, shard, 128), f32),
         "KZ": vm((nz - 1, shard, 128), f32),
         "KY": vm((2, shard, 128), f32),
-        "S": vm((4, 32, width), f32),
-        "SR": vm((3, 32, width), f32),
-        "SZ": vm((nz, 32, width), f32),
+        "S": vm((4, 32, width), bf16),
+        "SR": vm((3, 32, width), bf16),
+        "SZ": vm((nz, 32, width), bf16),
         "send": pltpu.SemaphoreType.DMA((128,)),
         "recv": pltpu.SemaphoreType.DMA((128,)),
         "local": pltpu.SemaphoreType.DMA((16,)),
@@ -562,8 +562,8 @@
     routed = jnp.zeros((128, width), f32)
     for i in range(nb):
         routed = routed + tn(r.glog[i * rb : (i + 1) * rb, :], r.h1[own(i)])
-    r.S[0] = routed[0:32]
-    r.S[0, 31:32, :] = r.gain_rows[1:2, :]
+    bottom = lax.broadcasted_iota(jnp.int32, (32, width), 0) == 31
+    r.S[0] = jnp.where(bottom, r.gain_rows[1:2, :], routed[0:32]).astype(bf16)
     s_c = send(r.S.at[0], r.SR.at[0], over_c)
     got(f0_y)
 
@@ -632,14 +632,19 @@
         at = pl.ds(i * rb, rb)
         low = (r.kvs[i, y].astype(f32) + r.kvr[i].astype(f32)).astype(bf16)
         r.kvr[i] = low
-        g = nn(r.glog[at, :], r.wrp[...]) + nt(low, r.wkvg[...].reshape(width, 128))
-        for e in range(2):
-            g = g + nt(r.gq[at, e * half : (e + 1) * half], r.WQ[e])
+        g = r.acc[at, :] + nt(low, r.wkvg[...].reshape(width, 128))
         normed, inv = norm_rows(r.tok[own(i)].astype(f32))
         r.gain_rows[0:1, :] += jnp.sum(g * normed, axis=0, keepdims=True)
         back = norm_back(g, normed, inv, r.gain1[...])
         r.gts[i] = (r.res[at, :] + back).astype(bf16)
         return here(9 + i, r.gts.at[i], r.gt.at[i, y])
+
+    def before(u):
+        at = pl.ds(u * 2 * rb, 2 * rb)
+        g = nn(r.glog[at, :], r.wrp[...])
+        for e in range(2):
+            g = g + nt(r.gq[at, e * half : (e + 1) * half], r.WQ[e])
+        r.acc[at, :] = g
 
     def give(i):
         return send(r.gts.at[i], r.gt.at[i, y], over_y)
@@ -669,6 +674,8 @@
     f1_y = send(r.F.at[1, 1 - y, :, x, c], r.FY1, over_y)
     back(2)
     keys[2] = key_sums(2)
+    for u in range(1, nb // 2):
+        before(u)
     for i in range(nb - 1, 2, -1):
         got(keys[i])
         ends.append(finish(i))
@@ -738,6 +745,7 @@
             qa_x = send(r.Q.at[:, :, 1 - x, c, :, one], r.QXA, over_x)
     qb_y = send(r.Q.at[1 - y, :, :, c, :, two], r.QYB, over_y)
     gts_y.append(give(2))
+    before(0)
     got(keys[1])
     ends.append(finish(1))
     got(p_y)
@@ -818,9 +826,9 @@
     r.gwh[:, ch : 2 * ch] = v[:, 0:ch]
     r.gwT[:, ch : 2 * ch] = v[:, ch : 2 * ch]
     got(*s_z)
-    v = r.SZ[0]
+    v = r.SZ[0].astype(f32)
     for k in range(1, nz):
-        v = v + r.SZ[k]
+        v = v + r.SZ[k].astype(f32)
     r.small[...] = v
     got(*pa_z)
     pa_x = send(r.PA.at[:, x, c], r.PA.at[:, x, c], over_x)

time: 122 us -> 120 us (0.984)
  Pallas kernels: 120 us -> 118 us
    pallas_call x1, Pallas kernels: 116 us -> 114 us  [shards(): pl.pallas_call(functools.partial(kernel, names, outer), out_shape=(sds((n...]
where the time goes in v7:
time: 120 us; the launch traced here: 119 us
  Pallas kernels  118 us (98%)
  between operations  1.5 us (1%)
    pallas_call x1, Pallas kernels, shards(): pl.pallas_call(functools.partial(kernel, names, outer), out_shape=(sds((n...  114 us
    pallas_call x1, Pallas kernels, shards(): pl.pallas_call(close, out_shape=(sds(out.shape, bf16), sds(gt.shape, bf16...  4.29 us

profile of v7, /device:TPU:0, one launch (start us, length us, event | category | flops | bytes accessed | tf_op | source)
XLA Modules:
  0.0 119.4 jit_solution(10955649246678461081)
XLA Ops:
  1.3 113.6 %shard_map.212 = (bf16[4,2,128,256]{3,2,1,0:T(8,128)(2,1)}, bf16[4,2,128,512]{3,2,1,0:T(8,128)(2,1)}, bf16[4,2,2,32,768]{4,3,2,1,0:T(8,128)(2,1)}, bf16[4,2,2,48...) custom-call(s32[1]{0:T(128)S(6)} %copy.24.refs_0_, ...), custom_call_target="tpu_custom_call" | custom-call | tf_op jit(solution)/shard_map/pallas_call | solution.py:935
  114.9 4.3 %shard_map.213 = (bf16[4,2,128,256]{3,2,1,0:T(8,128)(2,1)}, bf16[4,2,128,512]{3,2,1,0:T(8,128)(2,1)}, f32[512,768]{1,0:T(8,128)}, f32[768,512]{1,0:T(8,128)}, f3...) custom-call(bf16[4,2,128,256]{3,2,1,0:T(8,128)(2,1)} %get-tuple-elem, ...), custom_call_target="tpu_custom_call" | custom-call | tf_op jit(solution)/shard_map/pallas_call | solution.py:959
